TPU v7x, 32 devices: a whole 2x2x4 slice. The times are simulated.
32 devices in a mesh: tp: 4 (over y, x), ctx: 2 (over core), outer: 4 (over z).
Axes of the slice: x: 2, y: 2, z: 4, core: 2. Of those that a mesh axis runs over, the one named last changes fastest.
Arguments:
- queries_in: bfloat16 [4096, 2048], P(('outer', 'ctx'), 'tp'), may hold values from -6 to 6
- keys_in: bfloat16 [4096, 2048], P(('outer', 'ctx'), 'tp'), may hold values from -6 to 6
- values_in: bfloat16 [4096, 4096], P(('outer', 'ctx'), 'tp'), may hold values from -6 to 6
- gate_in: bfloat16 [4096, 4096], P(('outer', 'ctx'), 'tp'), may hold values from -6 to 6
- log_decay: float32 [32, 4096], P('tp', ('outer', 'ctx')), may hold values from -1 to 0
- write_strength: float32 [32, 4096], P('tp', ('outer', 'ctx')), may hold values from 0 to 0.95
- doc_lengths: int32 [8], replicated, may hold values from 1 to 32, 64 in all
- norm_gain: float32 [128], replicated, may hold values from 0.1 to 1.9
- out_weight: bfloat16 [4096, 2048], P('tp'), may hold values from -0.09375 to 0.09375
Outputs:
- mixed: bfloat16 [4096, 2048], P(('outer', 'ctx', 'tp'))
Inputs may be any that keep to these rules, and one draw needn't show every extreme that they name: `doc_lengths`: the lengths sum to 64, and one document spans 32 stretches.
All inputs are finite; a program needn't handle non-finite values.
Results may differ from a plain program's by a relative error of at most 0.0066.
Values sent between devices are 32-bit elements; how exact they have to be, the bound alone decides.
No kernel may reach another device: no remote copies, remote signals or barrier semaphores. Data moves between devices by JAX's collectives and lax.ppermute only.
A program may use at most 128 MiB of HBM per device.

v0:
```python
import jax
import jax.numpy as jnp
from jax import lax
from jax.sharding import PartitionSpec as P

DK = 128
DV = 128
STRETCH = 64


def carried_in(shard, axis, combine, identity):
    length, place = (lax.axis_size(axis), lax.axis_index(axis))
    everything = jax.tree.map(lambda part: lax.all_gather(part, axis), shard)
    start = jax.tree.map(
        lambda part, zero: jnp.broadcast_to(jnp.asarray(zero, part.dtype), part.shape),
        shard,
        identity,
    )

    def hop(k, before):
        reached = k < place
        new = combine(before, jax.tree.map(lambda part: part[k], everything))
        return jax.tree.map(lambda a, b: jnp.where(reached, a, b), new, before)

    return lax.fori_loop(0, length, hop, start)


def from_root(value, axis, source):
    kept = jnp.where(lax.axis_index(axis) == source, value, 0).astype(value.dtype)
    return lax.psum(kept, axis)


def unit_norm(rows):
    return rows * lax.rsqrt(jnp.sum(rows * rows, axis=-1, keepdims=True) + 1e-06)


def matmul_heads(left, right):
    return jnp.einsum("...ij,...jk->...ik", left, right, precision=lax.Precision.HIGHEST)


def lower_inverse(strict_part):
    length = strict_part.shape[-1]
    power = -strict_part
    result = jnp.eye(length, dtype=strict_part.dtype) + power
    span = 1
    while 2 * span < length:
        power = matmul_heads(power, power)
        result = result + matmul_heads(result, power)
        span = 2 * span
    return result


def stretch_parts(query_half, key_half, value_rows, decay_rows, beta_rows):
    key_rows = key_half.astype(jnp.float32)
    query_rows = query_half.astype(jnp.float32)
    width = key_rows.shape[-1]
    length = decay_rows.shape[-1]
    cumulative = jnp.cumsum(decay_rows, axis=-1)
    order = jnp.arange(length)
    strict = order[:, None] > order[None, :]
    inclusive = order[:, None] >= order[None, :]
    gaps = cumulative[..., :, None] - cumulative[..., None, :]
    decay_strict = jnp.where(strict, jnp.exp(jnp.where(strict, gaps, 0.0)), 0.0)
    decay_incl = jnp.where(inclusive, jnp.exp(jnp.where(inclusive, gaps, 0.0)), 0.0)
    key_gram = jnp.einsum(
        "...id,...jd->...ij", key_half, key_half, preferred_element_type=jnp.float32
    )
    strict_part = beta_rows[..., :, None] * key_gram * decay_strict
    right_sides = jnp.concatenate(
        [
            (beta_rows * jnp.exp(cumulative))[..., None] * key_rows,
            beta_rows[..., None] * value_rows,
        ],
        axis=-1,
    )
    solved = matmul_heads(lower_inverse(strict_part), right_sides)
    wy_keys = solved[..., :width]
    wy_values = solved[..., width:]
    decayed_query = query_rows * jnp.exp(cumulative)[..., None]
    intra_scores = (
        jnp.einsum("...id,...jd->...ij", query_half, key_half, preferred_element_type=jnp.float32)
        * decay_incl
    )
    last_cum = cumulative[..., -1:]
    decayed_keys = key_rows * jnp.exp(last_cum - cumulative)[..., None]
    stretch_decay = jnp.exp(last_cum)
    return (wy_keys, wy_values, decayed_query, intra_scores, decayed_keys, stretch_decay)


def combine(earlier, later):
    return (matmul_heads(later[0], earlier[0]), matmul_heads(later[0], earlier[1]) + later[1])


def shards(
    queries_in,
    keys_in,
    values_in,
    gate_in,
    log_decay,
    write_strength,
    doc_lengths,
    norm_gain,
    out_weight,
):
    tokens_here = queries_in.shape[0]
    head_count = log_decay.shape[0]
    key_heads = queries_in.shape[1] // DK
    group_size = head_count // key_heads
    local_stretches = tokens_here // STRETCH
    unit_q = unit_norm(queries_in.astype(jnp.float32).reshape(tokens_here, key_heads, DK)).astype(
        jnp.bfloat16
    )
    unit_k = unit_norm(keys_in.astype(jnp.float32).reshape(tokens_here, key_heads, DK)).astype(
        jnp.bfloat16
    )
    queries = jnp.repeat(unit_q, group_size, axis=1)
    key_rows = jnp.repeat(unit_k, group_size, axis=1)
    value_rows = values_in.astype(jnp.float32).reshape(tokens_here, head_count, DV)

    def blocks(rows):
        return rows.reshape(local_stretches, STRETCH, head_count, rows.shape[-1]).transpose(
            0, 2, 1, 3
        )

    decay_blocks = log_decay.reshape(head_count, local_stretches, STRETCH).transpose(1, 0, 2)
    beta_blocks = write_strength.reshape(head_count, local_stretches, STRETCH).transpose(1, 0, 2)
    position = lax.axis_index("outer") * lax.axis_size("ctx") + lax.axis_index("ctx")
    starts = jnp.cumsum(doc_lengths) - doc_lengths
    stretch_ids = position * local_stretches + jnp.arange(local_stretches, dtype=jnp.int32)
    keep_flags = 1.0 - jnp.any(stretch_ids[:, None] == starts[None, :], axis=1).astype(jnp.float32)
    wy_keys, wy_values, decayed_query, intra_scores, decayed_keys, stretch_decay = stretch_parts(
        blocks(queries), blocks(key_rows), blocks(value_rows), decay_blocks, beta_blocks
    )
    identity_mat = jnp.broadcast_to(jnp.eye(DK, dtype=jnp.float32), (head_count, DK, DK))
    zero_state = jnp.zeros((head_count, DK, DV), jnp.float32)
    identity_pair = (identity_mat, zero_state)
    transition = stretch_decay[..., None] * jnp.eye(DK, dtype=jnp.float32) - jnp.einsum(
        "nhcd,nhce->nhde", decayed_keys, wy_keys, precision=lax.Precision.HIGHEST
    )
    transition = transition * keep_flags[:, None, None, None]
    own_state = jnp.einsum(
        "nhcd,nhce->nhde", decayed_keys, wy_values, precision=lax.Precision.HIGHEST
    )

    def fold_stretch(carried, inputs):
        step_map, step_state = inputs
        return (combine(carried, (step_map, step_state)), None)

    (block_m, block_b), _ = lax.scan(fold_stretch, identity_pair, (transition, own_state))
    before = carried_in((block_m, block_b), "ctx", combine, identity_pair)
    through = combine(before, (block_m, block_b))
    joined = from_root(jnp.concatenate(through, axis=2), "ctx", lax.axis_size("ctx") - 1)
    group_pair = (joined[:, :, :DK], joined[:, :, DK:])
    outer_before = carried_in(group_pair, "outer", combine, identity_pair)
    state_in = matmul_heads(before[0], outer_before[1]) + before[1]

    def advance(state_now, inputs):
        step_keys, step_values, step_query, step_scores, step_decayed, step_decay, keep_one = inputs
        state_now = state_now * keep_one
        fresh_vals = step_values - matmul_heads(step_keys, state_now)
        step_out = matmul_heads(step_query, state_now) + matmul_heads(step_scores, fresh_vals)
        state_now = step_decay[..., None] * state_now + jnp.einsum(
            "hcd,hce->hde", step_decayed, fresh_vals, precision=lax.Precision.HIGHEST
        )
        return (state_now, step_out)

    _, stretch_outs = lax.scan(
        advance,
        state_in,
        (wy_keys, wy_values, decayed_query, intra_scores, decayed_keys, stretch_decay, keep_flags),
    )
    core = stretch_outs.transpose(0, 2, 1, 3).reshape(tokens_here, head_count, DV)
    gate_rows = gate_in.astype(jnp.float32).reshape(tokens_here, head_count, DV)
    normed = core * lax.rsqrt(jnp.mean(core * core, axis=-1, keepdims=True) + 1e-06)
    gated = (
        (normed * norm_gain * jax.nn.silu(gate_rows))
        .astype(jnp.bfloat16)
        .reshape(tokens_here, head_count * DV)
    )
    mixed = lax.psum_scatter(
        jnp.dot(gated, out_weight, preferred_element_type=jnp.float32),
        "tp",
        scatter_dimension=0,
        tiled=True,
    )
    return mixed.astype(jnp.bfloat16)


def solution(mesh):
    in_specs = (
        P(("outer", "ctx"), "tp"),
        P(("outer", "ctx"), "tp"),
        P(("outer", "ctx"), "tp"),
        P(("outer", "ctx"), "tp"),
        P("tp", ("outer", "ctx")),
        P("tp", ("outer", "ctx")),
        P(),
        P(),
        P("tp", None),
    )
    out_specs = P(("outer", "ctx", "tp"), None)
    return jax.shard_map(shards, mesh=mesh, in_specs=in_specs, out_specs=out_specs, check_vma=False)
```

profile of v0, /device:TPU:0, one launch (start us, length us, event | category | flops | bytes accessed | tf_op | source)
XLA Modules:
  0.0 413.7 jit_solution(5998886388961936692)
XLA Ops:
  17.4 2.7 add_add_fusion
  20.1 2.3 fusion.99
  22.4 11.2 %convolution_add_fusion.6 = f32[8,8,64,64]{3,2,1,0:T(8,128)S(1)} fusion(f32[8,8,64,64]{3,2,1,0:T(8,128)S(1)} %add_add_fusion, f32[8,8,64,64]{3,2,1,0:T(8,128)S(1)} %fusion.98), kind=kOutput, calls=%fused_computation.93 | convolution fusion | flops 201588736 | bytes 3145728 | tf_op jit(solution)/shard_map/...ij,...jk->...ik/dot_general | solution.py:38
  35.9 2.3 fusion.100
  38.2 2.3 fusion.102
  40.5 2.5 convolution_add_fusion.5
  43.8 2.5 fusion.103
  46.3 3.0 convert_multiply_fusion.2
  49.4 4.3 %fusion.50 = f32[8,8,64,256]{3,2,1,0:T(8,128)S(1)} fusion(f32[8,8,64,128]{3,2,1,0:T(8,128)S(1)} %get-tuple-element.478, f32[8,8,64,128]{3,2,1,0:T(8,128)S(1)} %get-tuple-element.469, f32[8,8,64,64]{3,2,1,0:T(8,128)S(1)} %convolution_add_fusion.5, f32[8,8,64,64]{3,2,1,0:T(8,128)S(1)} %fusion.103), kind=kOutput, calls=%fused_computation.58 | convolution fusion | flops 806617088 | bytes 10485760 | tf_op jit(solution)/shard_map/...ij,...jk->...ik/dot_general | solution.py:38
  55.6 8.8 %fusion.81 = f32[8,8,128,128]{3,2,1,0:T(8,128)} fusion(f32[8,8,64]{2,1,0:T(8,128)S(1)} %get-tuple-element.474, bf16[8,64,8,128]{3,1,0,2:T(8,128)(2,1)S(1)} %bitcast.170, f32[8,8,64,256]{3,2,1,0:T(8,128)S(1)} %fusion.50), kind=kOutput, calls=%fused_computation.108 | convolution fusion | flops 806354944 | bytes 7372800 | tf_op jit(solution)/shard_map/nhcd,nhce->nhde/dot_general | solution.py:141
  64.9 11.0 %subtract_multiply_fusion = f32[8,8,128,128]{3,2,1,0:T(8,128)} fusion(f32[8]{0:T(128)S(1)} %convert_subtract_fusion, f32[128,128]{1,0:T(8,128)S(1)} %fusion.86, f32[8,8]{1,0:T(8,128)S(1)} %get-tuple-element.413, f32[8,8,64]{2,1,0:T(8,128)S(1)} %get-tuple-element.474, bf16[8,64,8,128]{3,1,0,2:T(8,128)(2,1)S(1)} %bitcast.171, f32[8,8,64,256]{3,2,1,0:T(8,128)} %copy-done.3), kind=kOutput, calls=%fused_computation.62 | convolution fusion | flops 809500672 | bytes 7422240 | tf_op jit(solution)/shard_map/nhcd,nhce->nhde/dot_general | solution.py:137
  75.9 29.6 %while.56 = (s32[]{:T(128)}, f32[8,128,128]{2,1,0:T(8,128)S(1)}, f32[8,128,128]{2,1,0:T(8,128)S(1)}, f32[8,8,128,128]{3,2,1,0:T(8,128)}, f32[8,8,128,128]{3,2,1,0:T(8,128)}, /*index=5*/s32[]{:T(128)}, s32[]{:T(128)}) while((s32[]{:T(128)}, f32[8,128,128]{2,1,0:T(8,128)S(1)}, f32[8,128,128]{2,1,0:T(8,128)S(1)}, ...), condition=%wide.region_5.6_spmd.clone, body=%wide.region_4.5_spmd.clone.sunk | while | flops 402915328 | bytes 5768791 | solution.py:149
  108.4 9.8 %all-gather.9.cloned.1.call-done = f32[16,128,128]{2,1,0:T(8,128)} async-done(((f32[8,128,128]{2,1,0:T(8,128)}), f32[16,128,128]{2,1,0:T(8,128)}) %all-gather.9.cloned.1.call-update) | async-done | bytes 1048592 | tf_op jit(solution)/shard_map/all_gather | solution.py:13
  118.3 11.8 %all-gather.11.cloned.1.call-done = f32[16,128,128]{2,1,0:T(8,128)} async-done(((f32[8,128,128]{2,1,0:T(8,128)}), f32[16,128,128]{2,1,0:T(8,128)}) %all-gather.11.cloned.1.call-update) | async-done | bytes 1048592 | tf_op jit(solution)/shard_map/all_gather | solution.py:13
  130.1 5.6 %while.57 = (s32[]{:T(128)}, f32[8,128,128]{2,1,0:T(8,128)S(1)}, f32[8,128,128]{2,1,0:T(8,128)S(1)}, s32[]{:T(128)}, f32[2,8,128,128]{3,2,1,0:T(8,128)}, /*index=5*/f32[2,8,128,128]{3,2,1,0:T(8,128)}, s32[]{:T(128)}, s32[]{:T(128)}) while((s32[]{:T(128)}, f32[8,128,128]{2,1,0:T(8,128)S(1)}, f32[8,128,128]{2,1,0:T(8,128)S(1)}, ...), condition=%wide.region_7.8_spmd.clone, body=%wide.region_6.7_spmd.clone.sunk | while | flops 403308544 | bytes 11012744 | solution.py:25
  138.9 20.9 %all-reduce.2.cloned.1.call-done = f32[8,128,256]{1,2,0:T(8,128)} async-done(((f32[8,128,256]{1,2,0:T(8,128)}), f32[8,128,256]{1,2,0:T(8,128)}) %all-reduce.2.cloned.1.call-update) | async-done | bytes 1048592 | tf_op jit(solution)/shard_map/psum | solution.py:30
  173.0 2.5 fusion.94
  175.5 33.8 %all-gather.13.cloned.1.call-done = f32[32,128,128]{2,1,0:T(8,128)} async-done(((f32[8,128,128]{2,1,0:T(8,128)}), f32[32,128,128]{2,1,0:T(8,128)}) %all-gather.13.cloned.1.call-update) | async-done | bytes 2097168 | tf_op jit(solution)/shard_map/all_gather | solution.py:13
  209.4 46.2 %all-gather.15.cloned.1.call-done = f32[32,128,128]{2,1,0:T(8,128)} async-done(((f32[8,128,128]{2,1,0:T(8,128)}), f32[32,128,128]{2,1,0:T(8,128)}) %all-gather.15.cloned.1.call-update) | async-done | bytes 2097168 | tf_op jit(solution)/shard_map/all_gather | solution.py:13
  255.5 7.9 %while.58 = (s32[]{:T(128)}, f32[8,128,128]{2,1,0:T(8,128)S(1)}, s32[]{:T(128)}, f32[4,8,128,128]{3,2,1,0:T(8,128)}, f32[4,8,128,128]{3,2,1,0:T(8,128)}, /*index=5*/s32[]{:T(128)}, s32[]{:T(128)}) while((s32[]{:T(128)}, f32[8,128,128]{2,1,0:T(8,128)S(1)}, s32[]{:T(128)}, f32[4,8,128,128]{3,2,1,0:T(8,128)}, ...), condition=%wide.region_10.11_spmd.clone, body=%wide.region_9.10_spmd.clone.sunk | while | flops 201850880 | bytes 3672671 | solution.py:25
  264.1 79.0 %while.55 = (s32[]{:T(128)}, f32[8,128,128]{2,1,0:T(8,128)S(1)}, f32[8,8,64,128]{3,2,1,0:T(8,128)}, f32[8,8,1]{1,2,0:T(1,128)S(1)}, f32[8]{0:T(128)S(1)}, /*inde...) while((s32[]{:T(128)}, f32[8,128,128]{2,1,0:T(8,128)S(1)}, ...), condition=%wide.region_13.14_spmd, body=%wide.region_12.13_spmd.sunk | while | flops 353107968 | bytes 4985565 | solution.py:167
  271.2 2.7 convolution_add_fusion.11
  281.1 2.7 convolution_add_fusion.11
  291.0 2.7 convolution_add_fusion.11
  300.9 2.7 convolution_add_fusion.11
  310.7 2.7 convolution_add_fusion.11
  320.6 2.7 convolution_add_fusion.11
  330.4 2.7 convolution_add_fusion.11
  340.3 2.7 convolution_add_fusion.11
  343.1 2.4 multiply_reduce_fusion
  348.3 4.7 %fusion.73 = f32[512,2048]{1,0:T(8,128)} fusion(bf16[1024,2048]{1,0:T(8,128)(2,1)S(1)} %copy-done.14, bf16[512,1024]{1,0:T(8,128)(2,1)S(1)} %copy-done.15, f32[64,8,8,128]{3,2,1,0:T(8,128)S(1)} %bitcast.180, f32[64,8,8,128]{3,2,1,0:T(8,128)S(1)} %bitcast.181, f32[1024]{0:T(1024)S(1)} %broadcast_bitcast_fusion), kind=kOutput, calls=%fused_computation.96 | convolution fusion | flops 2152202240 | bytes 13635584 | tf_op jit(solution)/shard_map/dot_general | solution.py:181
  353.0 51.6 %reduce-scatter.2.cloned.1.call-done = f32[128,2048]{1,0:T(8,128)} async-done(((f32[512,2048]{1,0:T(8,128)}), f32[128,2048]{1,0:T(8,128)}) %reduce-scatter.2.cloned.1.call-update) | async-done | bytes 1048592 | tf_op jit(solution)/shard_map/reduce_scatter | solution.py:180
  (191 shorter events, 140.2 us)
Async XLA Ops:
  6.5 161.2 %copy-start = (f32[128]{0:T(128)S(1)}, f32[128]{0:T(128)}, u32[]{:S(2)}) copy-start(f32[128]{0:T(128)} %param.24) | copy-start | bytes 1540
  6.5 111.7 %all-gather.9.cloned.1.call-start = ((), (), s32[]{:S(2)}) async-start(), calls=%async_computation.3 | async-start | bytes 1572864 | tf_op jit(solution)/shard_map/all_gather | solution.py:13
  8.0 1.5 copy-start.11
  8.0 1.6 copy-start.12
  40.5 2.6 copy-start.9
  53.7 1.9 copy-start.3
  55.6 8.8 %copy-start.13 = (s32[8]{0:T(128)S(1)}, s32[8]{0:T(128)}, u32[]{:S(2)}) copy-start(s32[8]{0:T(128)} %param.23) | copy-start | bytes 100
  105.6 0.8 copy-start.1
  105.6 1.0 copy-start.6
  106.4 23.7 %all-gather.11.cloned.1.call-start = ((), (), s32[]{:S(2)}) async-start(), calls=%async_computation.4 | async-start | bytes 1572864 | tf_op jit(solution)/shard_map/all_gather | solution.py:13
  107.1 52.7 %all-reduce.2.cloned.1.call-start = ((), (), s32[]{:S(2)}) async-start(), calls=%async_computation.1 | async-start | bytes 2097152 | tf_op jit(solution)/shard_map/psum | solution.py:30
  130.1 5.6 %copy-start.2 = (f32[8,128,128]{2,1,0:T(8,128)S(1)}, f32[8,128,128]{2,1,0:T(8,128)}, u32[]{:S(2)}) copy-start(f32[8,128,128]{2,1,0:T(8,128)} %copy-done.1) | copy-start | bytes 1572868
  130.1 2.1 copy-start.5
  132.9 2.1 copy-start.5
  138.9 70.5 %all-gather.13.cloned.1.call-start = ((), (), s32[]{:S(2)}) async-start(), calls=%async_computation.5 | async-start | bytes 2621440 | tf_op jit(solution)/shard_map/all_gather | solution.py:13
  162.1 1.2 copy-start.10
  162.1 93.5 %all-gather.15.cloned.1.call-start = ((), (), s32[]{:S(2)}) async-start(), calls=%async_computation.6 | async-start | bytes 2621440 | tf_op jit(solution)/shard_map/all_gather | solution.py:13
  163.2 241.5 %reduce-scatter.2.cloned.1.call-start = ((), (), s32[]{:S(2)}) async-start(), calls=%async_computation.2 | async-start | bytes 5242880 | tf_op jit(solution)/shard_map/reduce_scatter | solution.py:180
  164.6 2.0 copy-start.7
  169.8 3.2 copy-start.4
  343.0 2.5 copy-start.8
  345.6 2.2 copy-start.14
  346.8 1.5 copy-start.15
Sparse Core Ops, SparseCore 0:
  106.5 11.7 all-gather.8
  119.8 10.1 all-gather.10
  139.0 20.7 all-reduce.1
  162.2 47.1 all-gather.12
  210.9 44.6 all-gather.14
  353.2 51.4 reduce-scatter.1
where the time goes:
time: 421 us; the launch traced here: 414 us
  matrix products  183 us (43%)
  waiting for transfers between devices  175 us (42%)
  local copies, waits for them, and re-layouts  23.7 us (6%)
  other arithmetic  17.3 us (4%)
  between operations  14.2 us (3%)
    dot_general x62, matrix products, matmul_heads(): jnp.einsum('...ij,...jk->...ik', left, right, precision=lax.Precision.HIG...  133 us
    all_gather x4, waiting for transfers between devices, carried_in(): everything = jax.tree.map(lambda part: lax.all_gather(part, axis), shard)  102 us
    reduce_scatter x1, waiting for transfers between devices, shards(): lax.psum_scatter(jnp.dot(gated, out_weight, preferred_element_type=jnp.fl...  51.6 us
    dot_general x8, matrix products, advance(): jnp.einsum('hcd,hce->hde', step_decayed, fresh_vals, precision=lax.Precis...  21.8 us
    psum x1, waiting for transfers between devices, from_root(): return lax.psum(kept, axis)  20.9 us
    dot_general x1, matrix products, shards(): jnp.einsum('nhcd,nhce->nhde', decayed_keys, wy_keys, precision=lax.Precis...  11 us
    dot_general x1, matrix products, shards(): jnp.einsum('nhcd,nhce->nhde', decayed_keys, wy_values, precision=lax.Prec...  8.84 us
  transfers between devices with their start and end apart: 6, of which 6 were waited for; matrix products, arithmetic and copies ran while one was open for 3% of the time, Pallas kernels for 0%

commit v1 on v0

v1 whole, which is shorter than its diff:
```python
import functools

import jax
import jax.numpy as jnp
from jax import lax
from jax.experimental import pallas as pl
from jax.experimental.pallas import tpu as pltpu
from jax.sharding import PartitionSpec as P

DK = 128
DV = 128
STRETCH = 64
CHUNK = 2 * STRETCH
F32 = jnp.float32
BF16 = jnp.bfloat16
VMEM_LIMIT = 56 * 1024 * 1024
FAR = 1e30


def mm(left, right):
    return jnp.dot(left, right, preferred_element_type=F32)


def unit_rows(ref, rows):
    raw = ref[rows, :].astype(F32)
    return (raw * lax.rsqrt(jnp.sum(raw * raw, axis=-1, keepdims=True) + 1e-6)).astype(BF16)


def local_kernel(
    chunks, key_heads, place_ref, docs_ref, q_ref, k_ref, v_ref, decay_ref, beta_ref, theirs_ref, mine_ref, reach_ref, core_ref
):
    step = pl.program_id(0)
    key_head = lax.rem(step + place_ref[0], key_heads)
    row = lax.broadcasted_iota(jnp.int32, (CHUNK, CHUNK), 0)
    col = lax.broadcasted_iota(jnp.int32, (CHUNK, CHUNK), 1)
    upper = (row <= col).astype(F32)
    eye = (row == col).astype(F32)
    strict = (row > col).astype(F32)
    crossing = (row >= STRETCH) & (col < STRETCH)
    tri_bias = jnp.where(row >= col, 0.0, -FAR)
    masks = {}
    span = 1
    while span < CHUNK:
        odd_row = lax.rem(row // span, 2) == 1
        masks[span] = (odd_row & (col // span == row // span - 1)).astype(F32).astype(BF16)
        span *= 2
    second = lax.broadcasted_iota(jnp.int32, (1, CHUNK), 1) >= STRETCH
    second_col = lax.broadcasted_iota(jnp.int32, (CHUNK, 1), 0) >= STRETCH

    starts, total = [], jnp.int32(0)
    for j in range(docs_ref.shape[0]):
        starts.append(total)
        total = total + docs_ref[j]

    def keep_flag(stretch):
        here = place_ref[1] * (2 * chunks) + stretch
        hit = here == starts[0]
        for s in starts[1:]:
            hit = hit | (here == s)
        return jnp.where(hit, 0.0, 1.0).astype(F32)

    keeps = [(keep_flag(2 * n), keep_flag(2 * n + 1)) for n in range(chunks)]
    heads_all = decay_ref.shape[0]
    turn = lax.rem(heads_all - 2 * key_head, heads_all)

    units = []
    for n in range(chunks):
        rows = slice(n * CHUNK, (n + 1) * CHUNK)
        k_unit, q_unit = unit_rows(k_ref, rows), unit_rows(q_ref, rows)
        k_turned = k_unit.astype(F32).T.astype(BF16)
        grams = mm(jnp.concatenate([k_unit, q_unit], axis=0), k_turned)
        key_gram, query_gram = grams[:CHUNK], grams[CHUNK:]
        decay = pltpu.roll(decay_ref[:, rows], turn, 0)
        beta = pltpu.roll(beta_ref[:, rows], turn, 0)
        cum = jnp.dot(decay, upper, precision=lax.Precision.HIGHEST, preferred_element_type=F32)
        cum_col, beta_col = cum.T, beta.T
        k1, k2 = keeps[n]
        bias = tri_bias + jnp.where(crossing, (k2 - 1.0) * FAR, 0.0)
        entry = jnp.where(second, k1 * k2, k1)
        leave = jnp.where(second, 1.0, k2)
        entry_col = jnp.where(second_col, k1 * k2, k1)
        for e in range(2):
            c_row, c_col = cum[e : e + 1, :], cum_col[:, e : e + 1]
            b_row = beta[e : e + 1, :]
            fade = jnp.exp((c_col - c_row) + bias)
            noise = (key_gram * fade * beta_col[:, e : e + 1] * strict).astype(BF16)
            last = c_row[:, CHUNK - 1 : CHUNK]
            units.append(
                dict(
                    n=n,
                    e=e,
                    noise=noise,
                    scores=(query_gram * fade).astype(BF16),
                    b_row=b_row,
                    be_row=b_row * jnp.exp(c_row) * entry,
                    q_in=q_unit.astype(F32) * (jnp.exp(c_col) * entry_col),
                    k_out=(k_turned.astype(F32) * (jnp.exp(last - c_row) * leave)).astype(BF16),
                    through=jnp.exp(last) * (k1 * k2),
                    k=k_unit,
                )
            )

    inverses = [eye - (u["noise"] * masks[1]).astype(F32) for u in units]
    span = 2
    while span < CHUNK:
        held = [t.astype(BF16) for t in inverses]
        half = [mm(t, u["noise"] * masks[span]).astype(BF16) for t, u in zip(held, units)]
        inverses = [t - mm(h, b) for t, h, b in zip(inverses, half, held)]
        span *= 2
    outs = []
    for u, t in zip(units, inverses):
        rows = slice(u["n"] * CHUNK, (u["n"] + 1) * CHUNK)
        values = v_ref[rows, u["e"] * DV : (u["e"] + 1) * DV]
        wy_values = mm((t * u["b_row"]).astype(BF16), values)
        wy_keys = mm((t * u["be_row"]).astype(BF16), u["k"])
        pair = jnp.concatenate([wy_keys, wy_values], axis=1).astype(BF16)
        moved = mm(u["k_out"], pair)
        seen = mm(u["scores"], pair)
        outs.append((moved, u["q_in"] - seen[:, :DK], seen[:, DK:], u["through"]))

    for e in range(2):
        cols = slice(e * DV, (e + 1) * DV)
        carried = None
        for n in range(chunks):
            moved, q_eff, own, through = outs[2 * n + e]
            rows = slice(n * CHUNK, (n + 1) * CHUNK)
            if carried is None:
                reach_ref[rows, cols] = q_eff.astype(BF16)
                core_ref[rows, cols] = own
                carried = jnp.concatenate([eye * through - moved[:, :DK], moved[:, DK:]], axis=1)
            else:
                held = carried.astype(BF16)
                read = mm(q_eff.astype(BF16), held)
                reach_ref[rows, cols] = read[:, :DK].astype(BF16)
                core_ref[rows, cols] = read[:, DK:] + own
                step_map = mm(moved[:, :DK].astype(BF16), held)
                carried = carried * through - step_map
                carried = jnp.concatenate([carried[:, :DK], carried[:, DK:] + moved[:, DK:]], axis=1)

        @pl.when(step < key_heads // 2)
        def _():
            theirs_ref[e] = carried

        @pl.when(step >= key_heads // 2)
        def _():
            mine_ref[e] = carried


def local_maps(place, docs, queries, keys, values, decay, beta):
    tokens, key_width = queries.shape
    key_heads = key_width // DK
    heads = decay.shape[0]
    chunks = tokens // CHUNK
    half = key_heads // 2

    def head_block(i, place_ref, docs_ref):
        return (0, lax.rem(i + place_ref[0], key_heads))

    whole = lambda i, place_ref, docs_ref: (0, 0)
    return pl.pallas_call(
        functools.partial(local_kernel, chunks, key_heads),
        out_shape=[
            jax.ShapeDtypeStruct((heads // 2, DK, DK + DV), F32),
            jax.ShapeDtypeStruct((heads // 2, DK, DK + DV), F32),
            jax.ShapeDtypeStruct((tokens, heads * DV), BF16),
            jax.ShapeDtypeStruct((tokens, heads * DV), F32),
        ],
        grid_spec=pltpu.PrefetchScalarGridSpec(
            num_scalar_prefetch=2,
            grid=(key_heads,),
            in_specs=[
                pl.BlockSpec((tokens, DK), head_block),
                pl.BlockSpec((tokens, DK), head_block),
                pl.BlockSpec((tokens, 2 * DV), head_block),
                pl.BlockSpec((heads, tokens), whole),
                pl.BlockSpec((heads, tokens), whole),
            ],
            out_specs=[
                pl.BlockSpec((2, DK, DK + DV), lambda i, p, d: (jnp.minimum(i, half - 1), 0, 0)),
                pl.BlockSpec((2, DK, DK + DV), lambda i, p, d: (jnp.maximum(i - half, 0), 0, 0)),
                pl.BlockSpec((tokens, 2 * DV), head_block),
                pl.BlockSpec((tokens, 2 * DV), head_block),
            ],
        ),
        compiler_params=pltpu.CompilerParams(vmem_limit_bytes=VMEM_LIMIT),
        name="local_maps",
    )(place, docs, queries, keys, values, decay, beta)


def finish_kernel(
    heads, place_ref, reach_ref, core_ref, gate_ref, gain_ref, kept_ref, got_ref, weight_ref,
    send_x_ref, send_y_ref, keep_l_ref, keep_r_ref, gated_ref,
):
    step = pl.program_id(0)
    gain = gain_ref[...]
    first = place_ref[1]
    half = heads // 2
    for side, state_ref in enumerate((kept_ref, got_ref)):
        for j in range(half):
            head = first + j if side == 0 else half - first + j
            cols = pl.ds(pl.multiple_of(head * DV, DV), DV)
            core = core_ref[:, cols] + mm(reach_ref[:, cols], state_ref[j].astype(BF16))
            gate = gate_ref[:, cols].astype(F32)
            normed = core * lax.rsqrt(jnp.mean(core * core, axis=-1, keepdims=True) + 1e-6)
            gated_ref[:, cols] = (normed * gain * (gate / (1.0 + jnp.exp(-gate)))).astype(BF16)
    width = weight_ref.shape[1] // 2
    left = mm(gated_ref[...], weight_ref[:, :width])
    right = mm(gated_ref[...], weight_ref[:, width:])
    for i, (l_ref, l_at, r_ref, r_at) in enumerate(
        (
            (keep_l_ref, 0, keep_r_ref, 0),
            (send_x_ref, 0, keep_r_ref, 1),
            (keep_l_ref, 1, send_y_ref, 0),
            (send_x_ref, 1, send_y_ref, 1),
        )
    ):

        @pl.when(step == i)
        def _(l_ref=l_ref, l_at=l_at, r_ref=r_ref, r_at=r_at):
            l_ref[l_at] = left
            r_ref[r_at] = right


def finish(place, reach, core, gate, gain, kept, got, weight):
    tokens, depth = reach.shape
    width = weight.shape[1] // 2
    heads = depth // DV
    rows = tokens // 4
    row_block = lambda i, place_ref: (i ^ place_ref[0], 0)
    part = jax.ShapeDtypeStruct((2, rows, width), F32)
    part_spec = pl.BlockSpec((2, rows, width), lambda i, p: (0, 0, 0))
    return pl.pallas_call(
        functools.partial(finish_kernel, heads),
        out_shape=[part] * 4,
        grid_spec=pltpu.PrefetchScalarGridSpec(
            num_scalar_prefetch=1,
            grid=(4,),
            in_specs=[
                pl.BlockSpec((rows, depth), row_block),
                pl.BlockSpec((rows, depth), row_block),
                pl.BlockSpec((rows, depth), row_block),
                pl.BlockSpec((1, DV), lambda i, p: (0, 0)),
                pl.BlockSpec(kept.shape, lambda i, p: (0, 0, 0)),
                pl.BlockSpec(got.shape, lambda i, p: (0, 0, 0)),
                pl.BlockSpec(weight.shape, lambda i, p: (0, 0)),
            ],
            out_specs=[part_spec] * 4,
            scratch_shapes=[pltpu.VMEM((rows, depth), BF16)],
        ),
        compiler_params=pltpu.CompilerParams(vmem_limit_bytes=VMEM_LIMIT),
        name="finish",
    )(place, reach, core, gate, gain.reshape(1, DV), kept, got, weight)


def precise(left, right):
    return jnp.einsum("hij,hjk->hik", left, right, precision=lax.Precision.HIGHEST)


def combine(earlier, later):
    joined = precise(later[..., :DK], earlier)
    return jnp.concatenate([joined[..., :DK], joined[..., DK:] + later[..., DK:]], axis=-1)


def apply_map(pair, state):
    return precise(pair[..., :DK], state) + pair[..., DK:]


def group_hops(pair_map, pair_state, outer):
    step = [(i, i + 1) for i in range(outer - 1)]
    state = lax.ppermute(pair_state, "outer", step)
    for _ in range(outer // 2 - 1):
        state = lax.ppermute(precise(pair_map, state) + pair_state, "outer", step)
    return state


def states_before(theirs, mine, ctx, outer):
    here = lax.axis_index("ctx")
    if ctx == 2:
        swap = [(0, 1), (1, 0)]
        other = lax.ppermute(theirs, "ctx", swap)
        is_first = here == 0
        first = jnp.where(is_first, mine, other)
        second = jnp.where(is_first, other, mine)
        group = combine(first, second)
        entering = group_hops(group[..., :DK], group[..., DK:], outer)
        middle = apply_map(first, entering)
        kept = jnp.where(is_first, entering, middle)
        got = lax.ppermute(jnp.where(is_first, middle, entering), "ctx", swap)
        return kept, got
    both = jnp.concatenate([mine, theirs], axis=0)
    blocks = lax.all_gather(both, "ctx")
    identity = jnp.concatenate([jnp.eye(DK, dtype=F32), jnp.zeros((DK, DV), F32)], axis=1)
    start = jnp.broadcast_to(identity, both.shape)

    def hop(k, carry):
        before, through = carry
        through = combine(through, blocks[k])
        return jnp.where(k < here, through, before), through

    before, through = lax.fori_loop(0, ctx, hop, (start, start))
    entering = group_hops(through[..., :DK], through[..., DK:], outer)
    state = apply_map(before, entering)
    half = mine.shape[0]
    return state[:half], state[half:]


def shards(ctx, outer, queries, keys, values, gate, decay, beta, docs, gain, weight):
    heads = decay.shape[0]
    key_heads = queries.shape[1] // DK
    half = key_heads // 2
    here = lax.axis_index("ctx")
    tp_here = lax.axis_index("tp")
    position = lax.axis_index("outer") * ctx + here
    second = here if ctx == 2 else 0 * here
    place = jnp.stack([half * (1 - second), position]).astype(jnp.int32)
    theirs, mine, reach, core = local_maps(place, docs, queries, keys, values, decay, beta)
    kept, got = states_before(theirs, mine, ctx, outer)
    place2 = jnp.stack([tp_here, second * (heads // 2)]).astype(jnp.int32)
    send_x, send_y, keep_l, keep_r = finish(place2, reach, core, gate, gain, kept, got, weight)
    along_x = [(i, i ^ 1) for i in range(4)]
    along_y = [(i, i ^ 2) for i in range(4)]
    got_x = lax.ppermute(send_x, "tp", along_x)
    got_y = lax.ppermute(send_y, "tp", along_y)
    last_l = lax.ppermute(keep_l[1] + got_x[1], "tp", along_y)
    last_r = lax.ppermute(keep_r[1] + got_y[1], "tp", along_x)
    out_l = keep_l[0] + got_x[0] + last_l
    out_r = keep_r[0] + got_y[0] + last_r
    return jnp.concatenate([out_l, out_r], axis=1).astype(BF16)


def solution(mesh):
    ctx, outer = mesh.shape["ctx"], mesh.shape["outer"]
    in_specs = (
        P(("outer", "ctx"), "tp"),
        P(("outer", "ctx"), "tp"),
        P(("outer", "ctx"), "tp"),
        P(("outer", "ctx"), "tp"),
        P("tp", ("outer", "ctx")),
        P("tp", ("outer", "ctx")),
        P(),
        P(),
        P("tp", None),
    )
    out_specs = P(("outer", "ctx", "tp"), None)
    return jax.shard_map(
        functools.partial(shards, ctx, outer), mesh=mesh, in_specs=in_specs, out_specs=out_specs, check_vma=False
    )
```

time: 421 us -> 106 us (0.25)
  the two profiles are of different devices: /device:TPU:0 before, /device:TPU:12 now
where the time goes in v1:
time: 106 us; the launch traced here: 104 us
  waiting for transfers between devices  49.4 us (47%)
  Pallas kernels  33.8 us (32%)
  starting transfers between devices  11.1 us (10%)
  other arithmetic  6.68 us (6%)
  matrix products  2.11 us (2%)
    ppermute x1, waiting for transfers between devices, shards(): got_x = lax.ppermute(send_x, 'tp', along_x)  23.4 us
    pallas_call x1, Pallas kernels, local_maps(): pl.pallas_call(functools.partial(local_kernel, chunks, key_heads), out_sh...  23.1 us
    pallas_call x1, Pallas kernels, finish(): pl.pallas_call(functools.partial(finish_kernel, heads), out_shape=[part]...  10.7 us
    ppermute x1, waiting for transfers between devices, shards(): last_l = lax.ppermute(keep_l[1] + got_x[1], 'tp', along_y)  9.99 us
    ppermute x1, waiting for transfers between devices, group_hops(): state = lax.ppermute(pair_state, 'outer', step)  6.75 us
    ppermute x1, waiting for transfers between devices, group_hops(): state = lax.ppermute(precise(pair_map, state) + pair_state, 'outer', step)  5.92 us
    ppermute x1, starting transfers between devices, group_hops(): state = lax.ppermute(precise(pair_map, state) + pair_state, 'outer', step)  3.49 us
    ppermute x1, starting transfers between devices, group_hops(): state = lax.ppermute(pair_state, 'outer', step)  3.49 us
  transfers between devices with their start and end apart: 8, of which 7 were waited for; matrix products, arithmetic and copies ran while one was open for 4% of the time, Pallas kernels for 0%

profile of v1, /device:TPU:12, one launch (start us, length us, event | category | flops | bytes accessed | tf_op | source)
XLA Modules:
  0.0 103.9 jit_solution(4608990511437414079)
XLA Ops:
  0.0 0.6 pad_add_fusion.1.place_ref
  0.6 23.1 %local_maps.1 = (f32[4,128,256]{2,1,0:T(8,128)}, f32[4,128,256]{2,1,0:T(8,128)}, bf16[512,1024]{1,0:T(8,128)(2,1)}, f32[512,1024]{1,0:T(8,128)}) custom-call(s32[2]{0:T(128)} %pad_add_fusion.1.place_ref, s32[8]{0:T(128)} %docs_ref.1, bf16[512,512]{1,0:T(8,128)(2,1)} %q_ref.1, bf16[512,512]{1,0:T(8,128)(2,1)} %k_ref.1, bf16[512,1024]{1,0:T(8,128)(2,1)} %v_ref.1, ...), custom_call_target="tpu_custom_call" | custom-call | tf_op jit(solution)/shard_map/local_maps/pallas_call | solution.py:160
  23.8 0.0 collective-permute-start
  23.8 2.1 %collective-permute-done = f32[4,128,256]{2,1,0:T(8,128)S(1)} collective-permute-done((f32[4,128,256]{2,1,0:T(8,128)}, f32[4,128,256]{2,1,0:T(8,128)S(1)}, u32[]{:S(2)}, u32[]{:S(2)}) %collective-permute-start) | collective-permute-done | bytes 524320 | tf_op jit(solution)/shard_map/ppermute | solution.py:280
  25.9 1.1 %broadcast_select_fusion = (f32[4,128,256]{2,1,0:T(8,128)S(1)}, f32[4,128,256]{2,1,0:T(8,128)S(1)}) fusion(f32[4,128,256]{2,1,0:T(8,128)} %get-tuple-element.16, f32[4,128,256]{2,1,0:T(8,128)S(1)} %collective-permute-done, pred[]{:T(512)S(6)} %eq.3), kind=kLoop, calls=%fused_computation.20 | loop fusion | flops 262144 | bytes 2097153 | tf_op jit(solution)/shard_map/jit(_where)/select_n | solution.py:282
  27.0 0.6 fusion.10
  27.7 3.5 %collective-permute-start.1 = (f32[4,128,128]{2,1,0:T(8,128)S(1)}, f32[4,128,128]{2,1,0:T(8,128)S(1)}, u32[]{:S(2)}, u32[]{:S(2)}) collective-permute-start(f32[4,128,128]{2,1,0:T(8,128)S(1)} %slice_add_fusion.4), channel_id=1, source_target_pairs={{0,1},{1,2},{2,3},{4,5},{5,6},{6,7},{8,9},{9,10},{10,11},{12,13},{... | collective-permute-start | bytes 786440 | tf_op jit(solution)/shard_map/ppermute | solution.py:270
  31.2 6.7 %collective-permute-done.1 = f32[4,128,128]{2,1,0:T(8,128)S(1)} collective-permute-done((f32[4,128,128]{2,1,0:T(8,128)S(1)}, f32[4,128,128]{2,1,0:T(8,128)S(1)}, u32[]{:S(2)}, u32[]{:S(2)}) %collective-permute-start.1) | collective-permute-done | bytes 262176 | tf_op jit(solution)/shard_map/ppermute | solution.py:270
  37.9 0.4 convolution_add_fusion.1
  38.3 3.5 %collective-permute-start.2 = (f32[4,128,128]{2,1,0:T(8,128)S(1)}, f32[4,128,128]{2,1,0:T(8,128)S(1)}, u32[]{:S(2)}, u32[]{:S(2)}) collective-permute-start(f32[4,128,128]{2,1,0:T(8,128)S(1)} %convolution_add_fusion.1), channel_id=1, source_target_pairs={{0,1},{1,2},{2,3},{4,5},{5,6},{6,7},{8,9},{9,10},{10,11},{12,13},{... | collective-permute-start | bytes 786440 | tf_op jit(solution)/shard_map/ppermute | solution.py:272
  41.8 5.9 %collective-permute-done.2 = f32[4,128,128]{2,1,0:T(8,128)S(1)} collective-permute-done((f32[4,128,128]{2,1,0:T(8,128)S(1)}, f32[4,128,128]{2,1,0:T(8,128)S(1)}, u32[]{:S(2)}, u32[]{:S(2)}) %collective-permute-start.2) | collective-permute-done | bytes 262176 | tf_op jit(solution)/shard_map/ppermute | solution.py:272
  47.7 1.1 %broadcast_select_fusion.2 = (f32[4,128,128]{2,1,0:T(8,128)S(1)}, f32[4,128,128]{2,1,0:T(8,128)}) fusion(f32[4,128,128]{2,1,0:T(8,128)S(1)} %collective-permute-done.2, pred[]{:T(512)S(6)} %eq.3, f32[4,128,256]{2,1,0:T(8,128)S(1)} %get-tuple-element.21), kind=kOutput, calls=%fused_computation.22 | convolution fusion | flops 100859904 | bytes 1572865 | tf_op jit(solution)/shard_map/hij,hjk->hik/dot_general | solution.py:256
  48.9 0.0 collective-permute-start.3
  48.9 0.6 pad_add_fusion.place_ref
  49.5 0.9 collective-permute-done.3.got_ref
  50.4 0.0 copy-start.1
  50.4 0.7 copy-done.1
  51.1 10.7 %finish.1 = (f32[2,128,1024]{2,1,0:T(8,128)}, f32[2,128,1024]{2,1,0:T(8,128)}, f32[2,128,1024]{2,1,0:T(8,128)}, f32[2,128,1024]{2,1,0:T(8,128)}) custom-call(s32[2]{0:T(128)} %pad_add_fusion.place_ref, bf16[512,1024]{1,0:T(8,128)(2,1)} %get-tuple-element.13.reach_ref, f32[512,1024]{1,0:T(8,128)} %get-tuple-element.14.core_ref, bf16[512,1024]{1,0:T(8,128)(2,1)} %gate_ref.1, ...), custom_call_target="tpu_custom_call" | custom-call | tf_op jit(solution)/shard_map/finish/pallas_call | solution.py:232
  61.8 1.5 %collective-permute-start.4 = (f32[2,128,1024]{2,1,0:T(8,128)}, f32[2,128,1024]{2,1,0:T(8,128)S(1)}, u32[]{:S(2)}, u32[]{:S(2)}) collective-permute-start(f32[2,128,1024]{2,1,0:T(8,128)} %get-tuple-element.18), channel_id=1, source_target_pairs={{0,8},{8,0},{16,24},{24,16},{1,9},{9,1},{17,25},{25,17},{2,10},{10... | collective-permute-start | bytes 3145736 | tf_op jit(solution)/shard_map/ppermute | solution.py:322
  63.3 0.5 collective-permute-start.6
  63.8 23.4 %collective-permute-done.4 = f32[2,128,1024]{2,1,0:T(8,128)S(1)} collective-permute-done((f32[2,128,1024]{2,1,0:T(8,128)}, f32[2,128,1024]{2,1,0:T(8,128)S(1)}, u32[]{:S(2)}, u32[]{:S(2)}) %collective-permute-start.4) | collective-permute-done | bytes 1048608 | tf_op jit(solution)/shard_map/ppermute | solution.py:322
  87.2 1.1 %fusion.4 = f32[128,1024]{1,0:T(8,128)S(1)} fusion(f32[2,128,1024]{2,1,0:T(8,128)S(1)} %collective-permute-done.4, f32[2,128,1024]{2,1,0:T(8,128)} %get-tuple-element.17), kind=kLoop, calls=%fused_computation.9 | loop fusion | flops 131072 | bytes 1572864 | tf_op jit(solution)/shard_map/add | solution.py:324
  88.3 0.6 collective-permute-start.5
  88.9 0.0 collective-permute-done.6
  88.9 1.1 %fusion = f32[128,1024]{1,0:T(8,128)S(1)} fusion(f32[2,128,1024]{2,1,0:T(8,128)S(1)} %collective-permute-done.6, f32[2,128,1024]{2,1,0:T(8,128)} %get-tuple-element.19), kind=kLoop, calls=%fused_computation.3 | loop fusion | flops 131072 | bytes 1572864 | tf_op jit(solution)/shard_map/add | solution.py:325
  90.0 1.6 %collective-permute-start.7 = (f32[128,1024]{1,0:T(8,128)S(1)}, f32[128,1024]{1,0:T(8,128)S(1)}, u32[]{:S(2)}, u32[]{:S(2)}) collective-permute-start(f32[128,1024]{1,0:T(8,128)S(1)} %fusion), channel_id=1, source_target_pairs={{0,8},{8,0},{16,24},{24,16},{1,9},{9,1},{17,25},{25,17},{2,10},{10... | collective-permute-start | bytes 1572872 | tf_op jit(solution)/shard_map/ppermute | solution.py:325
  91.6 10.0 %collective-permute-done.5 = f32[128,1024]{1,0:T(8,128)S(1)} collective-permute-done((f32[128,1024]{1,0:T(8,128)S(1)}, f32[128,1024]{1,0:T(8,128)S(1)}, u32[]{:S(2)}, u32[]{:S(2)}) %collective-permute-start.5) | collective-permute-done | bytes 524320 | tf_op jit(solution)/shard_map/ppermute | solution.py:324
  101.6 1.1 %fusion.7 = bf16[128,1024]{1,0:T(8,128)(2,1)S(1)} fusion(f32[128,1024]{1,0:T(8,128)S(1)} %collective-permute-done.5, f32[2,128,1024]{2,1,0:T(8,128)S(1)} %collective-permute-done.4, f32[2,128,1024]{2,1,0:T(8,128)} %get-tuple-element.17), kind=kLoop, calls=%fused_computation.13 | loop fusion | flops 393216 | bytes 1835008 | tf_op jit(solution)/shard_map/convert
  102.7 0.3 collective-permute-done.7
  103.0 0.0 copy-done
  103.0 0.1 fusion.3
  103.1 0.8 pad_maximum_fusion
  (2 shorter events, 0.0 us)
Async XLA Ops:
  23.8 2.1 %collective-permute-start = (f32[4,128,256]{2,1,0:T(8,128)}, f32[4,128,256]{2,1,0:T(8,128)S(1)}, u32[]{:S(2)}, u32[]{:S(2)}) collective-permute-start(f32[4,128,256]{2,1,0:T(8,128)} %get-tuple-element.15), channel_id=1, source_target_pairs={{0,4},{4,0},{1,5},{5,1},{2,6},{6,2},{3,7},{7,3},{8,12},{12,8},{9,1... | collective-permute-start | bytes 1572872 | tf_op jit(solution)/shard_map/ppermute | solution.py:280
  27.7 10.2 %collective-permute-start.1 = (f32[4,128,128]{2,1,0:T(8,128)S(1)}, f32[4,128,128]{2,1,0:T(8,128)S(1)}, u32[]{:S(2)}, u32[]{:S(2)}) collective-permute-start(f32[4,128,128]{2,1,0:T(8,128)S(1)} %slice_add_fusion.4), channel_id=1, source_target_pairs={{0,1},{1,2},{2,3},{4,5},{5,6},{6,7},{8,9},{9,10},{10,11},{12,13},{... | collective-permute-start | bytes 786440 | tf_op jit(solution)/shard_map/ppermute | solution.py:270
  38.3 9.4 %collective-permute-start.2 = (f32[4,128,128]{2,1,0:T(8,128)S(1)}, f32[4,128,128]{2,1,0:T(8,128)S(1)}, u32[]{:S(2)}, u32[]{:S(2)}) collective-permute-start(f32[4,128,128]{2,1,0:T(8,128)S(1)} %convolution_add_fusion.1), channel_id=1, source_target_pairs={{0,1},{1,2},{2,3},{4,5},{5,6},{6,7},{8,9},{9,10},{10,11},{12,13},{... | collective-permute-start | bytes 786440 | tf_op jit(solution)/shard_map/ppermute | solution.py:272
  48.9 1.5 %collective-permute-start.3 = (f32[4,128,128]{2,1,0:T(8,128)S(1)}, f32[4,128,128]{2,1,0:T(8,128)S(1)}, u32[]{:S(2)}, u32[]{:S(2)}) collective-permute-start(f32[4,128,128]{2,1,0:T(8,128)S(1)} %get-tuple-element.23), channel_id=1, source_target_pairs={{0,4},{4,0},{1,5},{5,1},{2,6},{6,2},{3,7},{7,3},{8,12},{12,8},{9,1... | collective-permute-start | bytes 786440 | tf_op jit(solution)/shard_map/ppermute | solution.py:288
  50.4 0.7 copy-start.1
  61.8 41.2 %copy-start = (f32[2,128,1024]{2,1,0:T(8,128)S(1)}, f32[2,128,1024]{2,1,0:T(8,128)}, u32[]{:S(2)}) copy-start(f32[2,128,1024]{2,1,0:T(8,128)} %get-tuple-element.19) | copy-start | bytes 3145732
  61.8 25.4 %collective-permute-start.4 = (f32[2,128,1024]{2,1,0:T(8,128)}, f32[2,128,1024]{2,1,0:T(8,128)S(1)}, u32[]{:S(2)}, u32[]{:S(2)}) collective-permute-start(f32[2,128,1024]{2,1,0:T(8,128)} %get-tuple-element.18), channel_id=1, source_target_pairs={{0,8},{8,0},{16,24},{24,16},{1,9},{9,1},{17,25},{25,17},{2,10},{10... | collective-permute-start | bytes 3145736 | tf_op jit(solution)/shard_map/ppermute | solution.py:322
  63.3 25.6 %collective-permute-start.6 = (f32[2,128,1024]{2,1,0:T(8,128)}, f32[2,128,1024]{2,1,0:T(8,128)S(1)}, u32[]{:S(2)}, u32[]{:S(2)}) collective-permute-start(f32[2,128,1024]{2,1,0:T(8,128)} %get-tuple-element.20), channel_id=1, source_target_pairs={{0,16},{8,24},{16,0},{24,8},{1,17},{9,25},{17,1},{25,9},{2,18},{10... | collective-permute-start | bytes 3145736 | tf_op jit(solution)/shard_map/ppermute | solution.py:323
  88.3 13.2 %collective-permute-start.5 = (f32[128,1024]{1,0:T(8,128)S(1)}, f32[128,1024]{1,0:T(8,128)S(1)}, u32[]{:S(2)}, u32[]{:S(2)}) collective-permute-start(f32[128,1024]{1,0:T(8,128)S(1)} %fusion.4), channel_id=1, source_target_pairs={{0,16},{8,24},{16,0},{24,8},{1,17},{9,25},{17,1},{25,9},{2,18},{10... | collective-permute-start | bytes 1572872 | tf_op jit(solution)/shard_map/ppermute | solution.py:324
  90.0 12.9 %collective-permute-start.7 = (f32[128,1024]{1,0:T(8,128)S(1)}, f32[128,1024]{1,0:T(8,128)S(1)}, u32[]{:S(2)}, u32[]{:S(2)}) collective-permute-start(f32[128,1024]{1,0:T(8,128)S(1)} %fusion), channel_id=1, source_target_pairs={{0,8},{8,0},{16,24},{24,16},{1,9},{9,1},{17,25},{25,17},{2,10},{10... | collective-permute-start | bytes 1572872 | tf_op jit(solution)/shard_map/ppermute | solution.py:325

commit v2 on v1

v2 whole, which is shorter than its diff:
```python
import functools

import jax
import jax.numpy as jnp
from jax import lax
from jax.experimental import pallas as pl
from jax.experimental.pallas import tpu as pltpu
from jax.sharding import PartitionSpec as P

DK = 128
DV = 128
STRETCH = 64
CHUNK = 2 * STRETCH
F32 = jnp.float32
BF16 = jnp.bfloat16
MIB = 1024 * 1024
MAPS_VMEM = 48 * MIB
READ_VMEM = 12 * MIB
SMALL_VMEM = 4 * MIB
FINISH_VMEM = 16 * MIB
PARTS = (32, 48, 48)
PLACES = 6
FAR = 1e30


def mm(left, right):
    return jnp.dot(left, right, preferred_element_type=F32)


def unit_rows(raw):
    raw = raw.astype(F32)
    return raw * lax.rsqrt(jnp.sum(raw * raw, axis=-1, keepdims=True) + 1e-6)


def corners(left, right):
    nil = jnp.zeros_like(left)
    return jnp.concatenate(
        [jnp.concatenate([left, nil], axis=1), jnp.concatenate([nil, right], axis=1)], axis=0
    )


def doc_starts(place_ref):
    starts, total = [], jnp.int32(0)
    for j in range(PLACES, place_ref.shape[0]):
        starts.append(total)
        total = total + place_ref[j]
    return starts


def chunk_flags(first_stretch, starts, chunks):
    def flag(stretch):
        hit = stretch == starts[0]
        for s in starts[1:]:
            hit = hit | (stretch == s)
        return jnp.where(hit, 0.0, 1.0).astype(F32)

    return [(flag(first_stretch + 2 * n), flag(first_stretch + 2 * n + 1)) for n in range(chunks)]


def fade_bias(row, col, k2):
    crossing = (row >= STRETCH) & (col < STRETCH)
    return jnp.where(row >= col, 0.0, -FAR) + jnp.where(crossing, (k2 - 1.0) * FAR, 0.0)


def maps_kernel(
    chunks, key_heads, place_ref, k_hbm, v_hbm, rates_hbm,
    theirs_ref, mine_ref, pair_t_ref, pair_m_ref, held_t_ref, held_m_ref, cum_t_ref, cum_m_ref,
    k_ref, v_ref, rates_ref, sems,
):
    half = key_heads // 2
    loads = [
        pltpu.make_async_copy(src, dst, sems.at[i])
        for i, (src, dst) in enumerate(
            (
                (rates_hbm, rates_ref),
                (k_hbm, k_ref),
                (v_hbm, v_ref),
            )
        )
    ]
    for load in loads:
        load.start()
    row = lax.broadcasted_iota(jnp.int32, (CHUNK, CHUNK), 0)
    col = lax.broadcasted_iota(jnp.int32, (CHUNK, CHUNK), 1)
    upper = (row <= col).astype(F32)
    eye = (row == col).astype(F32)
    below = (row > col).astype(F32)
    apart = row ^ col
    levels = CHUNK.bit_length() - 1
    masks = [((apart >> level) == 1).astype(F32).astype(BF16) for level in range(levels)]
    second = lax.broadcasted_iota(jnp.int32, (1, CHUNK), 1) >= STRETCH
    both_eye = jnp.concatenate([eye, eye], axis=1)
    loads[0].wait()
    keeps = chunk_flags(place_ref[1] * (2 * chunks), doc_starts(place_ref), chunks)
    heads_all = rates_ref.shape[0] // 2
    loads[1].wait()

    for step in range(2):
        side = lax.rem(step + place_ref[0], 2)
        turn = lax.rem(heads_all - 2 * half * side, heads_all)

        def by_chunk(first):
            rolled = pltpu.roll(rates_ref[first : first + heads_all, :], turn, 0)
            return jnp.concatenate(
                [rolled[:, n * CHUNK : (n + 1) * CHUNK] for n in range(chunks)], axis=0
            )

        decay, beta = by_chunk(0), by_chunk(heads_all)
        cum = jnp.dot(decay, upper, precision=lax.Precision.HIGHEST, preferred_element_type=F32)
        (cum_t_ref if step == 0 else cum_m_ref)[...] = cum
        grown = jnp.exp(cum)
        cum_col, beta_col = cum.T, beta.T

        pairs = []
        for n in range(chunks):
            rows = slice(n * CHUNK, (n + 1) * CHUNK)
            k1, k2 = keeps[n]
            bias = fade_bias(row, col, k2)
            entry = jnp.where(second, k1 * k2, k1)
            leave = jnp.where(second, 1.0, k2)
            for g in range(half):
                key_cols = pl.ds(pl.multiple_of((side * half + g) * DK, DK), DK)
                k_unit = unit_rows(k_ref[rows, key_cols]).astype(BF16)
                k_turned = k_unit.astype(F32).T
                key_gram = mm(k_unit, k_turned.astype(BF16)) * below
                heads = []
                for e in range(2):
                    at = n * heads_all + 2 * g + e
                    c_row, c_col = cum[at : at + 1, :], cum_col[:, at : at + 1]
                    b_row = beta[at : at + 1, :]
                    fade = jnp.exp((c_col - c_row) + bias)
                    last = c_row[:, CHUNK - 1 : CHUNK]
                    heads.append(
                        dict(
                            noise=(key_gram * fade * beta_col[:, at : at + 1]).astype(BF16),
                            b_row=b_row,
                            be_row=b_row * grown[at : at + 1, :] * entry,
                            k_out=(k_turned * (jnp.exp(last - c_row) * leave)).astype(BF16),
                            through=jnp.exp(last) * (k1 * k2),
                        )
                    )
                pairs.append((n, g, k_unit, heads))

        inverses = [
            both_eye - jnp.concatenate([h["noise"] * masks[0] for h in heads], axis=1).astype(F32)
            for _, _, _, heads in pairs
        ]
        for level in range(1, levels):
            held = [t.astype(BF16) for t in inverses]
            part = [
                mm(t, corners(heads[0]["noise"] * masks[level], heads[1]["noise"] * masks[level])).astype(BF16)
                for t, (_, _, _, heads) in zip(held, pairs)
            ]
            inverses = [
                t - mm(p, corners(b[:, :CHUNK], b[:, CHUNK:])) for t, p, b in zip(inverses, part, held)
            ]

        if step == 0:
            loads[2].wait()
        pair_ref, held_ref = ((pair_t_ref, held_t_ref), (pair_m_ref, held_m_ref))[step]
        outs = {}
        for (n, g, k_unit, heads), t in zip(pairs, inverses):
            rows = slice(n * CHUNK, (n + 1) * CHUNK)
            values = v_ref[rows, pl.ds(pl.multiple_of((side * half + g) * 2 * DV, 2 * DV), 2 * DV)]
            b_rows = jnp.concatenate([h["b_row"] for h in heads], axis=1)
            wy_values = mm((t * b_rows).astype(BF16), corners(values[:, :DV], values[:, DV:])).astype(BF16)
            weighted = jnp.concatenate(
                [t[:, e * CHUNK : (e + 1) * CHUNK] * heads[e]["be_row"] for e in range(2)], axis=0
            )
            wy_keys = mm(weighted.astype(BF16), k_unit).astype(BF16)
            for e in range(2):
                pair = jnp.concatenate(
                    [wy_keys[e * CHUNK : (e + 1) * CHUNK], wy_values[:, e * DV : (e + 1) * DV]], axis=1
                )
                pair_ref[2 * g + e, rows, :] = pair
                outs[n, 2 * g + e] = (mm(heads[e]["k_out"], pair), heads[e]["through"])

        carried = [None] * (2 * half)
        for n in range(chunks):
            for j in range(2 * half):
                moved, through = outs[n, j]
                if n == 0:
                    carried[j] = jnp.concatenate([eye * through - moved[:, :DK], moved[:, DK:]], axis=1)
                    continue
                held = carried[j].astype(BF16)
                held_ref[j, n - 1] = held
                after = carried[j] * through - mm(moved[:, :DK].astype(BF16), held)
                carried[j] = jnp.concatenate([after[:, :DK], after[:, DK:] + moved[:, DK:]], axis=1)
        for j in range(2 * half):
            (theirs_ref if step == 0 else mine_ref)[j] = carried[j]


def state_maps(place, keys, values, rates):
    tokens, key_width = keys.shape
    key_heads = key_width // DK
    heads = rates.shape[0] // 2
    chunks = tokens // CHUNK
    part = heads // 2
    local = pl.BlockSpec(memory_space=pltpu.VMEM)
    remote = pl.BlockSpec(memory_space=pltpu.HBM)
    return pl.pallas_call(
        functools.partial(maps_kernel, chunks, key_heads),
        out_shape=[jax.ShapeDtypeStruct((part, DK, DK + DV), F32)] * 2
        + [jax.ShapeDtypeStruct((part, tokens, DK + DV), BF16)] * 2
        + [jax.ShapeDtypeStruct((part, chunks - 1, DK, DK + DV), BF16)] * 2
        + [jax.ShapeDtypeStruct((chunks * heads, CHUNK), F32)] * 2,
        in_specs=[pl.BlockSpec(memory_space=pltpu.SMEM)] + [remote] * 3,
        out_specs=[local] * 8,
        scratch_shapes=[
            pltpu.VMEM(keys.shape, keys.dtype),
            pltpu.VMEM(values.shape, values.dtype),
            pltpu.VMEM(rates.shape, rates.dtype),
            pltpu.SemaphoreType.DMA((3,)),
        ],
        compiler_params=pltpu.CompilerParams(vmem_limit_bytes=MAPS_VMEM),
        name="state_maps",
    )(place, keys, values, rates)


def read_kernel(
    step, chunks, key_heads, place_ref, q_ref, k_ref, cum_ref, pair_ref, held_ref, reach_ref, core_ref
):
    half = key_heads // 2
    side = lax.rem(step + place_ref[0], 2)
    heads_all = 4 * half
    row = lax.broadcasted_iota(jnp.int32, (CHUNK, CHUNK), 0)
    col = lax.broadcasted_iota(jnp.int32, (CHUNK, CHUNK), 1)
    second_col = lax.broadcasted_iota(jnp.int32, (CHUNK, 1), 0) >= STRETCH
    keeps = chunk_flags(place_ref[1] * (2 * chunks), doc_starts(place_ref), chunks)
    cum = cum_ref[...]
    cum_col = cum.T
    grown_col = jnp.exp(cum_col)
    for n in range(chunks):
        rows = slice(n * CHUNK, (n + 1) * CHUNK)
        k1, k2 = keeps[n]
        bias = fade_bias(row, col, k2)
        entry_col = jnp.where(second_col, k1 * k2, k1)
        for g in range(half):
            key_cols = pl.ds(pl.multiple_of((side * half + g) * DK, DK), DK)
            k_unit = unit_rows(k_ref[rows, key_cols]).astype(BF16)
            q_unit = unit_rows(q_ref[rows, key_cols]).astype(BF16)
            query_gram = mm(q_unit, k_unit.astype(F32).T.astype(BF16))
            for e in range(2):
                j = 2 * g + e
                at = n * heads_all + j
                cols = slice(j * DV, (j + 1) * DV)
                fade = jnp.exp((cum_col[:, at : at + 1] - cum[at : at + 1, :]) + bias)
                seen = mm((query_gram * fade).astype(BF16), pair_ref[j, rows, :])
                q_in = q_unit.astype(F32) * (grown_col[:, at : at + 1] * entry_col)
                q_eff = (q_in - seen[:, :DK]).astype(BF16)
                if n == 0:
                    reach_ref[rows, cols] = q_eff
                    core_ref[rows, cols] = seen[:, DK:]
                else:
                    read = mm(q_eff, held_ref[j, n - 1])
                    reach_ref[rows, cols] = read[:, :DK].astype(BF16)
                    core_ref[rows, cols] = read[:, DK:] + seen[:, DK:]


def read_out(step, place, queries, keys, cum, pair, held):
    tokens, key_width = queries.shape
    key_heads = key_width // DK
    chunks = tokens // CHUNK
    local = pl.BlockSpec(memory_space=pltpu.VMEM)
    scalar = pl.BlockSpec(memory_space=pltpu.SMEM)
    width = pair.shape[0] * DV
    return pl.pallas_call(
        functools.partial(read_kernel, step, chunks, key_heads),
        out_shape=[
            jax.ShapeDtypeStruct((tokens, width), BF16),
            jax.ShapeDtypeStruct((tokens, width), F32),
        ],
        in_specs=[scalar] + [local] * 5,
        out_specs=[local] * 2,
        compiler_params=pltpu.CompilerParams(vmem_limit_bytes=READ_VMEM),
        cost_estimate=pl.CostEstimate(flops=2 * 10**9, bytes_accessed=6 * 10**6, transcendentals=10**6),
        name="read_out",
    )(place, queries, keys, cum, pair, held)


def exact(left, right):
    return jnp.dot(left, right, precision=lax.Precision.HIGHEST, preferred_element_type=F32)


def group_kernel(core_ref, mine_ref, other_ref, map_ref, state_ref):
    def join(first_ref, second_ref):
        for j in range(first_ref.shape[0]):
            joined = exact(second_ref[j][:, :DK], first_ref[j])
            map_ref[j] = joined[:, :DK]
            state_ref[j] = joined[:, DK:] + second_ref[j][:, DK:]

    @pl.when(core_ref[2] == 0)
    def _():
        join(mine_ref, other_ref)

    @pl.when(core_ref[2] == 1)
    def _():
        join(other_ref, mine_ref)


def enter_kernel(hops, core_ref, mine_ref, other_ref, former_ref, latter_ref, keep_ref, send_ref):
    early = core_ref[5] < hops

    def through(first_ref, same_ref, out_ref):
        for j in range(first_ref.shape[0]):
            state = jnp.where(early, former_ref[j], latter_ref[j])
            same_ref[j] = state
            out_ref[j] = exact(first_ref[j][:, :DK], state) + first_ref[j][:, DK:]

    @pl.when(core_ref[2] == 0)
    def _():
        through(mine_ref, keep_ref, send_ref)

    @pl.when(core_ref[2] == 1)
    def _():
        through(other_ref, send_ref, keep_ref)


def small_call(kernel, place, *operands):
    part = operands[0].shape[0]
    local = pl.BlockSpec(memory_space=pltpu.VMEM)
    return pl.pallas_call(
        kernel,
        out_shape=[jax.ShapeDtypeStruct((part, DK, DV), F32)] * 2,
        in_specs=[pl.BlockSpec(memory_space=pltpu.SMEM)] + [local] * len(operands),
        out_specs=[local] * 2,
        compiler_params=pltpu.CompilerParams(vmem_limit_bytes=SMALL_VMEM),
    )(place, *operands)


def finish_kernel(
    offset, heads, place_ref, reach_m_ref, core_m_ref, reach_t_ref, core_t_ref, gate_ref, gain_ref, kept_ref, got_ref,
    weight_ref, send_x_ref, send_y_ref, keep_l_ref, keep_r_ref, gated_ref,
):
    size = send_x_ref.shape[1]
    share = gate_ref.shape[0] // 4
    gain = gain_ref[...]
    first = place_ref[4]
    half = heads // 2
    for i in range(4):
        rows = pl.ds(pl.multiple_of((i ^ place_ref[3]) * share + offset, 16), size)
        for side, (reach_ref, core_ref, state_ref) in enumerate(
            ((reach_m_ref, core_m_ref, kept_ref), (reach_t_ref, core_t_ref, got_ref))
        ):
            for j in range(half):
                head = first + j if side == 0 else half - first + j
                cols = pl.ds(pl.multiple_of(head * DV, DV), DV)
                own = slice(j * DV, (j + 1) * DV)
                core = core_ref[rows, own] + mm(reach_ref[rows, own], state_ref[j].astype(BF16))
                gate = gate_ref[rows, cols].astype(F32)
                normed = core * lax.rsqrt(jnp.mean(core * core, axis=-1, keepdims=True) + 1e-6)
                gated = normed * gain * (gate / (1.0 + jnp.exp(-gate)))
                gated_ref[i * size : (i + 1) * size, cols] = gated.astype(BF16)
    width = weight_ref.shape[1] // 2
    left = mm(gated_ref[...], weight_ref[:, :width])
    right = mm(gated_ref[...], weight_ref[:, width:])
    for i, (l_ref, l_at, r_ref, r_at) in enumerate(
        (
            (keep_l_ref, 0, keep_r_ref, 0),
            (send_x_ref, 0, keep_r_ref, 1),
            (keep_l_ref, 1, send_y_ref, 0),
            (send_x_ref, 1, send_y_ref, 1),
        )
    ):
        l_ref[l_at] = left[i * size : (i + 1) * size]
        r_ref[r_at] = right[i * size : (i + 1) * size]


def finish(offset, size, place, reads, gate, gain, kept, got, weight):
    depth = gate.shape[1]
    width = weight.shape[1] // 2
    heads = depth // DV
    local = pl.BlockSpec(memory_space=pltpu.VMEM)
    return pl.pallas_call(
        functools.partial(finish_kernel, offset, heads),
        out_shape=[jax.ShapeDtypeStruct((2, size, width), F32)] * 4,
        in_specs=[pl.BlockSpec(memory_space=pltpu.SMEM)] + [local] * 9,
        out_specs=[local] * 4,
        scratch_shapes=[pltpu.VMEM((4 * size, depth), BF16)],
        compiler_params=pltpu.CompilerParams(vmem_limit_bytes=FINISH_VMEM),
        cost_estimate=pl.CostEstimate(
            flops=8 * size * depth * width * 2, bytes_accessed=16 * size * width, transcendentals=4 * size * depth
        ),
        name="finish",
    )(place, *reads, gate, gain.reshape(1, DV), kept, got, weight)


def precise(left, right):
    return jnp.einsum("hij,hjk->hik", left, right, precision=lax.Precision.HIGHEST)


def combine(earlier, later):
    joined = precise(later[..., :DK], earlier)
    return jnp.concatenate([joined[..., :DK], joined[..., DK:] + later[..., DK:]], axis=-1)


def apply_map(pair, state):
    return precise(pair[..., :DK], state) + pair[..., DK:]


def group_hops(pair_map, pair_state, outer, beside=()):
    results, arrivals = [], []
    leaving = pair_state
    for hop in range(outer // 2):
        step = [(i, i + 1) for i in range(hop, outer - 1)] + [(outer - 1, hop)]
        state = lax.ppermute(leaving, "outer", step)
        if hop < len(beside):
            call, place, rest = beside[hop]
            place, _ = lax.optimization_barrier((place, leaving))
            result = call(place, *rest)
            state, result = lax.optimization_barrier((state, result))
            results.append(result)
        arrivals.append(state)
        if hop < outer // 2 - 1:
            if hop:
                state = jnp.where(lax.axis_index("outer") <= hop, arrivals[-2], state)
                arrivals[-1] = state
            leaving = precise(pair_map, state) + pair_state
    return arrivals[-2], arrivals[-1], results


def whole_prefix(mine, theirs, ctx, outer):
    here = lax.axis_index("ctx")
    both = jnp.concatenate([mine, theirs], axis=0)
    blocks = lax.all_gather(both, "ctx")
    identity = jnp.concatenate([jnp.eye(DK, dtype=F32), jnp.zeros((DK, DV), F32)], axis=1)
    start = jnp.broadcast_to(identity, both.shape)

    def hop(k, carry):
        before, through = carry
        through = combine(through, blocks[k])
        return jnp.where(k < here, through, before), through

    before, through = lax.fori_loop(0, ctx, hop, (start, start))
    former, latter, _ = group_hops(through[..., :DK], through[..., DK:], outer)
    entering = jnp.where(lax.axis_index("outer") < outer // 2, former, latter)
    state = apply_map(before, entering)
    half = mine.shape[0]
    return state[:half], state[half:]


def shards(ctx, outer, queries, keys, values, gate, decay, beta, docs, gain, weight):
    heads = decay.shape[0]
    here = lax.axis_index("ctx")
    position = lax.axis_index("outer") * ctx + here
    second = here if ctx == 2 else 0 * here
    group = lax.axis_index("outer")
    place = jnp.stack([1 - second, position, here, lax.axis_index("tp"), second * (heads // 2), group])
    place = jnp.concatenate([place.astype(jnp.int32), docs])
    rates = jnp.concatenate([decay, beta], axis=0)
    theirs, mine, pair_t, pair_m, held_t, held_m, cum_t, cum_m = state_maps(place, keys, values, rates)
    if ctx == 2:
        swap = [(0, 1), (1, 0)]
        other = lax.ppermute(theirs, "ctx", swap)
        group_map, group_state = small_call(group_kernel, place, mine, other)
        beside = (
            (functools.partial(read_out, 1), place, (queries, keys, cum_m, pair_m, held_m)),
            (functools.partial(read_out, 0), place, (queries, keys, cum_t, pair_t, held_t)),
        )
        former, latter, reads = group_hops(group_map, group_state, outer, beside)
        kept, sent = small_call(functools.partial(enter_kernel, outer // 2), place, mine, other, former, latter)
        got = lax.ppermute(sent, "ctx", swap)
    else:
        kept, got = whole_prefix(mine, theirs, ctx, outer)
        reads = [
            read_out(1, place, queries, keys, cum_m, pair_m, held_m),
            read_out(0, place, queries, keys, cum_t, pair_t, held_t),
        ]
    reads = [array for pair in reads for array in pair]
    along_x = [(i, i ^ 1) for i in range(4)]
    along_y = [(i, i ^ 2) for i in range(4)]
    halves, offset = [], 0
    for size in PARTS:
        send_x, send_y, keep_l, keep_r = finish(offset, size, place, reads, gate, gain, kept, got, weight)
        offset += size
        got_x = lax.ppermute(send_x, "tp", along_x)
        got_y = lax.ppermute(send_y, "tp", along_y)
        halves.append((keep_l, keep_r, got_x, got_y))
    outs = []
    for keep_l, keep_r, got_x, got_y in halves:
        last_l = lax.ppermute(keep_l[1] + got_x[1], "tp", along_y)
        last_r = lax.ppermute(keep_r[1] + got_y[1], "tp", along_x)
        out_l = keep_l[0] + got_x[0] + last_l
        out_r = keep_r[0] + got_y[0] + last_r
        outs.append(jnp.concatenate([out_l, out_r], axis=1).astype(BF16))
    return jnp.concatenate(outs, axis=0)


def solution(mesh):
    ctx, outer = mesh.shape["ctx"], mesh.shape["outer"]
    in_specs = (
        P(("outer", "ctx"), "tp"),
        P(("outer", "ctx"), "tp"),
        P(("outer", "ctx"), "tp"),
        P(("outer", "ctx"), "tp"),
        P("tp", ("outer", "ctx")),
        P("tp", ("outer", "ctx")),
        P(),
        P(),
        P("tp", None),
    )
    out_specs = P(("outer", "ctx", "tp"), None)
    return jax.shard_map(
        functools.partial(shards, ctx, outer), mesh=mesh, in_specs=in_specs, out_specs=out_specs, check_vma=False
    )
```

time: 106 us -> 78.6 us (0.74); the launches traced: 104 us -> 78.2 us
  waiting for transfers between devices: 49.4 us -> 30.9 us
  Pallas kernels: 33.8 us -> 24.1 us
  starting transfers between devices: 11.1 us -> 17.9 us
  other arithmetic: 6.68 us -> 1.9 us
  local copies, waits for them, and re-layouts: 0.69 us -> 2.84 us
  matrix products: 2.11 us -> 0.4 us
    ppermute x1 -> x3, waiting for transfers between devices: 23.4 us -> 11.5 us  [shards(): got_x = lax.ppermute(send_x, 'tp', along_x)]
    pallas_call x2 -> x8, Pallas kernels: 33.8 us -> 24.1 us  [the longest x1 10.5 us: state_maps(): pl.pallas_call(functools.partial(maps_kernel, chunks, key_heads), out_sha...]
    ppermute x4, waiting for transfers between devices: 15.7 us -> 10.5 us  [the longest x2 7.08 us: group_hops(): state = lax.ppermute(leaving, 'outer', step)]
    another operation x4 -> x6, other arithmetic: 2.49 us -> 0.2 us
    ppermute x1 -> x3, starting transfers between devices: 1.49 us -> 3.71 us  [shards(): got_x = lax.ppermute(send_x, 'tp', along_x)]
    ppermute x1 -> x3, starting transfers between devices: 0.57 us -> 2.73 us  [shards(): last_l = lax.ppermute(keep_l[1] + got_x[1], 'tp', along_y)]
    ppermute x1 -> x3, starting transfers between devices: 0.51 us -> 2.53 us  [shards(): got_y = lax.ppermute(send_y, 'tp', along_y)]
    ppermute x1 -> x3, starting transfers between devices: 1.55 us -> 3.51 us  [shards(): last_r = lax.ppermute(keep_r[1] + got_y[1], 'tp', along_x)]
  transfers between devices with their start and end apart: 8 -> 16, of which waited for: 7 -> 9; matrix products, arithmetic and copies ran while one was open for 4% -> 0% of each run, Pallas kernels for 0% -> 12%
where the time goes in v2:
time: 78.6 us; the launch traced here: 78.2 us
  waiting for transfers between devices  30.9 us (39%)
  Pallas kernels  24.1 us (31%)
  starting transfers between devices  17.9 us (23%)
  local copies, waits for them, and re-layouts  2.84 us (4%)
  other arithmetic  1.9 us (2%)
    ppermute x3, waiting for transfers between devices, shards(): got_x = lax.ppermute(send_x, 'tp', along_x)  11.5 us
    pallas_call x1, Pallas kernels, state_maps(): pl.pallas_call(functools.partial(maps_kernel, chunks, key_heads), out_sha...  10.5 us
    ppermute x3, waiting for transfers between devices, shards(): last_l = lax.ppermute(keep_l[1] + got_x[1], 'tp', along_y)  8.8 us
    ppermute x2, waiting for transfers between devices, group_hops(): state = lax.ppermute(leaving, 'outer', step)  7.08 us
    pallas_call x3, Pallas kernels, finish(): pl.pallas_call(functools.partial(finish_kernel, offset, heads), out_shape...  6.25 us
    ppermute x2, starting transfers between devices, group_hops(): state = lax.ppermute(leaving, 'outer', step)  5.3 us
    pallas_call x2, Pallas kernels, read_out(): pl.pallas_call(functools.partial(read_kernel, step, chunks, key_heads), o...  5.23 us
    ppermute x3, starting transfers between devices, shards(): got_x = lax.ppermute(send_x, 'tp', along_x)  3.71 us
  transfers between devices with their start and end apart: 16, of which 9 were waited for; matrix products, arithmetic and copies ran while one was open for 0% of the time, Pallas kernels for 12%

profile of v2, /device:TPU:12, one launch (start us, length us, event | category | flops | bytes accessed | tf_op | source)
XLA Modules:
  0.0 78.2 jit_solution(6383578623339278218)
XLA Ops:
  0.0 0.7 pad_maximum_fusion.rates_hbm
  0.7 0.7 concatenate.21.place_ref.core_ref
  1.5 1.0 %copy-done.2 = bf16[512,512]{1,0:T(8,128)(2,1)S(1)} copy-done((bf16[512,512]{1,0:T(8,128)(2,1)S(1)}, bf16[512,512]{1,0:T(8,128)(2,1)}, u32[]{:S(2)}) %copy-start.2) | copy-done | bytes 524312
  2.5 10.5 %state_maps.1 = (f32[4,128,256]{2,1,0:T(8,128)S(1)}, f32[4,128,256]{2,1,0:T(8,128)S(1)}, bf16[4,512,256]{2,1,0:T(8,128)(2,1)S(1)}, bf16[4,512,256]{2,1,0:T(8,128...) custom-call(s32[14]{0:T(128)S(1)} %concatenate.21.place_ref.core_ref, ...), custom_call_target="tpu_custom_call" | custom-call | tf_op jit(solution)/shard_map/state_maps/pallas_call | solution.py:201
  13.1 1.9 %collective-permute-done.other_ref = f32[4,128,256]{2,1,0:T(8,128)S(1)} collective-permute-done((f32[4,128,256]{2,1,0:T(8,128)S(1)}, f32[4,128,256]{2,1,0:T(8,128)S(1)}, u32[]{:S(2)}, u32[]{:S(2)}) %collective-permute-start) | collective-permute-done | bytes 524320 | tf_op jit(solution)/shard_map/ppermute | solution.py:454
  15.0 1.1 %shard_map.91 = (f32[4,128,128]{2,1,0:T(8,128)S(1)}, f32[4,128,128]{2,1,0:T(8,128)S(1)}) custom-call(s32[14]{0:T(128)S(1)} %concatenate.21.place_ref.core_ref, f32[4,128,256]{2,1,0:T(8,128)S(1)} %get-tuple-element.41.mine_ref, f32[4,128,256]{2,1,0:T(8,128)S(1)} %collective-permute-done.other_ref), custom_call_target="tpu_custom_call" | custom-call | tf_op jit(solution)/shard_map/pallas_call | solution.py:322
  16.2 1.6 %collective-permute-start.1 = (f32[4,128,128]{2,1,0:T(8,128)S(1)}, f32[4,128,128]{2,1,0:T(8,128)S(1)}, u32[]{:S(2)}, u32[]{:S(2)}) collective-permute-start(f32[4,128,128]{2,1,0:T(8,128)S(1)} %get-tuple-element.43), channel_id=1, source_target_pairs={{0,1},{1,2},{2,3},{3,0},{4,5},{5,6},{6,7},{7,4},{8,9},{9,10},{10,1... | collective-permute-start | bytes 786440 | tf_op jit(solution)/shard_map/ppermute | solution.py:406
  17.8 1.0 %copy-done.4 = bf16[512,512]{1,0:T(8,128)(2,1)S(1)} copy-done((bf16[512,512]{1,0:T(8,128)(2,1)S(1)}, bf16[512,512]{1,0:T(8,128)(2,1)}, u32[]{:S(2)}) %copy-start.4) | copy-done | bytes 524312
  18.8 2.6 %read_out.2 = (bf16[512,512]{1,0:T(8,128)(2,1)S(1)}, f32[512,512]{1,0:T(8,128)S(1)}) custom-call(s32[14]{0:T(128)S(1)} %concatenate.21.place_ref.core_ref, bf16[512,512]{1,0:T(8,128)(2,1)S(1)} %copy-done.4, bf16[512,512]{1,0:T(8,128)(2,1)S(1)} %copy-done.2, f32[32,128]{1,0:T(8,128)S(1)} %get-tuple-element.45.cum_ref, ...), custom_call_target="tpu_custom_call" | custom-call | flops 2000000000 | bytes 6000000 | tf_op jit(solution)/shard_map/read_out/pallas_call | solution.py:267
  21.5 3.1 %collective-permute-done.1.former_ref = f32[4,128,128]{2,1,0:T(8,128)S(1)} collective-permute-done((f32[4,128,128]{2,1,0:T(8,128)S(1)}, f32[4,128,128]{2,1,0:T(8,128)S(1)}, u32[]{:S(2)}, u32[]{:S(2)}) %collective-permute-start.1) | collective-permute-done | bytes 262176 | tf_op jit(solution)/shard_map/ppermute | solution.py:406
  25.0 3.7 %collective-permute-start.2 = (f32[4,128,128]{2,1,0:T(8,128)S(1)}, f32[4,128,128]{2,1,0:T(8,128)S(1)}, u32[]{:S(2)}, u32[]{:S(2)}) collective-permute-start(f32[4,128,128]{2,1,0:T(8,128)S(1)} %convolution_add_fusion), channel_id=1, source_target_pairs={{1,2},{2,3},{3,1},{5,6},{6,7},{7,5},{9,10},{10,11},{11,9},{13,14},... | collective-permute-start | bytes 786440 | tf_op jit(solution)/shard_map/ppermute | solution.py:406
  28.7 2.6 %read_out.3 = (bf16[512,512]{1,0:T(8,128)(2,1)S(1)}, f32[512,512]{1,0:T(8,128)S(1)}) custom-call(s32[14]{0:T(128)S(1)} %concatenate.21.place_ref.core_ref, bf16[512,512]{1,0:T(8,128)(2,1)S(1)} %copy-done.4, bf16[512,512]{1,0:T(8,128)(2,1)S(1)} %copy-done.2, f32[32,128]{1,0:T(8,128)S(1)} %get-tuple-element.55.cum_ref, ...), custom_call_target="tpu_custom_call" | custom-call | flops 2000000000 | bytes 6000000 | tf_op jit(solution)/shard_map/read_out/pallas_call | solution.py:267
  31.3 4.0 %collective-permute-done.2.latter_ref = f32[4,128,128]{2,1,0:T(8,128)S(1)} collective-permute-done((f32[4,128,128]{2,1,0:T(8,128)S(1)}, f32[4,128,128]{2,1,0:T(8,128)S(1)}, u32[]{:S(2)}, u32[]{:S(2)}) %collective-permute-start.2) | collective-permute-done | bytes 262176 | tf_op jit(solution)/shard_map/ppermute | solution.py:406
  35.3 0.9 %shard_map.92 = (f32[4,128,128]{2,1,0:T(8,128)S(1)}, f32[4,128,128]{2,1,0:T(8,128)S(1)}) custom-call(s32[14]{0:T(128)S(1)} %concatenate.21.place_ref.core_ref, f32[4,128,256]{2,1,0:T(8,128)S(1)} %get-tuple-element.41.mine_ref, f32[4,128,256]{2,1,0:T(8,128)S(1)} %collective-permute-done.other_ref, f32[4,128,128]{2,1,0:T(8,128)S(1)} %collective-permute-done.1.former_ref, ...), custom_call_target="tpu_custom_call" | custom-call | tf_op jit(solution)/shard_map/pallas_call | solution.py:322
  36.3 1.5 %collective-permute-done.3.got_ref = f32[4,128,128]{2,1,0:T(8,128)S(1)} collective-permute-done((f32[4,128,128]{2,1,0:T(8,128)S(1)}, f32[4,128,128]{2,1,0:T(8,128)S(1)}, u32[]{:S(2)}, u32[]{:S(2)}) %collective-permute-start.3) | collective-permute-done | bytes 262176 | tf_op jit(solution)/shard_map/ppermute | solution.py:462
  37.8 1.7 %finish.3 = (f32[2,32,1024]{2,1,0:T(8,128)S(1)}, f32[2,32,1024]{2,1,0:T(8,128)S(1)}, f32[2,32,1024]{2,1,0:T(8,128)S(1)}, f32[2,32,1024]{2,1,0:T(8,128)S(1)}) custom-call(s32[14]{0:T(128)S(1)} %concatenate.21.place_ref.core_ref, bf16[512,512]{1,0:T(8,128)(2,1)S(1)} %get-tuple-element.50.reach_m_ref, f32[512,512]{1,0:T(8,128)S(1)} %get-tuple-element.51.core_m_ref, ...), custom_call_target="tpu_custom_call" | custom-call | flops 536870912 | bytes 524288 | tf_op jit(solution)/shard_map/finish/pallas_call | solution.py:374
  39.6 1.6 %collective-permute-start.4 = (f32[2,32,1024]{2,1,0:T(8,128)S(1)}, f32[2,32,1024]{2,1,0:T(8,128)S(1)}, u32[]{:S(2)}, u32[]{:S(2)}) collective-permute-start(f32[2,32,1024]{2,1,0:T(8,128)S(1)} %get-tuple-element.66), channel_id=1, source_target_pairs={{0,8},{8,0},{16,24},{24,16},{1,9},{9,1},{17,25},{25,17},{2,10},{10... | collective-permute-start | bytes 786440 | tf_op jit(solution)/shard_map/ppermute | solution.py:476
  41.6 2.2 %finish.4 = (f32[2,48,1024]{2,1,0:T(8,128)S(1)}, f32[2,48,1024]{2,1,0:T(8,128)S(1)}, f32[2,48,1024]{2,1,0:T(8,128)S(1)}, f32[2,48,1024]{2,1,0:T(8,128)S(1)}) custom-call(s32[14]{0:T(128)S(1)} %concatenate.21.place_ref.core_ref, bf16[512,512]{1,0:T(8,128)(2,1)S(1)} %get-tuple-element.50.reach_m_ref, f32[512,512]{1,0:T(8,128)S(1)} %get-tuple-element.51.core_m_ref, ...), custom_call_target="tpu_custom_call" | custom-call | flops 805306368 | bytes 786432 | tf_op jit(solution)/shard_map/finish/pallas_call | solution.py:374
  43.9 0.6 collective-permute-start.8
  44.5 1.5 %collective-permute-start.10 = (f32[2,48,1024]{2,1,0:T(8,128)S(1)}, f32[2,48,1024]{2,1,0:T(8,128)S(1)}, u32[]{:S(2)}, u32[]{:S(2)}) collective-permute-start(f32[2,48,1024]{2,1,0:T(8,128)S(1)} %get-tuple-element.72), channel_id=1, source_target_pairs={{0,16},{8,24},{16,0},{24,8},{1,17},{9,25},{17,1},{25,9},{2,18},{10... | collective-permute-start | bytes 1179656 | tf_op jit(solution)/shard_map/ppermute | solution.py:477
  46.0 2.2 %finish.5 = (f32[2,48,1024]{2,1,0:T(8,128)S(1)}, f32[2,48,1024]{2,1,0:T(8,128)S(1)}, f32[2,48,1024]{2,1,0:T(8,128)S(1)}, f32[2,48,1024]{2,1,0:T(8,128)S(1)}) custom-call(s32[14]{0:T(128)S(1)} %concatenate.21.place_ref.core_ref, bf16[512,512]{1,0:T(8,128)(2,1)S(1)} %get-tuple-element.50.reach_m_ref, f32[512,512]{1,0:T(8,128)S(1)} %get-tuple-element.51.core_m_ref, ...), custom_call_target="tpu_custom_call" | custom-call | flops 805306368 | bytes 786432 | tf_op jit(solution)/shard_map/finish/pallas_call | solution.py:374
  48.3 1.6 %collective-permute-start.12 = (f32[2,48,1024]{2,1,0:T(8,128)S(1)}, f32[2,48,1024]{2,1,0:T(8,128)S(1)}, u32[]{:S(2)}, u32[]{:S(2)}) collective-permute-start(f32[2,48,1024]{2,1,0:T(8,128)S(1)} %get-tuple-element.74), channel_id=1, source_target_pairs={{0,8},{8,0},{16,24},{24,16},{1,9},{9,1},{17,25},{25,17},{2,10},{10... | collective-permute-start | bytes 1179656 | tf_op jit(solution)/shard_map/ppermute | solution.py:476
  50.4 1.6 %collective-permute-start.5 = (f32[32,1024]{1,0:T(8,128)S(1)}, f32[32,1024]{1,0:T(8,128)S(1)}, u32[]{:S(2)}, u32[]{:S(2)}) collective-permute-start(f32[32,1024]{1,0:T(8,128)S(1)} %fusion.20), channel_id=1, source_target_pairs={{0,16},{8,24},{16,0},{24,8},{1,17},{9,25},{17,1},{25,9},{2,18},{10... | collective-permute-start | bytes 393224 | tf_op jit(solution)/shard_map/ppermute | solution.py:481
  52.0 5.2 %collective-permute-done.8 = f32[2,48,1024]{2,1,0:T(8,128)S(1)} collective-permute-done((f32[2,48,1024]{2,1,0:T(8,128)S(1)}, f32[2,48,1024]{2,1,0:T(8,128)S(1)}, u32[]{:S(2)}, u32[]{:S(2)}) %collective-permute-start.8) | collective-permute-done | bytes 393248 | tf_op jit(solution)/shard_map/ppermute | solution.py:476
  57.2 1.5 %collective-permute-start.7 = (f32[32,1024]{1,0:T(8,128)S(1)}, f32[32,1024]{1,0:T(8,128)S(1)}, u32[]{:S(2)}, u32[]{:S(2)}) collective-permute-start(f32[32,1024]{1,0:T(8,128)S(1)} %fusion.16), channel_id=1, source_target_pairs={{0,8},{8,0},{16,24},{24,16},{1,9},{9,1},{17,25},{25,17},{2,10},{10... | collective-permute-start | bytes 393224 | tf_op jit(solution)/shard_map/ppermute | solution.py:482
  59.4 6.3 %collective-permute-done.12 = f32[2,48,1024]{2,1,0:T(8,128)S(1)} collective-permute-done((f32[2,48,1024]{2,1,0:T(8,128)S(1)}, f32[2,48,1024]{2,1,0:T(8,128)S(1)}, u32[]{:S(2)}, u32[]{:S(2)}) %collective-permute-start.12) | collective-permute-done | bytes 393248 | tf_op jit(solution)/shard_map/ppermute | solution.py:476
  65.7 1.5 %collective-permute-start.11 = (f32[48,1024]{1,0:T(8,128)S(1)}, f32[48,1024]{1,0:T(8,128)S(1)}, u32[]{:S(2)}, u32[]{:S(2)}) collective-permute-start(f32[48,1024]{1,0:T(8,128)S(1)} %fusion.8), channel_id=1, source_target_pairs={{0,8},{8,0},{16,24},{24,16},{1,9},{9,1},{17,25},{25,17},{2,10},{10... | collective-permute-start | bytes 589832 | tf_op jit(solution)/shard_map/ppermute | solution.py:482
  67.2 0.6 collective-permute-start.13
  67.8 2.2 %collective-permute-done.5 = f32[32,1024]{1,0:T(8,128)S(1)} collective-permute-done((f32[32,1024]{1,0:T(8,128)S(1)}, f32[32,1024]{1,0:T(8,128)S(1)}, u32[]{:S(2)}, u32[]{:S(2)}) %collective-permute-start.5) | collective-permute-done | bytes 131104 | tf_op jit(solution)/shard_map/ppermute | solution.py:481
  70.6 3.6 %collective-permute-done.9 = f32[48,1024]{1,0:T(8,128)S(1)} collective-permute-done((f32[48,1024]{1,0:T(8,128)S(1)}, f32[48,1024]{1,0:T(8,128)S(1)}, u32[]{:S(2)}, u32[]{:S(2)}) %collective-permute-start.9) | collective-permute-done | bytes 196640 | tf_op jit(solution)/shard_map/ppermute | solution.py:481
  74.3 3.0 %collective-permute-done.13 = f32[48,1024]{1,0:T(8,128)S(1)} collective-permute-done((f32[48,1024]{1,0:T(8,128)S(1)}, f32[48,1024]{1,0:T(8,128)S(1)}, u32[]{:S(2)}, u32[]{:S(2)}) %collective-permute-start.13) | collective-permute-done | bytes 196640 | tf_op jit(solution)/shard_map/ppermute | solution.py:481
  77.4 0.8 %maximum_maximum_fusion = bf16[128,2048]{1,0:T(8,128)(2,1)} fusion(bf16[48,1024]{1,0:T(8,128)(2,1)S(1)} %fusion.3, bf16[48,1024]{1,0:T(8,128)(2,1)S(1)} %fusion.7, bf16[48,1024]{1,0:T(8,128)(2,1)S(1)} %fusion.11, bf16[48,1024]{1,0:T(8,128)(2,1)S(1)} %fusion.15, bf16[32,1024]{1,0:T(8,128)(2,1)S(1)} %fusion.19, bf16[32,1024]{1,0:T(8,128)(2,1)S(1)} %fusion.23), kind=kLoop, calls=%fused_computation.1 | loop fusion | flops 3145728 | bytes 1048576 | tf_op jit(solution)/shard_map/concatenate | solution.py:486
  (34 shorter events, 3.1 us)
Async XLA Ops:
  1.5 1.0 %copy-start.2 = (bf16[512,512]{1,0:T(8,128)(2,1)S(1)}, bf16[512,512]{1,0:T(8,128)(2,1)}, u32[]{:S(2)}) copy-start(bf16[512,512]{1,0:T(8,128)(2,1)} %k_ref.3) | copy-start | bytes 1572868
  13.0 2.0 %collective-permute-start = (f32[4,128,256]{2,1,0:T(8,128)S(1)}, f32[4,128,256]{2,1,0:T(8,128)S(1)}, u32[]{:S(2)}, u32[]{:S(2)}) collective-permute-start(f32[4,128,256]{2,1,0:T(8,128)S(1)} %get-tuple-element.42), channel_id=1, source_target_pairs={{0,4},{4,0},{1,5},{5,1},{2,6},{6,2},{3,7},{7,3},{8,12},{12,8},{9,1... | collective-permute-start | bytes 1572872 | tf_op jit(solution)/shard_map/ppermute | solution.py:454
  16.2 8.4 %collective-permute-start.1 = (f32[4,128,128]{2,1,0:T(8,128)S(1)}, f32[4,128,128]{2,1,0:T(8,128)S(1)}, u32[]{:S(2)}, u32[]{:S(2)}) collective-permute-start(f32[4,128,128]{2,1,0:T(8,128)S(1)} %get-tuple-element.43), channel_id=1, source_target_pairs={{0,1},{1,2},{2,3},{3,0},{4,5},{5,6},{6,7},{7,4},{8,9},{9,10},{10,1... | collective-permute-start | bytes 786440 | tf_op jit(solution)/shard_map/ppermute | solution.py:406
  17.8 1.0 %copy-start.4 = (bf16[512,512]{1,0:T(8,128)(2,1)S(1)}, bf16[512,512]{1,0:T(8,128)(2,1)}, u32[]{:S(2)}) copy-start(bf16[512,512]{1,0:T(8,128)(2,1)} %q_ref.3) | copy-start | bytes 1572868
  25.0 10.3 %collective-permute-start.2 = (f32[4,128,128]{2,1,0:T(8,128)S(1)}, f32[4,128,128]{2,1,0:T(8,128)S(1)}, u32[]{:S(2)}, u32[]{:S(2)}) collective-permute-start(f32[4,128,128]{2,1,0:T(8,128)S(1)} %convolution_add_fusion), channel_id=1, source_target_pairs={{1,2},{2,3},{3,1},{5,6},{6,7},{7,5},{9,10},{10,11},{11,9},{13,14},... | collective-permute-start | bytes 786440 | tf_op jit(solution)/shard_map/ppermute | solution.py:406
  28.6 9.2 %copy-start = (bf16[1024,2048]{1,0:T(8,128)(2,1)S(1)}, bf16[1024,2048]{1,0:T(8,128)(2,1)}, u32[]{:S(2)}) copy-start(bf16[1024,2048]{1,0:T(8,128)(2,1)} %weight_ref.5) | copy-start | bytes 12582916
  28.6 9.2 %copy-start.1 = (bf16[512,1024]{1,0:T(8,128)(2,1)S(1)}, bf16[512,1024]{1,0:T(8,128)(2,1)}, u32[]{:S(2)}) copy-start(bf16[512,1024]{1,0:T(8,128)(2,1)} %gate_ref.5) | copy-start | bytes 3145732
  28.7 9.2 %copy-start.3 = (f32[128]{0:T(128)S(1)}, f32[128]{0:T(128)}, u32[]{:S(2)}) copy-start(f32[128]{0:T(128)} %param.16) | copy-start | bytes 1540
  36.2 1.6 %collective-permute-start.3 = (f32[4,128,128]{2,1,0:T(8,128)S(1)}, f32[4,128,128]{2,1,0:T(8,128)S(1)}, u32[]{:S(2)}, u32[]{:S(2)}) collective-permute-start(f32[4,128,128]{2,1,0:T(8,128)S(1)} %get-tuple-element.64), channel_id=1, source_target_pairs={{0,4},{4,0},{1,5},{5,1},{2,6},{6,2},{3,7},{7,3},{8,12},{12,8},{9,1... | collective-permute-start | bytes 786440 | tf_op jit(solution)/shard_map/ppermute | solution.py:462
  39.6 10.3 %collective-permute-start.4 = (f32[2,32,1024]{2,1,0:T(8,128)S(1)}, f32[2,32,1024]{2,1,0:T(8,128)S(1)}, u32[]{:S(2)}, u32[]{:S(2)}) collective-permute-start(f32[2,32,1024]{2,1,0:T(8,128)S(1)} %get-tuple-element.66), channel_id=1, source_target_pairs={{0,8},{8,0},{16,24},{24,16},{1,9},{9,1},{17,25},{25,17},{2,10},{10... | collective-permute-start | bytes 786440 | tf_op jit(solution)/shard_map/ppermute | solution.py:476
  41.1 9.2 %collective-permute-start.6 = (f32[2,32,1024]{2,1,0:T(8,128)S(1)}, f32[2,32,1024]{2,1,0:T(8,128)S(1)}, u32[]{:S(2)}, u32[]{:S(2)}) collective-permute-start(f32[2,32,1024]{2,1,0:T(8,128)S(1)} %get-tuple-element.68), channel_id=1, source_target_pairs={{0,16},{8,24},{16,0},{24,8},{1,17},{9,25},{17,1},{25,9},{2,18},{10... | collective-permute-start | bytes 786440 | tf_op jit(solution)/shard_map/ppermute | solution.py:477
  43.9 13.3 %collective-permute-start.8 = (f32[2,48,1024]{2,1,0:T(8,128)S(1)}, f32[2,48,1024]{2,1,0:T(8,128)S(1)}, u32[]{:S(2)}, u32[]{:S(2)}) collective-permute-start(f32[2,48,1024]{2,1,0:T(8,128)S(1)} %get-tuple-element.70), channel_id=1, source_target_pairs={{0,8},{8,0},{16,24},{24,16},{1,9},{9,1},{17,25},{25,17},{2,10},{10... | collective-permute-start | bytes 1179656 | tf_op jit(solution)/shard_map/ppermute | solution.py:476
  44.5 14.3 %collective-permute-start.10 = (f32[2,48,1024]{2,1,0:T(8,128)S(1)}, f32[2,48,1024]{2,1,0:T(8,128)S(1)}, u32[]{:S(2)}, u32[]{:S(2)}) collective-permute-start(f32[2,48,1024]{2,1,0:T(8,128)S(1)} %get-tuple-element.72), channel_id=1, source_target_pairs={{0,16},{8,24},{16,0},{24,8},{1,17},{9,25},{17,1},{25,9},{2,18},{10... | collective-permute-start | bytes 1179656 | tf_op jit(solution)/shard_map/ppermute | solution.py:477
  48.3 17.4 %collective-permute-start.12 = (f32[2,48,1024]{2,1,0:T(8,128)S(1)}, f32[2,48,1024]{2,1,0:T(8,128)S(1)}, u32[]{:S(2)}, u32[]{:S(2)}) collective-permute-start(f32[2,48,1024]{2,1,0:T(8,128)S(1)} %get-tuple-element.74), channel_id=1, source_target_pairs={{0,8},{8,0},{16,24},{24,16},{1,9},{9,1},{17,25},{25,17},{2,10},{10... | collective-permute-start | bytes 1179656 | tf_op jit(solution)/shard_map/ppermute | solution.py:476
  49.8 17.3 %collective-permute-start.14 = (f32[2,48,1024]{2,1,0:T(8,128)S(1)}, f32[2,48,1024]{2,1,0:T(8,128)S(1)}, u32[]{:S(2)}, u32[]{:S(2)}) collective-permute-start(f32[2,48,1024]{2,1,0:T(8,128)S(1)} %get-tuple-element.76), channel_id=1, source_target_pairs={{0,16},{8,24},{16,0},{24,8},{1,17},{9,25},{17,1},{25,9},{2,18},{10... | collective-permute-start | bytes 1179656 | tf_op jit(solution)/shard_map/ppermute | solution.py:477
  50.4 19.6 %collective-permute-start.5 = (f32[32,1024]{1,0:T(8,128)S(1)}, f32[32,1024]{1,0:T(8,128)S(1)}, u32[]{:S(2)}, u32[]{:S(2)}) collective-permute-start(f32[32,1024]{1,0:T(8,128)S(1)} %fusion.20), channel_id=1, source_target_pairs={{0,16},{8,24},{16,0},{24,8},{1,17},{9,25},{17,1},{25,9},{2,18},{10... | collective-permute-start | bytes 393224 | tf_op jit(solution)/shard_map/ppermute | solution.py:481
  57.2 13.3 %collective-permute-start.7 = (f32[32,1024]{1,0:T(8,128)S(1)}, f32[32,1024]{1,0:T(8,128)S(1)}, u32[]{:S(2)}, u32[]{:S(2)}) collective-permute-start(f32[32,1024]{1,0:T(8,128)S(1)} %fusion.16), channel_id=1, source_target_pairs={{0,8},{8,0},{16,24},{24,16},{1,9},{9,1},{17,25},{25,17},{2,10},{10... | collective-permute-start | bytes 393224 | tf_op jit(solution)/shard_map/ppermute | solution.py:482
  58.8 15.4 %collective-permute-start.9 = (f32[48,1024]{1,0:T(8,128)S(1)}, f32[48,1024]{1,0:T(8,128)S(1)}, u32[]{:S(2)}, u32[]{:S(2)}) collective-permute-start(f32[48,1024]{1,0:T(8,128)S(1)} %fusion.12), channel_id=1, source_target_pairs={{0,16},{8,24},{16,0},{24,8},{1,17},{9,25},{17,1},{25,9},{2,18},{10... | collective-permute-start | bytes 589832 | tf_op jit(solution)/shard_map/ppermute | solution.py:481
  65.7 8.6 %collective-permute-start.11 = (f32[48,1024]{1,0:T(8,128)S(1)}, f32[48,1024]{1,0:T(8,128)S(1)}, u32[]{:S(2)}, u32[]{:S(2)}) collective-permute-start(f32[48,1024]{1,0:T(8,128)S(1)} %fusion.8), channel_id=1, source_target_pairs={{0,8},{8,0},{16,24},{24,16},{1,9},{9,1},{17,25},{25,17},{2,10},{10... | collective-permute-start | bytes 589832 | tf_op jit(solution)/shard_map/ppermute | solution.py:482
  67.2 10.1 %collective-permute-start.13 = (f32[48,1024]{1,0:T(8,128)S(1)}, f32[48,1024]{1,0:T(8,128)S(1)}, u32[]{:S(2)}, u32[]{:S(2)}) collective-permute-start(f32[48,1024]{1,0:T(8,128)S(1)} %fusion.4), channel_id=1, source_target_pairs={{0,16},{8,24},{16,0},{24,8},{1,17},{9,25},{17,1},{25,9},{2,18},{10... | collective-permute-start | bytes 589832 | tf_op jit(solution)/shard_map/ppermute | solution.py:481
  70.0 7.3 %collective-permute-start.15 = (f32[48,1024]{1,0:T(8,128)S(1)}, f32[48,1024]{1,0:T(8,128)S(1)}, u32[]{:S(2)}, u32[]{:S(2)}) collective-permute-start(f32[48,1024]{1,0:T(8,128)S(1)} %fusion), channel_id=1, source_target_pairs={{0,8},{8,0},{16,24},{24,16},{1,9},{9,1},{17,25},{25,17},{2,10},{10... | collective-permute-start | bytes 589832 | tf_op jit(solution)/shard_map/ppermute | solution.py:482

commit v3 on v2

--- a/solution.py
+++ b/solution.py
@@ -19,7 +19,7 @@
 SMALL_VMEM = 4 * MIB
 FINISH_VMEM = 16 * MIB
 PARTS = (32, 48, 48)
-PLACES = 6
+DOC_ROWS = 8
 FAR = 1e30
 
 
@@ -39,22 +39,11 @@
     )
 
 
-def doc_starts(place_ref):
-    starts, total = [], jnp.int32(0)
-    for j in range(PLACES, place_ref.shape[0]):
-        starts.append(total)
-        total = total + place_ref[j]
-    return starts
-
-
-def chunk_flags(first_stretch, starts, chunks):
-    def flag(stretch):
-        hit = stretch == starts[0]
-        for s in starts[1:]:
-            hit = hit | (stretch == s)
-        return jnp.where(hit, 0.0, 1.0).astype(F32)
-
-    return [(flag(first_stretch + 2 * n), flag(first_stretch + 2 * n + 1)) for n in range(chunks)]
+def keep_flags(docs, first_stretch, stretches):
+    before = lax.broadcasted_iota(jnp.int32, (CHUNK, CHUNK), 0) < lax.broadcasted_iota(jnp.int32, (CHUNK, CHUNK), 1)
+    starts = mm(docs.astype(BF16), before.astype(F32).astype(BF16))[0:1, :]
+    ids = (lax.broadcasted_iota(jnp.int32, (stretches, CHUNK), 0) + first_stretch).astype(F32)
+    return 1.0 - jnp.max(jnp.where(ids == starts, 1.0, 0.0), axis=1, keepdims=True)
 
 
 def fade_bias(row, col, k2):
@@ -91,10 +80,12 @@
     second = lax.broadcasted_iota(jnp.int32, (1, CHUNK), 1) >= STRETCH
     both_eye = jnp.concatenate([eye, eye], axis=1)
     loads[0].wait()
-    keeps = chunk_flags(place_ref[1] * (2 * chunks), doc_starts(place_ref), chunks)
-    heads_all = rates_ref.shape[0] // 2
+    heads_all = (rates_ref.shape[0] - DOC_ROWS) // 2
+    keep = keep_flags(rates_ref[2 * heads_all :, :CHUNK], place_ref[1] * (2 * chunks), 2 * chunks)
+    keeps = [(keep[2 * n : 2 * n + 1], keep[2 * n + 1 : 2 * n + 2]) for n in range(chunks)]
     loads[1].wait()
 
+    outs = {}
     for step in range(2):
         side = lax.rem(step + place_ref[0], 2)
         turn = lax.rem(heads_all - 2 * half * side, heads_all)
@@ -107,7 +98,9 @@
 
         decay, beta = by_chunk(0), by_chunk(heads_all)
         cum = jnp.dot(decay, upper, precision=lax.Precision.HIGHEST, preferred_element_type=F32)
-        (cum_t_ref if step == 0 else cum_m_ref)[...] = cum
+        cum_ref = (cum_t_ref, cum_m_ref)[step]
+        cum_ref[: chunks * heads_all, :] = cum
+        cum_ref[chunks * heads_all :, :] = jnp.broadcast_to(keep, (2 * chunks, CHUNK))
         grown = jnp.exp(cum)
         cum_col, beta_col = cum.T, beta.T
 
@@ -157,8 +150,7 @@
 
         if step == 0:
             loads[2].wait()
-        pair_ref, held_ref = ((pair_t_ref, held_t_ref), (pair_m_ref, held_m_ref))[step]
-        outs = {}
+        pair_ref = (pair_t_ref, pair_m_ref)[step]
         for (n, g, k_unit, heads), t in zip(pairs, inverses):
             rows = slice(n * CHUNK, (n + 1) * CHUNK)
             values = v_ref[rows, pl.ds(pl.multiple_of((side * half + g) * 2 * DV, 2 * DV), 2 * DV)]
@@ -173,27 +165,29 @@
                     [wy_keys[e * CHUNK : (e + 1) * CHUNK], wy_values[:, e * DV : (e + 1) * DV]], axis=1
                 )
                 pair_ref[2 * g + e, rows, :] = pair
-                outs[n, 2 * g + e] = (mm(heads[e]["k_out"], pair), heads[e]["through"])
-
-        carried = [None] * (2 * half)
-        for n in range(chunks):
+                outs[step, n, 2 * g + e] = (mm(heads[e]["k_out"], pair), heads[e]["through"])
+
+    carried = {}
+    for n in range(chunks):
+        for step in range(2):
             for j in range(2 * half):
-                moved, through = outs[n, j]
+                moved, through = outs[step, n, j]
                 if n == 0:
-                    carried[j] = jnp.concatenate([eye * through - moved[:, :DK], moved[:, DK:]], axis=1)
+                    carried[step, j] = jnp.concatenate([eye * through - moved[:, :DK], moved[:, DK:]], axis=1)
                     continue
-                held = carried[j].astype(BF16)
-                held_ref[j, n - 1] = held
-                after = carried[j] * through - mm(moved[:, :DK].astype(BF16), held)
-                carried[j] = jnp.concatenate([after[:, :DK], after[:, DK:] + moved[:, DK:]], axis=1)
-        for j in range(2 * half):
-            (theirs_ref if step == 0 else mine_ref)[j] = carried[j]
+                held = carried[step, j].astype(BF16)
+                (held_t_ref, held_m_ref)[step][j, n - 1] = held
+                after = carried[step, j] * through - mm(moved[:, :DK].astype(BF16), held)
+                carried[step, j] = jnp.concatenate([after[:, :DK], after[:, DK:] + moved[:, DK:]], axis=1)
+    for j in range(2 * half):
+        theirs_ref[j] = carried[0, j]
+        mine_ref[j] = carried[1, j]
 
 
 def state_maps(place, keys, values, rates):
     tokens, key_width = keys.shape
     key_heads = key_width // DK
-    heads = rates.shape[0] // 2
+    heads = (rates.shape[0] - DOC_ROWS) // 2
     chunks = tokens // CHUNK
     part = heads // 2
     local = pl.BlockSpec(memory_space=pltpu.VMEM)
@@ -203,7 +197,7 @@
         out_shape=[jax.ShapeDtypeStruct((part, DK, DK + DV), F32)] * 2
         + [jax.ShapeDtypeStruct((part, tokens, DK + DV), BF16)] * 2
         + [jax.ShapeDtypeStruct((part, chunks - 1, DK, DK + DV), BF16)] * 2
-        + [jax.ShapeDtypeStruct((chunks * heads, CHUNK), F32)] * 2,
+        + [jax.ShapeDtypeStruct((chunks * (heads + 2), CHUNK), F32)] * 2,
         in_specs=[pl.BlockSpec(memory_space=pltpu.SMEM)] + [remote] * 3,
         out_specs=[local] * 8,
         scratch_shapes=[
@@ -226,8 +220,9 @@
     row = lax.broadcasted_iota(jnp.int32, (CHUNK, CHUNK), 0)
     col = lax.broadcasted_iota(jnp.int32, (CHUNK, CHUNK), 1)
     second_col = lax.broadcasted_iota(jnp.int32, (CHUNK, 1), 0) >= STRETCH
-    keeps = chunk_flags(place_ref[1] * (2 * chunks), doc_starts(place_ref), chunks)
-    cum = cum_ref[...]
+    keep = cum_ref[chunks * heads_all :, :]
+    keeps = [(keep[2 * n : 2 * n + 1, 0:1], keep[2 * n + 1 : 2 * n + 2, 0:1]) for n in range(chunks)]
+    cum = cum_ref[: chunks * heads_all, :]
     cum_col = cum.T
     grown_col = jnp.exp(cum_col)
     for n in range(chunks):
@@ -278,16 +273,23 @@
     )(place, queries, keys, cum, pair, held)
 
 
+def two_terms(value):
+    high = value.astype(BF16)
+    return high, (value - high.astype(F32)).astype(BF16)
+
+
 def exact(left, right):
-    return jnp.dot(left, right, precision=lax.Precision.HIGHEST, preferred_element_type=F32)
-
-
-def group_kernel(core_ref, mine_ref, other_ref, map_ref, state_ref):
+    (high, low), (right_high, right_low) = two_terms(left), two_terms(right)
+    rows = left.shape[0]
+    both = mm(jnp.concatenate([high, low], axis=0), right_high)
+    return both[:rows] + (both[rows:] + mm(high, right_low))
+
+
+def group_kernel(columns, core_ref, mine_ref, other_ref, out_ref):
     def join(first_ref, second_ref):
         for j in range(first_ref.shape[0]):
-            joined = exact(second_ref[j][:, :DK], first_ref[j])
-            map_ref[j] = joined[:, :DK]
-            state_ref[j] = joined[:, DK:] + second_ref[j][:, DK:]
+            joined = exact(second_ref[j][:, :DK], first_ref[j][:, columns])
+            out_ref[j] = joined + second_ref[j][:, DK:] if columns.start else joined
 
     @pl.when(core_ref[2] == 0)
     def _():
@@ -316,44 +318,69 @@
         through(other_ref, send_ref, keep_ref)
 
 
-def small_call(kernel, place, *operands):
+def small_call(kernel, outs, place, *operands):
     part = operands[0].shape[0]
     local = pl.BlockSpec(memory_space=pltpu.VMEM)
     return pl.pallas_call(
         kernel,
-        out_shape=[jax.ShapeDtypeStruct((part, DK, DV), F32)] * 2,
+        out_shape=[jax.ShapeDtypeStruct((part, DK, DV), F32)] * outs,
         in_specs=[pl.BlockSpec(memory_space=pltpu.SMEM)] + [local] * len(operands),
-        out_specs=[local] * 2,
+        out_specs=[local] * outs,
         compiler_params=pltpu.CompilerParams(vmem_limit_bytes=SMALL_VMEM),
     )(place, *operands)
 
 
-def finish_kernel(
-    offset, heads, place_ref, reach_m_ref, core_m_ref, reach_t_ref, core_t_ref, gate_ref, gain_ref, kept_ref, got_ref,
-    weight_ref, send_x_ref, send_y_ref, keep_l_ref, keep_r_ref, gated_ref,
+def gated_rows(rows, own, cols, reach_ref, core_ref, gate_ref, gain, state):
+    reach = jnp.concatenate([reach_ref[r, own] for r in rows], axis=0)
+    core = jnp.concatenate([core_ref[r, own] for r in rows], axis=0)
+    gate = jnp.concatenate([gate_ref[r, cols] for r in rows], axis=0).astype(F32)
+    core = core + mm(reach, state.astype(BF16))
+    normed = core * lax.rsqrt(jnp.mean(core * core, axis=-1, keepdims=True) + 1e-6)
+    return (normed * gain * (gate / (1.0 + jnp.exp(-gate)))).astype(BF16)
+
+
+def part_rows(place_ref, share, offset, size):
+    return [pl.ds(pl.multiple_of((i ^ place_ref[3]) * share + offset, 16), size) for i in range(4)]
+
+
+def early_kernel(
+    size, place_ref, reach_ref, core_ref, gate_ref, gain_ref, kept_ref, weight_ref, gated_ref, product_ref
 ):
-    size = send_x_ref.shape[1]
     share = gate_ref.shape[0] // 4
     gain = gain_ref[...]
-    first = place_ref[4]
-    half = heads // 2
-    for i in range(4):
-        rows = pl.ds(pl.multiple_of((i ^ place_ref[3]) * share + offset, 16), size)
-        for side, (reach_ref, core_ref, state_ref) in enumerate(
-            ((reach_m_ref, core_m_ref, kept_ref), (reach_t_ref, core_t_ref, got_ref))
-        ):
-            for j in range(half):
-                head = first + j if side == 0 else half - first + j
-                cols = pl.ds(pl.multiple_of(head * DV, DV), DV)
-                own = slice(j * DV, (j + 1) * DV)
-                core = core_ref[rows, own] + mm(reach_ref[rows, own], state_ref[j].astype(BF16))
-                gate = gate_ref[rows, cols].astype(F32)
-                normed = core * lax.rsqrt(jnp.mean(core * core, axis=-1, keepdims=True) + 1e-6)
-                gated = normed * gain * (gate / (1.0 + jnp.exp(-gate)))
-                gated_ref[i * size : (i + 1) * size, cols] = gated.astype(BF16)
+    half = kept_ref.shape[0]
+    every = [slice(0, 4 * share)]
+    for j in range(half):
+        own = slice(j * DV, (j + 1) * DV)
+        cols = pl.ds(pl.multiple_of((place_ref[4] + j) * DV, DV), DV)
+        gated_ref[:, own] = gated_rows(every, own, cols, reach_ref, core_ref, gate_ref, gain, kept_ref[j])
+    first = jnp.concatenate([gated_ref[r, :] for r in part_rows(place_ref, share, 0, size)], axis=0)
+    depth = half * DV
+    product_ref[...] = mm(first, weight_ref[pl.ds(pl.multiple_of(place_ref[4] * DV, depth), depth), :])
+
+
+def finish_kernel(offset, place_ref, reach_ref, core_ref, gate_ref, gain_ref, got_ref, weight_ref, early_ref, *refs):
+    gated_ref, (send_x_ref, send_y_ref, keep_l_ref, keep_r_ref) = refs[-1], refs[-5:-1]
+    product_ref = refs[0] if len(refs) > 5 else None
+    size = send_x_ref.shape[1]
+    gain = gain_ref[...]
+    half = got_ref.shape[0]
+    depth = half * DV
+    rows = part_rows(place_ref, gate_ref.shape[0] // 4, offset, size)
+    for j in range(half):
+        own = slice(j * DV, (j + 1) * DV)
+        cols = pl.ds(pl.multiple_of((half - place_ref[4] + j) * DV, DV), DV)
+        gated_ref[:, own] = gated_rows(rows, own, cols, reach_ref, core_ref, gate_ref, gain, got_ref[j])
+    here = pl.ds(pl.multiple_of(place_ref[4] * DV, depth), depth)
+    there = pl.ds(pl.multiple_of((half - place_ref[4]) * DV, depth), depth)
+    if product_ref is None:
+        early = jnp.concatenate([early_ref[r, :] for r in rows], axis=0)
     width = weight_ref.shape[1] // 2
-    left = mm(gated_ref[...], weight_ref[:, :width])
-    right = mm(gated_ref[...], weight_ref[:, width:])
+    sums = []
+    for cols in (slice(0, width), slice(width, 2 * width)):
+        base = mm(early, weight_ref[here, cols]) if product_ref is None else product_ref[:, cols]
+        sums.append(base + mm(gated_ref[...], weight_ref[there, cols]))
+    left, right = sums
     for i, (l_ref, l_at, r_ref, r_at) in enumerate(
         (
             (keep_l_ref, 0, keep_r_ref, 0),
@@ -366,23 +393,39 @@
         r_ref[r_at] = right[i * size : (i + 1) * size]
 
 
-def finish(offset, size, place, reads, gate, gain, kept, got, weight):
-    depth = gate.shape[1]
-    width = weight.shape[1] // 2
-    heads = depth // DV
+def begin(size, place, reads, gate, gain, kept, weight):
+    tokens = gate.shape[0]
     local = pl.BlockSpec(memory_space=pltpu.VMEM)
     return pl.pallas_call(
-        functools.partial(finish_kernel, offset, heads),
+        functools.partial(early_kernel, size),
+        out_shape=[
+            jax.ShapeDtypeStruct((tokens, kept.shape[0] * DV), BF16),
+            jax.ShapeDtypeStruct((4 * size, weight.shape[1]), F32),
+        ],
+        in_specs=[pl.BlockSpec(memory_space=pltpu.SMEM)] + [local] * 6,
+        out_specs=[local] * 2,
+        compiler_params=pltpu.CompilerParams(vmem_limit_bytes=FINISH_VMEM),
+        cost_estimate=pl.CostEstimate(flops=10**9, bytes_accessed=6 * 10**6, transcendentals=tokens * 512),
+        name="early",
+    )(place, *reads, gate, gain, kept, weight)
+
+
+def finish(offset, size, place, reads, gate, gain, got, weight, early):
+    width = weight.shape[1] // 2
+    depth = got.shape[0] * DV
+    local = pl.BlockSpec(memory_space=pltpu.VMEM)
+    return pl.pallas_call(
+        functools.partial(finish_kernel, offset),
         out_shape=[jax.ShapeDtypeStruct((2, size, width), F32)] * 4,
-        in_specs=[pl.BlockSpec(memory_space=pltpu.SMEM)] + [local] * 9,
+        in_specs=[pl.BlockSpec(memory_space=pltpu.SMEM)] + [local] * (6 + len(early)),
         out_specs=[local] * 4,
         scratch_shapes=[pltpu.VMEM((4 * size, depth), BF16)],
         compiler_params=pltpu.CompilerParams(vmem_limit_bytes=FINISH_VMEM),
         cost_estimate=pl.CostEstimate(
-            flops=8 * size * depth * width * 2, bytes_accessed=16 * size * width, transcendentals=4 * size * depth
+            flops=16 * size * depth * width * 2, bytes_accessed=16 * size * width, transcendentals=8 * size * depth
         ),
         name="finish",
-    )(place, *reads, gate, gain.reshape(1, DV), kept, got, weight)
+    )(place, *reads, gate, gain, got, weight, *early)
 
 
 def precise(left, right):
@@ -446,19 +489,23 @@
     second = here if ctx == 2 else 0 * here
     group = lax.axis_index("outer")
     place = jnp.stack([1 - second, position, here, lax.axis_index("tp"), second * (heads // 2), group])
-    place = jnp.concatenate([place.astype(jnp.int32), docs])
-    rates = jnp.concatenate([decay, beta], axis=0)
+    place = place.astype(jnp.int32)
+    lengths = lax.broadcast_in_dim(docs, (DOC_ROWS, docs.shape[0]), (1,))
+    lengths = jnp.pad(lengths, ((0, 0), (0, decay.shape[1] - docs.shape[0]))).astype(F32)
+    rates = jnp.concatenate([decay, beta, lengths], axis=0)
     theirs, mine, pair_t, pair_m, held_t, held_m, cum_t, cum_m = state_maps(place, keys, values, rates)
     if ctx == 2:
         swap = [(0, 1), (1, 0)]
         other = lax.ppermute(theirs, "ctx", swap)
-        group_map, group_state = small_call(group_kernel, place, mine, other)
+        (group_state,) = small_call(functools.partial(group_kernel, slice(DK, DK + DV)), 1, place, mine, other)
+        later, _ = lax.optimization_barrier((place, group_state))
+        (group_map,) = small_call(functools.partial(group_kernel, slice(0, DK)), 1, later, mine, other)
         beside = (
             (functools.partial(read_out, 1), place, (queries, keys, cum_m, pair_m, held_m)),
             (functools.partial(read_out, 0), place, (queries, keys, cum_t, pair_t, held_t)),
         )
         former, latter, reads = group_hops(group_map, group_state, outer, beside)
-        kept, sent = small_call(functools.partial(enter_kernel, outer // 2), place, mine, other, former, latter)
+        kept, sent = small_call(functools.partial(enter_kernel, outer // 2), 2, place, mine, other, former, latter)
         got = lax.ppermute(sent, "ctx", swap)
     else:
         kept, got = whole_prefix(mine, theirs, ctx, outer)
@@ -466,12 +513,16 @@
             read_out(1, place, queries, keys, cum_m, pair_m, held_m),
             read_out(0, place, queries, keys, cum_t, pair_t, held_t),
         ]
-    reads = [array for pair in reads for array in pair]
+    gain = gain.reshape(1, DV)
+    early_place = place
+    if ctx == 2:
+        early_place, _ = lax.optimization_barrier((place, sent))
+    early = begin(PARTS[0], early_place, reads[0], gate, gain, kept, weight)
     along_x = [(i, i ^ 1) for i in range(4)]
     along_y = [(i, i ^ 2) for i in range(4)]
     halves, offset = [], 0
     for size in PARTS:
-        send_x, send_y, keep_l, keep_r = finish(offset, size, place, reads, gate, gain, kept, got, weight)
+        send_x, send_y, keep_l, keep_r = finish(offset, size, place, reads[1], gate, gain, got, weight, early[: 1 if offset else 2])
         offset += size
         got_x = lax.ppermute(send_x, "tp", along_x)
         got_y = lax.ppermute(send_y, "tp", along_y)

time: 78.6 us -> 78.1 us (level)
  Pallas kernels: 24.1 us -> 26.7 us
  local copies, waits for them, and re-layouts: 2.84 us -> 1.15 us
  waiting for transfers between devices: 30.9 us -> 29.5 us
    pallas_call x2, Pallas kernels: 5.23 us -> 7.26 us  [read_out(): pl.pallas_call(functools.partial(read_kernel, step, chunks, key_heads), o...]
    ppermute x2, waiting for transfers between devices: 7.08 us -> 5.29 us  [group_hops(): state = lax.ppermute(leaving, 'outer', step)]
    ppermute x1, waiting for transfers between devices: 1.52 us -> 0.01 us  [shards(): got = lax.ppermute(sent, 'ctx', swap)]
    unnamed x10, local copies, waits for them, and re-layouts: 2.1 us -> 1.07 us
    pallas_call x3 -> x4, Pallas kernels: 6.25 us -> 6.66 us  [the longest x3 4.94 us: finish(): pl.pallas_call(functools.partial(finish_kernel, offset), out_shape=[jax.S...]
    pallas_call x2 -> x3, Pallas kernels: 2.06 us -> 2.43 us  [small_call(): pl.pallas_call(kernel, out_shape=[jax.ShapeDtypeStruct((part, DK, DV), F3...]
  transfers between devices with their start and end apart: 16 -> 16, of which waited for: 9 -> 9; matrix products, arithmetic and copies ran while one was open for 0% -> 0% of each run, Pallas kernels for 12% -> 17%
where the time goes in v3:
time: 78.1 us; the launch traced here: 77.7 us
  waiting for transfers between devices  29.5 us (38%)
  Pallas kernels  26.7 us (34%)
  starting transfers between devices  17.2 us (22%)
  other arithmetic  2.58 us (3%)
  local copies, waits for them, and re-layouts  1.15 us (1%)
    ppermute x3, waiting for transfers between devices, shards(): got_x = lax.ppermute(send_x, 'tp', along_x)  12.3 us
    pallas_call x1, Pallas kernels, state_maps(): pl.pallas_call(functools.partial(maps_kernel, chunks, key_heads), out_sha...  10.3 us
    ppermute x3, waiting for transfers between devices, shards(): last_l = lax.ppermute(keep_l[1] + got_x[1], 'tp', along_y)  9.22 us
    pallas_call x2, Pallas kernels, read_out(): pl.pallas_call(functools.partial(read_kernel, step, chunks, key_heads), o...  7.26 us
    ppermute x2, starting transfers between devices, group_hops(): state = lax.ppermute(leaving, 'outer', step)  5.29 us
    ppermute x2, waiting for transfers between devices, group_hops(): state = lax.ppermute(leaving, 'outer', step)  5.29 us
    pallas_call x3, Pallas kernels, finish(): pl.pallas_call(functools.partial(finish_kernel, offset), out_shape=[jax.S...  4.94 us
    ppermute x3, starting transfers between devices, shards(): got_x = lax.ppermute(send_x, 'tp', along_x)  3.72 us
  transfers between devices with their start and end apart: 16, of which 9 were waited for; matrix products, arithmetic and copies ran while one was open for 0% of the time, Pallas kernels for 17%

profile of v3, /device:TPU:12, one launch (start us, length us, event | category | flops | bytes accessed | tf_op | source)
XLA Modules:
  0.0 77.7 jit_solution(16287183211696400924)
XLA Ops:
  0.0 0.7 pad_convert_fusion
  0.7 0.7 pad_maximum_fusion.rates_hbm
  1.5 1.0 %copy-done.2 = bf16[512,512]{1,0:T(8,128)(2,1)S(1)} copy-done((bf16[512,512]{1,0:T(8,128)(2,1)S(1)}, bf16[512,512]{1,0:T(8,128)(2,1)}, u32[]{:S(2)}) %copy-start.2) | copy-done | bytes 524312
  2.5 10.3 %state_maps.1 = (f32[4,128,256]{2,1,0:T(8,128)S(1)}, f32[4,128,256]{2,1,0:T(8,128)S(1)}, bf16[4,512,256]{2,1,0:T(8,128)(2,1)S(1)}, bf16[4,512,256]{2,1,0:T(8,128...) custom-call(s32[6]{0:T(128)S(1)} %stack.27.place_ref.core_ref, ...), custom_call_target="tpu_custom_call" | custom-call | tf_op jit(solution)/shard_map/state_maps/pallas_call | solution.py:195
  13.0 1.9 %collective-permute-done.other_ref = f32[4,128,256]{2,1,0:T(8,128)S(1)} collective-permute-done((f32[4,128,256]{2,1,0:T(8,128)S(1)}, f32[4,128,256]{2,1,0:T(8,128)S(1)}, u32[]{:S(2)}, u32[]{:S(2)}) %collective-permute-start) | collective-permute-done | bytes 524320 | tf_op jit(solution)/shard_map/ppermute | solution.py:499
  14.8 0.8 %shard_map.91 = f32[4,128,128]{2,1,0:T(8,128)S(1)} custom-call(s32[6]{0:T(128)S(1)} %stack.27.place_ref.core_ref, f32[4,128,256]{2,1,0:T(8,128)S(1)} %get-tuple-element.42.mine_ref, f32[4,128,256]{2,1,0:T(8,128)S(1)} %collective-permute-done.other_ref), custom_call_target="tpu_custom_call" | custom-call | tf_op jit(solution)/shard_map/pallas_call | solution.py:324
  15.7 1.6 %collective-permute-start.1 = (f32[4,128,128]{2,1,0:T(8,128)S(1)}, f32[4,128,128]{2,1,0:T(8,128)S(1)}, u32[]{:S(2)}, u32[]{:S(2)}) collective-permute-start(f32[4,128,128]{2,1,0:T(8,128)S(1)} %shard_map.91), channel_id=1, source_target_pairs={{0,1},{1,2},{2,3},{3,0},{4,5},{5,6},{6,7},{7,4},{8,9},{9,10},{10,1... | collective-permute-start | bytes 786440 | tf_op jit(solution)/shard_map/ppermute | solution.py:449
  17.3 0.8 %shard_map.92 = f32[4,128,128]{2,1,0:T(8,128)S(1)} custom-call(s32[6]{0:T(128)S(1)} %stack.27.place_ref.core_ref, f32[4,128,256]{2,1,0:T(8,128)S(1)} %get-tuple-element.42.mine_ref, f32[4,128,256]{2,1,0:T(8,128)S(1)} %collective-permute-done.other_ref), custom_call_target="tpu_custom_call" | custom-call | tf_op jit(solution)/shard_map/pallas_call | solution.py:324
  18.1 3.6 %read_out.2 = (bf16[512,512]{1,0:T(8,128)(2,1)S(1)}, f32[512,512]{1,0:T(8,128)S(1)}) custom-call(s32[6]{0:T(128)S(1)} %stack.27.place_ref.core_ref, bf16[512,512]{1,0:T(8,128)(2,1)S(1)} %copy-done.4, bf16[512,512]{1,0:T(8,128)(2,1)S(1)} %copy-done.2, f32[40,128]{1,0:T(8,128)S(1)} %get-tuple-element.45.cum_ref, ...), custom_call_target="tpu_custom_call" | custom-call | flops 2000000000 | bytes 6000000 | tf_op jit(solution)/shard_map/read_out/pallas_call | solution.py:262
  21.7 2.3 %collective-permute-done.1.former_ref = f32[4,128,128]{2,1,0:T(8,128)S(1)} collective-permute-done((f32[4,128,128]{2,1,0:T(8,128)S(1)}, f32[4,128,128]{2,1,0:T(8,128)S(1)}, u32[]{:S(2)}, u32[]{:S(2)}) %collective-permute-start.1) | collective-permute-done | bytes 262176 | tf_op jit(solution)/shard_map/ppermute | solution.py:449
  24.5 3.7 %collective-permute-start.2 = (f32[4,128,128]{2,1,0:T(8,128)S(1)}, f32[4,128,128]{2,1,0:T(8,128)S(1)}, u32[]{:S(2)}, u32[]{:S(2)}) collective-permute-start(f32[4,128,128]{2,1,0:T(8,128)S(1)} %convolution_add_fusion), channel_id=1, source_target_pairs={{1,2},{2,3},{3,1},{5,6},{6,7},{7,5},{9,10},{10,11},{11,9},{13,14},... | collective-permute-start | bytes 786440 | tf_op jit(solution)/shard_map/ppermute | solution.py:449
  28.2 3.6 %read_out.3 = (bf16[512,512]{1,0:T(8,128)(2,1)S(1)}, f32[512,512]{1,0:T(8,128)S(1)}) custom-call(s32[6]{0:T(128)S(1)} %stack.27.place_ref.core_ref, bf16[512,512]{1,0:T(8,128)(2,1)S(1)} %copy-done.4, bf16[512,512]{1,0:T(8,128)(2,1)S(1)} %copy-done.2, f32[40,128]{1,0:T(8,128)S(1)} %get-tuple-element.52.cum_ref, ...), custom_call_target="tpu_custom_call" | custom-call | flops 2000000000 | bytes 6000000 | tf_op jit(solution)/shard_map/read_out/pallas_call | solution.py:262
  31.8 3.0 %collective-permute-done.2.latter_ref = f32[4,128,128]{2,1,0:T(8,128)S(1)} collective-permute-done((f32[4,128,128]{2,1,0:T(8,128)S(1)}, f32[4,128,128]{2,1,0:T(8,128)S(1)}, u32[]{:S(2)}, u32[]{:S(2)}) %collective-permute-start.2) | collective-permute-done | bytes 262176 | tf_op jit(solution)/shard_map/ppermute | solution.py:449
  34.8 0.8 %shard_map.93 = (f32[4,128,128]{2,1,0:T(8,128)S(1)}, f32[4,128,128]{2,1,0:T(8,128)S(1)}) custom-call(s32[6]{0:T(128)S(1)} %stack.27.place_ref.core_ref, f32[4,128,256]{2,1,0:T(8,128)S(1)} %get-tuple-element.42.mine_ref, f32[4,128,256]{2,1,0:T(8,128)S(1)} %collective-permute-done.other_ref, f32[4,128,128]{2,1,0:T(8,128)S(1)} %collective-permute-done.1.former_ref, ...), custom_call_target="tpu_custom_call" | custom-call | tf_op jit(solution)/shard_map/pallas_call | solution.py:324
  35.7 1.7 %early.1 = (bf16[512,512]{1,0:T(8,128)(2,1)S(1)}, f32[128,2048]{1,0:T(8,128)S(1)}) custom-call(s32[6]{0:T(128)S(1)} %stack.27.place_ref.core_ref, bf16[512,512]{1,0:T(8,128)(2,1)S(1)} %get-tuple-element.62.reach_ref, f32[512,512]{1,0:T(8,128)S(1)} %get-tuple-element.63.core_ref, bf16[512,1024]{1,0:T(8,128)(2,1)S(1)} %copy-done.1, f32[1,128]{1,0:T(1,128)S(1)} %bitcast.57, ...), custom_call_target="tpu_custom_call" | custom-call | flops 1000000000 | bytes 6000000 | tf_op jit(solution)/shard_map/early/pallas_call | solution.py:399
  37.5 1.3 %finish.3 = (f32[2,32,1024]{2,1,0:T(8,128)S(1)}, f32[2,32,1024]{2,1,0:T(8,128)S(1)}, f32[2,32,1024]{2,1,0:T(8,128)S(1)}, f32[2,32,1024]{2,1,0:T(8,128)S(1)}) custom-call(s32[6]{0:T(128)S(1)} %stack.27.place_ref.core_ref, bf16[512,512]{1,0:T(8,128)(2,1)S(1)} %get-tuple-element.57.reach_ref, f32[512,512]{1,0:T(8,128)S(1)} %get-tuple-element.58.core_ref, ...), custom_call_target="tpu_custom_call" | custom-call | flops 536870912 | bytes 524288 | tf_op jit(solution)/shard_map/finish/pallas_call | solution.py:417
  38.7 1.6 %collective-permute-start.4 = (f32[2,32,1024]{2,1,0:T(8,128)S(1)}, f32[2,32,1024]{2,1,0:T(8,128)S(1)}, u32[]{:S(2)}, u32[]{:S(2)}) collective-permute-start(f32[2,32,1024]{2,1,0:T(8,128)S(1)} %get-tuple-element.68), channel_id=1, source_target_pairs={{0,8},{8,0},{16,24},{24,16},{1,9},{9,1},{17,25},{25,17},{2,10},{10... | collective-permute-start | bytes 786440 | tf_op jit(solution)/shard_map/ppermute | solution.py:527
  40.8 1.8 %finish.5 = (f32[2,48,1024]{2,1,0:T(8,128)S(1)}, f32[2,48,1024]{2,1,0:T(8,128)S(1)}, f32[2,48,1024]{2,1,0:T(8,128)S(1)}, f32[2,48,1024]{2,1,0:T(8,128)S(1)}) custom-call(s32[6]{0:T(128)S(1)} %stack.27.place_ref.core_ref, bf16[512,512]{1,0:T(8,128)(2,1)S(1)} %get-tuple-element.57.reach_ref, f32[512,512]{1,0:T(8,128)S(1)} %get-tuple-element.58.core_ref, ...), custom_call_target="tpu_custom_call" | custom-call | flops 805306368 | bytes 786432 | tf_op jit(solution)/shard_map/finish/pallas_call | solution.py:417
  42.6 0.6 collective-permute-start.12
  43.2 1.5 %collective-permute-start.14 = (f32[2,48,1024]{2,1,0:T(8,128)S(1)}, f32[2,48,1024]{2,1,0:T(8,128)S(1)}, u32[]{:S(2)}, u32[]{:S(2)}) collective-permute-start(f32[2,48,1024]{2,1,0:T(8,128)S(1)} %get-tuple-element.78), channel_id=1, source_target_pairs={{0,16},{8,24},{16,0},{24,8},{1,17},{9,25},{17,1},{25,9},{2,18},{10... | collective-permute-start | bytes 1179656 | tf_op jit(solution)/shard_map/ppermute | solution.py:528
  44.8 1.8 %finish.4 = (f32[2,48,1024]{2,1,0:T(8,128)S(1)}, f32[2,48,1024]{2,1,0:T(8,128)S(1)}, f32[2,48,1024]{2,1,0:T(8,128)S(1)}, f32[2,48,1024]{2,1,0:T(8,128)S(1)}) custom-call(s32[6]{0:T(128)S(1)} %stack.27.place_ref.core_ref, bf16[512,512]{1,0:T(8,128)(2,1)S(1)} %get-tuple-element.57.reach_ref, f32[512,512]{1,0:T(8,128)S(1)} %get-tuple-element.58.core_ref, ...), custom_call_target="tpu_custom_call" | custom-call | flops 805306368 | bytes 786432 | tf_op jit(solution)/shard_map/finish/pallas_call | solution.py:417
  46.6 1.6 %collective-permute-start.8 = (f32[2,48,1024]{2,1,0:T(8,128)S(1)}, f32[2,48,1024]{2,1,0:T(8,128)S(1)}, u32[]{:S(2)}, u32[]{:S(2)}) collective-permute-start(f32[2,48,1024]{2,1,0:T(8,128)S(1)} %get-tuple-element.72), channel_id=1, source_target_pairs={{0,8},{8,0},{16,24},{24,16},{1,9},{9,1},{17,25},{25,17},{2,10},{10... | collective-permute-start | bytes 1179656 | tf_op jit(solution)/shard_map/ppermute | solution.py:527
  48.7 0.7 collective-permute-done.6
  49.4 0.9 %collective-permute-start.5 = (f32[32,1024]{1,0:T(8,128)S(1)}, f32[32,1024]{1,0:T(8,128)S(1)}, u32[]{:S(2)}, u32[]{:S(2)}) collective-permute-start(f32[32,1024]{1,0:T(8,128)S(1)} %fusion.20), channel_id=1, source_target_pairs={{0,16},{8,24},{16,0},{24,8},{1,17},{9,25},{17,1},{25,9},{2,18},{10... | collective-permute-start | bytes 393224 | tf_op jit(solution)/shard_map/ppermute | solution.py:532
  50.3 6.0 %collective-permute-done.12 = f32[2,48,1024]{2,1,0:T(8,128)S(1)} collective-permute-done((f32[2,48,1024]{2,1,0:T(8,128)S(1)}, f32[2,48,1024]{2,1,0:T(8,128)S(1)}, u32[]{:S(2)}, u32[]{:S(2)}) %collective-permute-start.12) | collective-permute-done | bytes 393248 | tf_op jit(solution)/shard_map/ppermute | solution.py:527
  56.3 1.5 %collective-permute-start.7 = (f32[32,1024]{1,0:T(8,128)S(1)}, f32[32,1024]{1,0:T(8,128)S(1)}, u32[]{:S(2)}, u32[]{:S(2)}) collective-permute-start(f32[32,1024]{1,0:T(8,128)S(1)} %fusion.16), channel_id=1, source_target_pairs={{0,8},{8,0},{16,24},{24,16},{1,9},{9,1},{17,25},{25,17},{2,10},{10... | collective-permute-start | bytes 393224 | tf_op jit(solution)/shard_map/ppermute | solution.py:533
  58.4 6.3 %collective-permute-done.8 = f32[2,48,1024]{2,1,0:T(8,128)S(1)} collective-permute-done((f32[2,48,1024]{2,1,0:T(8,128)S(1)}, f32[2,48,1024]{2,1,0:T(8,128)S(1)}, u32[]{:S(2)}, u32[]{:S(2)}) %collective-permute-start.8) | collective-permute-done | bytes 393248 | tf_op jit(solution)/shard_map/ppermute | solution.py:527
  64.7 1.5 %collective-permute-start.15 = (f32[48,1024]{1,0:T(8,128)S(1)}, f32[48,1024]{1,0:T(8,128)S(1)}, u32[]{:S(2)}, u32[]{:S(2)}) collective-permute-start(f32[48,1024]{1,0:T(8,128)S(1)} %fusion), channel_id=1, source_target_pairs={{0,8},{8,0},{16,24},{24,16},{1,9},{9,1},{17,25},{25,17},{2,10},{10... | collective-permute-start | bytes 589832 | tf_op jit(solution)/shard_map/ppermute | solution.py:533
  66.9 2.2 %collective-permute-done.5 = f32[32,1024]{1,0:T(8,128)S(1)} collective-permute-done((f32[32,1024]{1,0:T(8,128)S(1)}, f32[32,1024]{1,0:T(8,128)S(1)}, u32[]{:S(2)}, u32[]{:S(2)}) %collective-permute-start.5) | collective-permute-done | bytes 131104 | tf_op jit(solution)/shard_map/ppermute | solution.py:532
  69.7 3.6 %collective-permute-done.13 = f32[48,1024]{1,0:T(8,128)S(1)} collective-permute-done((f32[48,1024]{1,0:T(8,128)S(1)}, f32[48,1024]{1,0:T(8,128)S(1)}, u32[]{:S(2)}, u32[]{:S(2)}) %collective-permute-start.13) | collective-permute-done | bytes 196640 | tf_op jit(solution)/shard_map/ppermute | solution.py:532
  73.4 3.4 %collective-permute-done.9 = f32[48,1024]{1,0:T(8,128)S(1)} collective-permute-done((f32[48,1024]{1,0:T(8,128)S(1)}, f32[48,1024]{1,0:T(8,128)S(1)}, u32[]{:S(2)}, u32[]{:S(2)}) %collective-permute-start.9) | collective-permute-done | bytes 196640 | tf_op jit(solution)/shard_map/ppermute | solution.py:532
  76.9 0.8 %maximum_maximum_fusion = bf16[128,2048]{1,0:T(8,128)(2,1)} fusion(bf16[48,1024]{1,0:T(8,128)(2,1)S(1)} %fusion.3, bf16[48,1024]{1,0:T(8,128)(2,1)S(1)} %fusion.7, bf16[48,1024]{1,0:T(8,128)(2,1)S(1)} %fusion.11, bf16[48,1024]{1,0:T(8,128)(2,1)S(1)} %fusion.15, bf16[32,1024]{1,0:T(8,128)(2,1)S(1)} %fusion.19, bf16[32,1024]{1,0:T(8,128)(2,1)S(1)} %fusion.23), kind=kLoop, calls=%fused_computation.1 | loop fusion | flops 3145728 | bytes 1048576 | tf_op jit(solution)/shard_map/concatenate | solution.py:537
  (38 shorter events, 3.7 us)
Async XLA Ops:
  1.5 1.0 %copy-start.2 = (bf16[512,512]{1,0:T(8,128)(2,1)S(1)}, bf16[512,512]{1,0:T(8,128)(2,1)}, u32[]{:S(2)}) copy-start(bf16[512,512]{1,0:T(8,128)(2,1)} %k_ref.3) | copy-start | bytes 1572868
  2.5 15.6 %copy-start.4 = (bf16[512,512]{1,0:T(8,128)(2,1)S(1)}, bf16[512,512]{1,0:T(8,128)(2,1)}, u32[]{:S(2)}) copy-start(bf16[512,512]{1,0:T(8,128)(2,1)} %q_ref.3) | copy-start | bytes 1572868
  12.9 2.0 %collective-permute-start = (f32[4,128,256]{2,1,0:T(8,128)S(1)}, f32[4,128,256]{2,1,0:T(8,128)S(1)}, u32[]{:S(2)}, u32[]{:S(2)}) collective-permute-start(f32[4,128,256]{2,1,0:T(8,128)S(1)} %get-tuple-element.43), channel_id=1, source_target_pairs={{0,4},{4,0},{1,5},{5,1},{2,6},{6,2},{3,7},{7,3},{8,12},{12,8},{9,1... | collective-permute-start | bytes 1572872 | tf_op jit(solution)/shard_map/ppermute | solution.py:499
  15.7 8.4 %collective-permute-start.1 = (f32[4,128,128]{2,1,0:T(8,128)S(1)}, f32[4,128,128]{2,1,0:T(8,128)S(1)}, u32[]{:S(2)}, u32[]{:S(2)}) collective-permute-start(f32[4,128,128]{2,1,0:T(8,128)S(1)} %shard_map.91), channel_id=1, source_target_pairs={{0,1},{1,2},{2,3},{3,0},{4,5},{5,6},{6,7},{7,4},{8,9},{9,10},{10,1... | collective-permute-start | bytes 786440 | tf_op jit(solution)/shard_map/ppermute | solution.py:449
  24.5 10.3 %collective-permute-start.2 = (f32[4,128,128]{2,1,0:T(8,128)S(1)}, f32[4,128,128]{2,1,0:T(8,128)S(1)}, u32[]{:S(2)}, u32[]{:S(2)}) collective-permute-start(f32[4,128,128]{2,1,0:T(8,128)S(1)} %convolution_add_fusion), channel_id=1, source_target_pairs={{1,2},{2,3},{3,1},{5,6},{6,7},{7,5},{9,10},{10,11},{11,9},{13,14},... | collective-permute-start | bytes 786440 | tf_op jit(solution)/shard_map/ppermute | solution.py:449
  28.1 7.5 %copy-start = (bf16[1024,2048]{1,0:T(8,128)(2,1)S(1)}, bf16[1024,2048]{1,0:T(8,128)(2,1)}, u32[]{:S(2)}) copy-start(bf16[1024,2048]{1,0:T(8,128)(2,1)} %weight_ref.7) | copy-start | bytes 12582916
  28.1 7.5 %copy-start.1 = (bf16[512,1024]{1,0:T(8,128)(2,1)S(1)}, bf16[512,1024]{1,0:T(8,128)(2,1)}, u32[]{:S(2)}) copy-start(bf16[512,1024]{1,0:T(8,128)(2,1)} %gate_ref.7) | copy-start | bytes 3145732
  28.2 7.5 %copy-start.3 = (f32[128]{0:T(128)S(1)}, f32[128]{0:T(128)}, u32[]{:S(2)}) copy-start(f32[128]{0:T(128)} %param.16) | copy-start | bytes 1540
  35.6 1.8 %collective-permute-start.3 = (f32[4,128,128]{2,1,0:T(8,128)S(1)}, f32[4,128,128]{2,1,0:T(8,128)S(1)}, u32[]{:S(2)}, u32[]{:S(2)}) collective-permute-start(f32[4,128,128]{2,1,0:T(8,128)S(1)} %get-tuple-element.60), channel_id=1, source_target_pairs={{0,4},{4,0},{1,5},{5,1},{2,6},{6,2},{3,7},{7,3},{8,12},{12,8},{9,1... | collective-permute-start | bytes 786440 | tf_op jit(solution)/shard_map/ppermute | solution.py:509
  38.7 9.4 %collective-permute-start.4 = (f32[2,32,1024]{2,1,0:T(8,128)S(1)}, f32[2,32,1024]{2,1,0:T(8,128)S(1)}, u32[]{:S(2)}, u32[]{:S(2)}) collective-permute-start(f32[2,32,1024]{2,1,0:T(8,128)S(1)} %get-tuple-element.68), channel_id=1, source_target_pairs={{0,8},{8,0},{16,24},{24,16},{1,9},{9,1},{17,25},{25,17},{2,10},{10... | collective-permute-start | bytes 786440 | tf_op jit(solution)/shard_map/ppermute | solution.py:527
  40.3 9.1 %collective-permute-start.6 = (f32[2,32,1024]{2,1,0:T(8,128)S(1)}, f32[2,32,1024]{2,1,0:T(8,128)S(1)}, u32[]{:S(2)}, u32[]{:S(2)}) collective-permute-start(f32[2,32,1024]{2,1,0:T(8,128)S(1)} %get-tuple-element.70), channel_id=1, source_target_pairs={{0,16},{8,24},{16,0},{24,8},{1,17},{9,25},{17,1},{25,9},{2,18},{10... | collective-permute-start | bytes 786440 | tf_op jit(solution)/shard_map/ppermute | solution.py:528
  42.6 13.7 %collective-permute-start.12 = (f32[2,48,1024]{2,1,0:T(8,128)S(1)}, f32[2,48,1024]{2,1,0:T(8,128)S(1)}, u32[]{:S(2)}, u32[]{:S(2)}) collective-permute-start(f32[2,48,1024]{2,1,0:T(8,128)S(1)} %get-tuple-element.76), channel_id=1, source_target_pairs={{0,8},{8,0},{16,24},{24,16},{1,9},{9,1},{17,25},{25,17},{2,10},{10... | collective-permute-start | bytes 1179656 | tf_op jit(solution)/shard_map/ppermute | solution.py:527
  43.2 14.6 %collective-permute-start.14 = (f32[2,48,1024]{2,1,0:T(8,128)S(1)}, f32[2,48,1024]{2,1,0:T(8,128)S(1)}, u32[]{:S(2)}, u32[]{:S(2)}) collective-permute-start(f32[2,48,1024]{2,1,0:T(8,128)S(1)} %get-tuple-element.78), channel_id=1, source_target_pairs={{0,16},{8,24},{16,0},{24,8},{1,17},{9,25},{17,1},{25,9},{2,18},{10... | collective-permute-start | bytes 1179656 | tf_op jit(solution)/shard_map/ppermute | solution.py:528
  46.6 18.1 %collective-permute-start.8 = (f32[2,48,1024]{2,1,0:T(8,128)S(1)}, f32[2,48,1024]{2,1,0:T(8,128)S(1)}, u32[]{:S(2)}, u32[]{:S(2)}) collective-permute-start(f32[2,48,1024]{2,1,0:T(8,128)S(1)} %get-tuple-element.72), channel_id=1, source_target_pairs={{0,8},{8,0},{16,24},{24,16},{1,9},{9,1},{17,25},{25,17},{2,10},{10... | collective-permute-start | bytes 1179656 | tf_op jit(solution)/shard_map/ppermute | solution.py:527
  48.2 18.1 %collective-permute-start.10 = (f32[2,48,1024]{2,1,0:T(8,128)S(1)}, f32[2,48,1024]{2,1,0:T(8,128)S(1)}, u32[]{:S(2)}, u32[]{:S(2)}) collective-permute-start(f32[2,48,1024]{2,1,0:T(8,128)S(1)} %get-tuple-element.74), channel_id=1, source_target_pairs={{0,16},{8,24},{16,0},{24,8},{1,17},{9,25},{17,1},{25,9},{2,18},{10... | collective-permute-start | bytes 1179656 | tf_op jit(solution)/shard_map/ppermute | solution.py:528
  49.4 19.7 %collective-permute-start.5 = (f32[32,1024]{1,0:T(8,128)S(1)}, f32[32,1024]{1,0:T(8,128)S(1)}, u32[]{:S(2)}, u32[]{:S(2)}) collective-permute-start(f32[32,1024]{1,0:T(8,128)S(1)} %fusion.20), channel_id=1, source_target_pairs={{0,16},{8,24},{16,0},{24,8},{1,17},{9,25},{17,1},{25,9},{2,18},{10... | collective-permute-start | bytes 393224 | tf_op jit(solution)/shard_map/ppermute | solution.py:532
  56.3 13.3 %collective-permute-start.7 = (f32[32,1024]{1,0:T(8,128)S(1)}, f32[32,1024]{1,0:T(8,128)S(1)}, u32[]{:S(2)}, u32[]{:S(2)}) collective-permute-start(f32[32,1024]{1,0:T(8,128)S(1)} %fusion.16), channel_id=1, source_target_pairs={{0,8},{8,0},{16,24},{24,16},{1,9},{9,1},{17,25},{25,17},{2,10},{10... | collective-permute-start | bytes 393224 | tf_op jit(solution)/shard_map/ppermute | solution.py:533
  57.9 15.4 %collective-permute-start.13 = (f32[48,1024]{1,0:T(8,128)S(1)}, f32[48,1024]{1,0:T(8,128)S(1)}, u32[]{:S(2)}, u32[]{:S(2)}) collective-permute-start(f32[48,1024]{1,0:T(8,128)S(1)} %fusion.4), channel_id=1, source_target_pairs={{0,16},{8,24},{16,0},{24,8},{1,17},{9,25},{17,1},{25,9},{2,18},{10... | collective-permute-start | bytes 589832 | tf_op jit(solution)/shard_map/ppermute | solution.py:532
  64.7 8.6 %collective-permute-start.15 = (f32[48,1024]{1,0:T(8,128)S(1)}, f32[48,1024]{1,0:T(8,128)S(1)}, u32[]{:S(2)}, u32[]{:S(2)}) collective-permute-start(f32[48,1024]{1,0:T(8,128)S(1)} %fusion), channel_id=1, source_target_pairs={{0,8},{8,0},{16,24},{24,16},{1,9},{9,1},{17,25},{25,17},{2,10},{10... | collective-permute-start | bytes 589832 | tf_op jit(solution)/shard_map/ppermute | solution.py:533
  66.3 10.5 %collective-permute-start.9 = (f32[48,1024]{1,0:T(8,128)S(1)}, f32[48,1024]{1,0:T(8,128)S(1)}, u32[]{:S(2)}, u32[]{:S(2)}) collective-permute-start(f32[48,1024]{1,0:T(8,128)S(1)} %fusion.12), channel_id=1, source_target_pairs={{0,16},{8,24},{16,0},{24,8},{1,17},{9,25},{17,1},{25,9},{2,18},{10... | collective-permute-start | bytes 589832 | tf_op jit(solution)/shard_map/ppermute | solution.py:532
  69.1 7.7 %collective-permute-start.11 = (f32[48,1024]{1,0:T(8,128)S(1)}, f32[48,1024]{1,0:T(8,128)S(1)}, u32[]{:S(2)}, u32[]{:S(2)}) collective-permute-start(f32[48,1024]{1,0:T(8,128)S(1)} %fusion.8), channel_id=1, source_target_pairs={{0,8},{8,0},{16,24},{24,16},{1,9},{9,1},{17,25},{25,17},{2,10},{10... | collective-permute-start | bytes 589832 | tf_op jit(solution)/shard_map/ppermute | solution.py:533

commit v4 on v3

--- a/solution.py
+++ b/solution.py
@@ -19,7 +19,6 @@
 SMALL_VMEM = 4 * MIB
 FINISH_VMEM = 16 * MIB
 PARTS = (32, 48, 48)
-DOC_ROWS = 8
 FAR = 1e30
 
 
@@ -39,11 +38,18 @@
     )
 
 
-def keep_flags(docs, first_stretch, stretches):
-    before = lax.broadcasted_iota(jnp.int32, (CHUNK, CHUNK), 0) < lax.broadcasted_iota(jnp.int32, (CHUNK, CHUNK), 1)
-    starts = mm(docs.astype(BF16), before.astype(F32).astype(BF16))[0:1, :]
-    ids = (lax.broadcasted_iota(jnp.int32, (stretches, CHUNK), 0) + first_stretch).astype(F32)
-    return 1.0 - jnp.max(jnp.where(ids == starts, 1.0, 0.0), axis=1, keepdims=True)
+def keep_flags(docs_ref, first_stretch, stretches):
+    starts, total = [], jnp.int32(0)
+    for j in range(docs_ref.shape[0]):
+        starts.append(total)
+        total = total + docs_ref[j]
+    flags = []
+    for stretch in range(stretches):
+        hit = starts[0] == first_stretch + stretch
+        for start in starts[1:]:
+            hit = hit | (start == first_stretch + stretch)
+        flags.append(jnp.where(hit, 0.0, 1.0).astype(F32))
+    return flags
 
 
 def fade_bias(row, col, k2):
@@ -52,7 +58,7 @@
 
 
 def maps_kernel(
-    chunks, key_heads, place_ref, k_hbm, v_hbm, rates_hbm,
+    chunks, key_heads, place_ref, docs_ref, k_hbm, v_hbm, rates_hbm,
     theirs_ref, mine_ref, pair_t_ref, pair_m_ref, held_t_ref, held_m_ref, cum_t_ref, cum_m_ref,
     k_ref, v_ref, rates_ref, sems,
 ):
@@ -80,9 +86,9 @@
     second = lax.broadcasted_iota(jnp.int32, (1, CHUNK), 1) >= STRETCH
     both_eye = jnp.concatenate([eye, eye], axis=1)
     loads[0].wait()
-    heads_all = (rates_ref.shape[0] - DOC_ROWS) // 2
-    keep = keep_flags(rates_ref[2 * heads_all :, :CHUNK], place_ref[1] * (2 * chunks), 2 * chunks)
-    keeps = [(keep[2 * n : 2 * n + 1], keep[2 * n + 1 : 2 * n + 2]) for n in range(chunks)]
+    heads_all = rates_ref.shape[0] // 2
+    keep = keep_flags(docs_ref, place_ref[1] * (2 * chunks), 2 * chunks)
+    keeps = [(keep[2 * n], keep[2 * n + 1]) for n in range(chunks)]
     loads[1].wait()
 
     outs = {}
@@ -100,7 +106,8 @@
         cum = jnp.dot(decay, upper, precision=lax.Precision.HIGHEST, preferred_element_type=F32)
         cum_ref = (cum_t_ref, cum_m_ref)[step]
         cum_ref[: chunks * heads_all, :] = cum
-        cum_ref[chunks * heads_all :, :] = jnp.broadcast_to(keep, (2 * chunks, CHUNK))
+        for i, flag in enumerate(keep):
+            cum_ref[chunks * heads_all + i : chunks * heads_all + i + 1, :] = jnp.full((1, CHUNK), flag, F32)
         grown = jnp.exp(cum)
         cum_col, beta_col = cum.T, beta.T
 
@@ -184,10 +191,10 @@
         mine_ref[j] = carried[1, j]
 
 
-def state_maps(place, keys, values, rates):
+def state_maps(place, docs, keys, values, rates):
     tokens, key_width = keys.shape
     key_heads = key_width // DK
-    heads = (rates.shape[0] - DOC_ROWS) // 2
+    heads = rates.shape[0] // 2
     chunks = tokens // CHUNK
     part = heads // 2
     local = pl.BlockSpec(memory_space=pltpu.VMEM)
@@ -198,7 +205,7 @@
         + [jax.ShapeDtypeStruct((part, tokens, DK + DV), BF16)] * 2
         + [jax.ShapeDtypeStruct((part, chunks - 1, DK, DK + DV), BF16)] * 2
         + [jax.ShapeDtypeStruct((chunks * (heads + 2), CHUNK), F32)] * 2,
-        in_specs=[pl.BlockSpec(memory_space=pltpu.SMEM)] + [remote] * 3,
+        in_specs=[pl.BlockSpec(memory_space=pltpu.SMEM)] * 2 + [remote] * 3,
         out_specs=[local] * 8,
         scratch_shapes=[
             pltpu.VMEM(keys.shape, keys.dtype),
@@ -208,7 +215,7 @@
         ],
         compiler_params=pltpu.CompilerParams(vmem_limit_bytes=MAPS_VMEM),
         name="state_maps",
-    )(place, keys, values, rates)
+    )(place, docs, keys, values, rates)
 
 
 def read_kernel(
@@ -490,10 +497,8 @@
     group = lax.axis_index("outer")
     place = jnp.stack([1 - second, position, here, lax.axis_index("tp"), second * (heads // 2), group])
     place = place.astype(jnp.int32)
-    lengths = lax.broadcast_in_dim(docs, (DOC_ROWS, docs.shape[0]), (1,))
-    lengths = jnp.pad(lengths, ((0, 0), (0, decay.shape[1] - docs.shape[0]))).astype(F32)
-    rates = jnp.concatenate([decay, beta, lengths], axis=0)
-    theirs, mine, pair_t, pair_m, held_t, held_m, cum_t, cum_m = state_maps(place, keys, values, rates)
+    rates = jnp.concatenate([decay, beta], axis=0)
+    theirs, mine, pair_t, pair_m, held_t, held_m, cum_t, cum_m = state_maps(place, docs, keys, values, rates)
     if ctx == 2:
         swap = [(0, 1), (1, 0)]
         other = lax.ppermute(theirs, "ctx", swap)

time: 78.1 us -> 77.8 us (level)
    unnamed x10 -> x12, local copies, waits for them, and re-layouts: 1.07 us -> 1.72 us
where the time goes in v4:
time: 77.8 us; the launch traced here: 77.5 us
  waiting for transfers between devices  29.4 us (38%)
  Pallas kernels  26.5 us (34%)
  starting transfers between devices  17.2 us (22%)
  other arithmetic  1.92 us (2%)
  local copies, waits for them, and re-layouts  1.8 us (2%)
    ppermute x3, waiting for transfers between devices, shards(): got_x = lax.ppermute(send_x, 'tp', along_x)  12.3 us
    pallas_call x1, Pallas kernels, state_maps(): pl.pallas_call(functools.partial(maps_kernel, chunks, key_heads), out_sha...  10.1 us
    ppermute x3, waiting for transfers between devices, shards(): last_l = lax.ppermute(keep_l[1] + got_x[1], 'tp', along_y)  9.15 us
    pallas_call x2, Pallas kernels, read_out(): pl.pallas_call(functools.partial(read_kernel, step, chunks, key_heads), o...  7.28 us
    ppermute x2, starting transfers between devices, group_hops(): state = lax.ppermute(leaving, 'outer', step)  5.3 us
    ppermute x2, waiting for transfers between devices, group_hops(): state = lax.ppermute(leaving, 'outer', step)  5.29 us
    pallas_call x3, Pallas kernels, finish(): pl.pallas_call(functools.partial(finish_kernel, offset), out_shape=[jax.S...  4.94 us
    ppermute x3, starting transfers between devices, shards(): got_x = lax.ppermute(send_x, 'tp', along_x)  3.69 us
  transfers between devices with their start and end apart: 16, of which 9 were waited for; matrix products, arithmetic and copies ran while one was open for 0% of the time, Pallas kernels for 17%

profile of v4, /device:TPU:12, one launch (start us, length us, event | category | flops | bytes accessed | tf_op | source)
XLA Modules:
  0.0 77.5 jit_solution(4526175741205913565)
XLA Ops:
  0.0 0.7 pad_maximum_fusion.rates_hbm
  0.8 1.0 %copy-done.2 = bf16[512,512]{1,0:T(8,128)(2,1)S(1)} copy-done((bf16[512,512]{1,0:T(8,128)(2,1)S(1)}, bf16[512,512]{1,0:T(8,128)(2,1)}, u32[]{:S(2)}) %copy-start.2) | copy-done | bytes 524312
  1.9 0.7 copy-done.4
  2.5 10.1 %state_maps.1 = (f32[4,128,256]{2,1,0:T(8,128)S(1)}, f32[4,128,256]{2,1,0:T(8,128)S(1)}, bf16[4,512,256]{2,1,0:T(8,128)(2,1)S(1)}, bf16[4,512,256]{2,1,0:T(8,128...) custom-call(s32[6]{0:T(128)S(1)} %stack.27.place_ref.core_ref, ...), custom_call_target="tpu_custom_call" | custom-call | tf_op jit(solution)/shard_map/state_maps/pallas_call | solution.py:202
  12.7 1.9 %collective-permute-done.other_ref = f32[4,128,256]{2,1,0:T(8,128)S(1)} collective-permute-done((f32[4,128,256]{2,1,0:T(8,128)S(1)}, f32[4,128,256]{2,1,0:T(8,128)S(1)}, u32[]{:S(2)}, u32[]{:S(2)}) %collective-permute-start) | collective-permute-done | bytes 524320 | tf_op jit(solution)/shard_map/ppermute | solution.py:504
  14.6 0.8 %shard_map.91 = f32[4,128,128]{2,1,0:T(8,128)S(1)} custom-call(s32[6]{0:T(128)S(1)} %stack.27.place_ref.core_ref, f32[4,128,256]{2,1,0:T(8,128)S(1)} %get-tuple-element.42.mine_ref, f32[4,128,256]{2,1,0:T(8,128)S(1)} %collective-permute-done.other_ref), custom_call_target="tpu_custom_call" | custom-call | tf_op jit(solution)/shard_map/pallas_call | solution.py:331
  15.4 1.6 %collective-permute-start.1 = (f32[4,128,128]{2,1,0:T(8,128)S(1)}, f32[4,128,128]{2,1,0:T(8,128)S(1)}, u32[]{:S(2)}, u32[]{:S(2)}) collective-permute-start(f32[4,128,128]{2,1,0:T(8,128)S(1)} %shard_map.91), channel_id=1, source_target_pairs={{0,1},{1,2},{2,3},{3,0},{4,5},{5,6},{6,7},{7,4},{8,9},{9,10},{10,1... | collective-permute-start | bytes 786440 | tf_op jit(solution)/shard_map/ppermute | solution.py:456
  17.1 0.8 %shard_map.92 = f32[4,128,128]{2,1,0:T(8,128)S(1)} custom-call(s32[6]{0:T(128)S(1)} %stack.27.place_ref.core_ref, f32[4,128,256]{2,1,0:T(8,128)S(1)} %get-tuple-element.42.mine_ref, f32[4,128,256]{2,1,0:T(8,128)S(1)} %collective-permute-done.other_ref), custom_call_target="tpu_custom_call" | custom-call | tf_op jit(solution)/shard_map/pallas_call | solution.py:331
  17.9 3.6 %read_out.2 = (bf16[512,512]{1,0:T(8,128)(2,1)S(1)}, f32[512,512]{1,0:T(8,128)S(1)}) custom-call(s32[6]{0:T(128)S(1)} %stack.27.place_ref.core_ref, bf16[512,512]{1,0:T(8,128)(2,1)S(1)} %copy-done.5, bf16[512,512]{1,0:T(8,128)(2,1)S(1)} %copy-done.2, f32[40,128]{1,0:T(8,128)S(1)} %get-tuple-element.45.cum_ref, ...), custom_call_target="tpu_custom_call" | custom-call | flops 2000000000 | bytes 6000000 | tf_op jit(solution)/shard_map/read_out/pallas_call | solution.py:269
  21.5 2.3 %collective-permute-done.1.former_ref = f32[4,128,128]{2,1,0:T(8,128)S(1)} collective-permute-done((f32[4,128,128]{2,1,0:T(8,128)S(1)}, f32[4,128,128]{2,1,0:T(8,128)S(1)}, u32[]{:S(2)}, u32[]{:S(2)}) %collective-permute-start.1) | collective-permute-done | bytes 262176 | tf_op jit(solution)/shard_map/ppermute | solution.py:456
  24.2 3.7 %collective-permute-start.2 = (f32[4,128,128]{2,1,0:T(8,128)S(1)}, f32[4,128,128]{2,1,0:T(8,128)S(1)}, u32[]{:S(2)}, u32[]{:S(2)}) collective-permute-start(f32[4,128,128]{2,1,0:T(8,128)S(1)} %convolution_add_fusion), channel_id=1, source_target_pairs={{1,2},{2,3},{3,1},{5,6},{6,7},{7,5},{9,10},{10,11},{11,9},{13,14},... | collective-permute-start | bytes 786440 | tf_op jit(solution)/shard_map/ppermute | solution.py:456
  28.0 3.6 %read_out.3 = (bf16[512,512]{1,0:T(8,128)(2,1)S(1)}, f32[512,512]{1,0:T(8,128)S(1)}) custom-call(s32[6]{0:T(128)S(1)} %stack.27.place_ref.core_ref, bf16[512,512]{1,0:T(8,128)(2,1)S(1)} %copy-done.5, bf16[512,512]{1,0:T(8,128)(2,1)S(1)} %copy-done.2, f32[40,128]{1,0:T(8,128)S(1)} %get-tuple-element.52.cum_ref, ...), custom_call_target="tpu_custom_call" | custom-call | flops 2000000000 | bytes 6000000 | tf_op jit(solution)/shard_map/read_out/pallas_call | solution.py:269
  31.6 3.0 %collective-permute-done.2.latter_ref = f32[4,128,128]{2,1,0:T(8,128)S(1)} collective-permute-done((f32[4,128,128]{2,1,0:T(8,128)S(1)}, f32[4,128,128]{2,1,0:T(8,128)S(1)}, u32[]{:S(2)}, u32[]{:S(2)}) %collective-permute-start.2) | collective-permute-done | bytes 262176 | tf_op jit(solution)/shard_map/ppermute | solution.py:456
  34.6 0.8 %shard_map.93 = (f32[4,128,128]{2,1,0:T(8,128)S(1)}, f32[4,128,128]{2,1,0:T(8,128)S(1)}) custom-call(s32[6]{0:T(128)S(1)} %stack.27.place_ref.core_ref, f32[4,128,256]{2,1,0:T(8,128)S(1)} %get-tuple-element.42.mine_ref, f32[4,128,256]{2,1,0:T(8,128)S(1)} %collective-permute-done.other_ref, f32[4,128,128]{2,1,0:T(8,128)S(1)} %collective-permute-done.1.former_ref, ...), custom_call_target="tpu_custom_call" | custom-call | tf_op jit(solution)/shard_map/pallas_call | solution.py:331
  35.5 1.7 %early.1 = (bf16[512,512]{1,0:T(8,128)(2,1)S(1)}, f32[128,2048]{1,0:T(8,128)S(1)}) custom-call(s32[6]{0:T(128)S(1)} %stack.27.place_ref.core_ref, bf16[512,512]{1,0:T(8,128)(2,1)S(1)} %get-tuple-element.62.reach_ref, f32[512,512]{1,0:T(8,128)S(1)} %get-tuple-element.63.core_ref, bf16[512,1024]{1,0:T(8,128)(2,1)S(1)} %copy-done.1, f32[1,128]{1,0:T(1,128)S(1)} %bitcast.57, ...), custom_call_target="tpu_custom_call" | custom-call | flops 1000000000 | bytes 6000000 | tf_op jit(solution)/shard_map/early/pallas_call | solution.py:406
  37.2 1.3 %finish.3 = (f32[2,32,1024]{2,1,0:T(8,128)S(1)}, f32[2,32,1024]{2,1,0:T(8,128)S(1)}, f32[2,32,1024]{2,1,0:T(8,128)S(1)}, f32[2,32,1024]{2,1,0:T(8,128)S(1)}) custom-call(s32[6]{0:T(128)S(1)} %stack.27.place_ref.core_ref, bf16[512,512]{1,0:T(8,128)(2,1)S(1)} %get-tuple-element.57.reach_ref, f32[512,512]{1,0:T(8,128)S(1)} %get-tuple-element.58.core_ref, ...), custom_call_target="tpu_custom_call" | custom-call | flops 536870912 | bytes 524288 | tf_op jit(solution)/shard_map/finish/pallas_call | solution.py:424
  38.5 1.5 %collective-permute-start.4 = (f32[2,32,1024]{2,1,0:T(8,128)S(1)}, f32[2,32,1024]{2,1,0:T(8,128)S(1)}, u32[]{:S(2)}, u32[]{:S(2)}) collective-permute-start(f32[2,32,1024]{2,1,0:T(8,128)S(1)} %get-tuple-element.68), channel_id=1, source_target_pairs={{0,8},{8,0},{16,24},{24,16},{1,9},{9,1},{17,25},{25,17},{2,10},{10... | collective-permute-start | bytes 786440 | tf_op jit(solution)/shard_map/ppermute | solution.py:532
  40.6 1.8 %finish.5 = (f32[2,48,1024]{2,1,0:T(8,128)S(1)}, f32[2,48,1024]{2,1,0:T(8,128)S(1)}, f32[2,48,1024]{2,1,0:T(8,128)S(1)}, f32[2,48,1024]{2,1,0:T(8,128)S(1)}) custom-call(s32[6]{0:T(128)S(1)} %stack.27.place_ref.core_ref, bf16[512,512]{1,0:T(8,128)(2,1)S(1)} %get-tuple-element.57.reach_ref, f32[512,512]{1,0:T(8,128)S(1)} %get-tuple-element.58.core_ref, ...), custom_call_target="tpu_custom_call" | custom-call | flops 805306368 | bytes 786432 | tf_op jit(solution)/shard_map/finish/pallas_call | solution.py:424
  42.4 0.6 collective-permute-start.12
  43.0 1.5 %collective-permute-start.14 = (f32[2,48,1024]{2,1,0:T(8,128)S(1)}, f32[2,48,1024]{2,1,0:T(8,128)S(1)}, u32[]{:S(2)}, u32[]{:S(2)}) collective-permute-start(f32[2,48,1024]{2,1,0:T(8,128)S(1)} %get-tuple-element.78), channel_id=1, source_target_pairs={{0,16},{8,24},{16,0},{24,8},{1,17},{9,25},{17,1},{25,9},{2,18},{10... | collective-permute-start | bytes 1179656 | tf_op jit(solution)/shard_map/ppermute | solution.py:533
  44.5 1.8 %finish.4 = (f32[2,48,1024]{2,1,0:T(8,128)S(1)}, f32[2,48,1024]{2,1,0:T(8,128)S(1)}, f32[2,48,1024]{2,1,0:T(8,128)S(1)}, f32[2,48,1024]{2,1,0:T(8,128)S(1)}) custom-call(s32[6]{0:T(128)S(1)} %stack.27.place_ref.core_ref, bf16[512,512]{1,0:T(8,128)(2,1)S(1)} %get-tuple-element.57.reach_ref, f32[512,512]{1,0:T(8,128)S(1)} %get-tuple-element.58.core_ref, ...), custom_call_target="tpu_custom_call" | custom-call | flops 805306368 | bytes 786432 | tf_op jit(solution)/shard_map/finish/pallas_call | solution.py:424
  46.4 1.5 %collective-permute-start.8 = (f32[2,48,1024]{2,1,0:T(8,128)S(1)}, f32[2,48,1024]{2,1,0:T(8,128)S(1)}, u32[]{:S(2)}, u32[]{:S(2)}) collective-permute-start(f32[2,48,1024]{2,1,0:T(8,128)S(1)} %get-tuple-element.72), channel_id=1, source_target_pairs={{0,8},{8,0},{16,24},{24,16},{1,9},{9,1},{17,25},{25,17},{2,10},{10... | collective-permute-start | bytes 1179656 | tf_op jit(solution)/shard_map/ppermute | solution.py:532
  48.5 0.7 collective-permute-done.6
  49.2 0.9 %collective-permute-start.5 = (f32[32,1024]{1,0:T(8,128)S(1)}, f32[32,1024]{1,0:T(8,128)S(1)}, u32[]{:S(2)}, u32[]{:S(2)}) collective-permute-start(f32[32,1024]{1,0:T(8,128)S(1)} %fusion.20), channel_id=1, source_target_pairs={{0,16},{8,24},{16,0},{24,8},{1,17},{9,25},{17,1},{25,9},{2,18},{10... | collective-permute-start | bytes 393224 | tf_op jit(solution)/shard_map/ppermute | solution.py:537
  50.1 6.0 %collective-permute-done.12 = f32[2,48,1024]{2,1,0:T(8,128)S(1)} collective-permute-done((f32[2,48,1024]{2,1,0:T(8,128)S(1)}, f32[2,48,1024]{2,1,0:T(8,128)S(1)}, u32[]{:S(2)}, u32[]{:S(2)}) %collective-permute-start.12) | collective-permute-done | bytes 393248 | tf_op jit(solution)/shard_map/ppermute | solution.py:532
  56.1 1.5 %collective-permute-start.7 = (f32[32,1024]{1,0:T(8,128)S(1)}, f32[32,1024]{1,0:T(8,128)S(1)}, u32[]{:S(2)}, u32[]{:S(2)}) collective-permute-start(f32[32,1024]{1,0:T(8,128)S(1)} %fusion.16), channel_id=1, source_target_pairs={{0,8},{8,0},{16,24},{24,16},{1,9},{9,1},{17,25},{25,17},{2,10},{10... | collective-permute-start | bytes 393224 | tf_op jit(solution)/shard_map/ppermute | solution.py:538
  58.2 6.3 %collective-permute-done.8 = f32[2,48,1024]{2,1,0:T(8,128)S(1)} collective-permute-done((f32[2,48,1024]{2,1,0:T(8,128)S(1)}, f32[2,48,1024]{2,1,0:T(8,128)S(1)}, u32[]{:S(2)}, u32[]{:S(2)}) %collective-permute-start.8) | collective-permute-done | bytes 393248 | tf_op jit(solution)/shard_map/ppermute | solution.py:532
  64.5 1.5 %collective-permute-start.15 = (f32[48,1024]{1,0:T(8,128)S(1)}, f32[48,1024]{1,0:T(8,128)S(1)}, u32[]{:S(2)}, u32[]{:S(2)}) collective-permute-start(f32[48,1024]{1,0:T(8,128)S(1)} %fusion), channel_id=1, source_target_pairs={{0,8},{8,0},{16,24},{24,16},{1,9},{9,1},{17,25},{25,17},{2,10},{10... | collective-permute-start | bytes 589832 | tf_op jit(solution)/shard_map/ppermute | solution.py:538
  66.7 2.2 %collective-permute-done.5 = f32[32,1024]{1,0:T(8,128)S(1)} collective-permute-done((f32[32,1024]{1,0:T(8,128)S(1)}, f32[32,1024]{1,0:T(8,128)S(1)}, u32[]{:S(2)}, u32[]{:S(2)}) %collective-permute-start.5) | collective-permute-done | bytes 131104 | tf_op jit(solution)/shard_map/ppermute | solution.py:537
  69.5 3.6 %collective-permute-done.13 = f32[48,1024]{1,0:T(8,128)S(1)} collective-permute-done((f32[48,1024]{1,0:T(8,128)S(1)}, f32[48,1024]{1,0:T(8,128)S(1)}, u32[]{:S(2)}, u32[]{:S(2)}) %collective-permute-start.13) | collective-permute-done | bytes 196640 | tf_op jit(solution)/shard_map/ppermute | solution.py:537
  73.2 3.4 %collective-permute-done.9 = f32[48,1024]{1,0:T(8,128)S(1)} collective-permute-done((f32[48,1024]{1,0:T(8,128)S(1)}, f32[48,1024]{1,0:T(8,128)S(1)}, u32[]{:S(2)}, u32[]{:S(2)}) %collective-permute-start.9) | collective-permute-done | bytes 196640 | tf_op jit(solution)/shard_map/ppermute | solution.py:537
  76.6 0.8 %maximum_maximum_fusion = bf16[128,2048]{1,0:T(8,128)(2,1)} fusion(bf16[48,1024]{1,0:T(8,128)(2,1)S(1)} %fusion.3, bf16[48,1024]{1,0:T(8,128)(2,1)S(1)} %fusion.7, bf16[48,1024]{1,0:T(8,128)(2,1)S(1)} %fusion.11, bf16[48,1024]{1,0:T(8,128)(2,1)S(1)} %fusion.15, bf16[32,1024]{1,0:T(8,128)(2,1)S(1)} %fusion.19, bf16[32,1024]{1,0:T(8,128)(2,1)S(1)} %fusion.23), kind=kLoop, calls=%fused_computation.1 | loop fusion | flops 3145728 | bytes 1048576 | tf_op jit(solution)/shard_map/concatenate | solution.py:542
  (38 shorter events, 3.8 us)
Async XLA Ops:
  0.8 1.0 %copy-start.2 = (bf16[512,512]{1,0:T(8,128)(2,1)S(1)}, bf16[512,512]{1,0:T(8,128)(2,1)}, u32[]{:S(2)}) copy-start(bf16[512,512]{1,0:T(8,128)(2,1)} %k_ref.3) | copy-start | bytes 1572868
  1.9 0.7 copy-start.4
  2.5 15.4 %copy-start.5 = (bf16[512,512]{1,0:T(8,128)(2,1)S(1)}, bf16[512,512]{1,0:T(8,128)(2,1)}, u32[]{:S(2)}) copy-start(bf16[512,512]{1,0:T(8,128)(2,1)} %q_ref.3) | copy-start | bytes 1572868
  12.6 2.0 %collective-permute-start = (f32[4,128,256]{2,1,0:T(8,128)S(1)}, f32[4,128,256]{2,1,0:T(8,128)S(1)}, u32[]{:S(2)}, u32[]{:S(2)}) collective-permute-start(f32[4,128,256]{2,1,0:T(8,128)S(1)} %get-tuple-element.43), channel_id=1, source_target_pairs={{0,4},{4,0},{1,5},{5,1},{2,6},{6,2},{3,7},{7,3},{8,12},{12,8},{9,1... | collective-permute-start | bytes 1572872 | tf_op jit(solution)/shard_map/ppermute | solution.py:504
  15.4 8.4 %collective-permute-start.1 = (f32[4,128,128]{2,1,0:T(8,128)S(1)}, f32[4,128,128]{2,1,0:T(8,128)S(1)}, u32[]{:S(2)}, u32[]{:S(2)}) collective-permute-start(f32[4,128,128]{2,1,0:T(8,128)S(1)} %shard_map.91), channel_id=1, source_target_pairs={{0,1},{1,2},{2,3},{3,0},{4,5},{5,6},{6,7},{7,4},{8,9},{9,10},{10,1... | collective-permute-start | bytes 786440 | tf_op jit(solution)/shard_map/ppermute | solution.py:456
  24.2 10.3 %collective-permute-start.2 = (f32[4,128,128]{2,1,0:T(8,128)S(1)}, f32[4,128,128]{2,1,0:T(8,128)S(1)}, u32[]{:S(2)}, u32[]{:S(2)}) collective-permute-start(f32[4,128,128]{2,1,0:T(8,128)S(1)} %convolution_add_fusion), channel_id=1, source_target_pairs={{1,2},{2,3},{3,1},{5,6},{6,7},{7,5},{9,10},{10,11},{11,9},{13,14},... | collective-permute-start | bytes 786440 | tf_op jit(solution)/shard_map/ppermute | solution.py:456
  27.9 7.6 %copy-start = (bf16[1024,2048]{1,0:T(8,128)(2,1)S(1)}, bf16[1024,2048]{1,0:T(8,128)(2,1)}, u32[]{:S(2)}) copy-start(bf16[1024,2048]{1,0:T(8,128)(2,1)} %weight_ref.7) | copy-start | bytes 12582916
  27.9 7.6 %copy-start.1 = (bf16[512,1024]{1,0:T(8,128)(2,1)S(1)}, bf16[512,1024]{1,0:T(8,128)(2,1)}, u32[]{:S(2)}) copy-start(bf16[512,1024]{1,0:T(8,128)(2,1)} %gate_ref.7) | copy-start | bytes 3145732
  27.9 7.6 %copy-start.3 = (f32[128]{0:T(128)S(1)}, f32[128]{0:T(128)}, u32[]{:S(2)}) copy-start(f32[128]{0:T(128)} %param.16) | copy-start | bytes 1540
  35.4 1.8 %collective-permute-start.3 = (f32[4,128,128]{2,1,0:T(8,128)S(1)}, f32[4,128,128]{2,1,0:T(8,128)S(1)}, u32[]{:S(2)}, u32[]{:S(2)}) collective-permute-start(f32[4,128,128]{2,1,0:T(8,128)S(1)} %get-tuple-element.60), channel_id=1, source_target_pairs={{0,4},{4,0},{1,5},{5,1},{2,6},{6,2},{3,7},{7,3},{8,12},{12,8},{9,1... | collective-permute-start | bytes 786440 | tf_op jit(solution)/shard_map/ppermute | solution.py:514
  38.5 9.4 %collective-permute-start.4 = (f32[2,32,1024]{2,1,0:T(8,128)S(1)}, f32[2,32,1024]{2,1,0:T(8,128)S(1)}, u32[]{:S(2)}, u32[]{:S(2)}) collective-permute-start(f32[2,32,1024]{2,1,0:T(8,128)S(1)} %get-tuple-element.68), channel_id=1, source_target_pairs={{0,8},{8,0},{16,24},{24,16},{1,9},{9,1},{17,25},{25,17},{2,10},{10... | collective-permute-start | bytes 786440 | tf_op jit(solution)/shard_map/ppermute | solution.py:532
  40.1 9.1 %collective-permute-start.6 = (f32[2,32,1024]{2,1,0:T(8,128)S(1)}, f32[2,32,1024]{2,1,0:T(8,128)S(1)}, u32[]{:S(2)}, u32[]{:S(2)}) collective-permute-start(f32[2,32,1024]{2,1,0:T(8,128)S(1)} %get-tuple-element.70), channel_id=1, source_target_pairs={{0,16},{8,24},{16,0},{24,8},{1,17},{9,25},{17,1},{25,9},{2,18},{10... | collective-permute-start | bytes 786440 | tf_op jit(solution)/shard_map/ppermute | solution.py:533
  42.4 13.7 %collective-permute-start.12 = (f32[2,48,1024]{2,1,0:T(8,128)S(1)}, f32[2,48,1024]{2,1,0:T(8,128)S(1)}, u32[]{:S(2)}, u32[]{:S(2)}) collective-permute-start(f32[2,48,1024]{2,1,0:T(8,128)S(1)} %get-tuple-element.76), channel_id=1, source_target_pairs={{0,8},{8,0},{16,24},{24,16},{1,9},{9,1},{17,25},{25,17},{2,10},{10... | collective-permute-start | bytes 1179656 | tf_op jit(solution)/shard_map/ppermute | solution.py:532
  43.0 14.6 %collective-permute-start.14 = (f32[2,48,1024]{2,1,0:T(8,128)S(1)}, f32[2,48,1024]{2,1,0:T(8,128)S(1)}, u32[]{:S(2)}, u32[]{:S(2)}) collective-permute-start(f32[2,48,1024]{2,1,0:T(8,128)S(1)} %get-tuple-element.78), channel_id=1, source_target_pairs={{0,16},{8,24},{16,0},{24,8},{1,17},{9,25},{17,1},{25,9},{2,18},{10... | collective-permute-start | bytes 1179656 | tf_op jit(solution)/shard_map/ppermute | solution.py:533
  46.4 18.2 %collective-permute-start.8 = (f32[2,48,1024]{2,1,0:T(8,128)S(1)}, f32[2,48,1024]{2,1,0:T(8,128)S(1)}, u32[]{:S(2)}, u32[]{:S(2)}) collective-permute-start(f32[2,48,1024]{2,1,0:T(8,128)S(1)} %get-tuple-element.72), channel_id=1, source_target_pairs={{0,8},{8,0},{16,24},{24,16},{1,9},{9,1},{17,25},{25,17},{2,10},{10... | collective-permute-start | bytes 1179656 | tf_op jit(solution)/shard_map/ppermute | solution.py:532
  47.9 18.1 %collective-permute-start.10 = (f32[2,48,1024]{2,1,0:T(8,128)S(1)}, f32[2,48,1024]{2,1,0:T(8,128)S(1)}, u32[]{:S(2)}, u32[]{:S(2)}) collective-permute-start(f32[2,48,1024]{2,1,0:T(8,128)S(1)} %get-tuple-element.74), channel_id=1, source_target_pairs={{0,16},{8,24},{16,0},{24,8},{1,17},{9,25},{17,1},{25,9},{2,18},{10... | collective-permute-start | bytes 1179656 | tf_op jit(solution)/shard_map/ppermute | solution.py:533
  49.2 19.7 %collective-permute-start.5 = (f32[32,1024]{1,0:T(8,128)S(1)}, f32[32,1024]{1,0:T(8,128)S(1)}, u32[]{:S(2)}, u32[]{:S(2)}) collective-permute-start(f32[32,1024]{1,0:T(8,128)S(1)} %fusion.20), channel_id=1, source_target_pairs={{0,16},{8,24},{16,0},{24,8},{1,17},{9,25},{17,1},{25,9},{2,18},{10... | collective-permute-start | bytes 393224 | tf_op jit(solution)/shard_map/ppermute | solution.py:537
  56.1 13.3 %collective-permute-start.7 = (f32[32,1024]{1,0:T(8,128)S(1)}, f32[32,1024]{1,0:T(8,128)S(1)}, u32[]{:S(2)}, u32[]{:S(2)}) collective-permute-start(f32[32,1024]{1,0:T(8,128)S(1)} %fusion.16), channel_id=1, source_target_pairs={{0,8},{8,0},{16,24},{24,16},{1,9},{9,1},{17,25},{25,17},{2,10},{10... | collective-permute-start | bytes 393224 | tf_op jit(solution)/shard_map/ppermute | solution.py:538
  57.6 15.4 %collective-permute-start.13 = (f32[48,1024]{1,0:T(8,128)S(1)}, f32[48,1024]{1,0:T(8,128)S(1)}, u32[]{:S(2)}, u32[]{:S(2)}) collective-permute-start(f32[48,1024]{1,0:T(8,128)S(1)} %fusion.4), channel_id=1, source_target_pairs={{0,16},{8,24},{16,0},{24,8},{1,17},{9,25},{17,1},{25,9},{2,18},{10... | collective-permute-start | bytes 589832 | tf_op jit(solution)/shard_map/ppermute | solution.py:537
  64.5 8.6 %collective-permute-start.15 = (f32[48,1024]{1,0:T(8,128)S(1)}, f32[48,1024]{1,0:T(8,128)S(1)}, u32[]{:S(2)}, u32[]{:S(2)}) collective-permute-start(f32[48,1024]{1,0:T(8,128)S(1)} %fusion), channel_id=1, source_target_pairs={{0,8},{8,0},{16,24},{24,16},{1,9},{9,1},{17,25},{25,17},{2,10},{10... | collective-permute-start | bytes 589832 | tf_op jit(solution)/shard_map/ppermute | solution.py:538
  66.1 10.5 %collective-permute-start.9 = (f32[48,1024]{1,0:T(8,128)S(1)}, f32[48,1024]{1,0:T(8,128)S(1)}, u32[]{:S(2)}, u32[]{:S(2)}) collective-permute-start(f32[48,1024]{1,0:T(8,128)S(1)} %fusion.12), channel_id=1, source_target_pairs={{0,16},{8,24},{16,0},{24,8},{1,17},{9,25},{17,1},{25,9},{2,18},{10... | collective-permute-start | bytes 589832 | tf_op jit(solution)/shard_map/ppermute | solution.py:537
  68.9 7.7 %collective-permute-start.11 = (f32[48,1024]{1,0:T(8,128)S(1)}, f32[48,1024]{1,0:T(8,128)S(1)}, u32[]{:S(2)}, u32[]{:S(2)}) collective-permute-start(f32[48,1024]{1,0:T(8,128)S(1)} %fusion.8), channel_id=1, source_target_pairs={{0,8},{8,0},{16,24},{24,16},{1,9},{9,1},{17,25},{25,17},{2,10},{10... | collective-permute-start | bytes 589832 | tf_op jit(solution)/shard_map/ppermute | solution.py:538

commit v5 on v3

--- a/solution.py
+++ b/solution.py
@@ -344,24 +344,23 @@
 
 
 def early_kernel(
-    size, place_ref, reach_ref, core_ref, gate_ref, gain_ref, kept_ref, weight_ref, gated_ref, product_ref
+    size, place_ref, reach_ref, core_ref, gate_ref, gain_ref, kept_ref, weight_ref, product_ref, gated_ref
 ):
     share = gate_ref.shape[0] // 4
     gain = gain_ref[...]
     half = kept_ref.shape[0]
-    every = [slice(0, 4 * share)]
+    rows = part_rows(place_ref, share, 0, size)
     for j in range(half):
         own = slice(j * DV, (j + 1) * DV)
         cols = pl.ds(pl.multiple_of((place_ref[4] + j) * DV, DV), DV)
-        gated_ref[:, own] = gated_rows(every, own, cols, reach_ref, core_ref, gate_ref, gain, kept_ref[j])
-    first = jnp.concatenate([gated_ref[r, :] for r in part_rows(place_ref, share, 0, size)], axis=0)
+        gated_ref[:, own] = gated_rows(rows, own, cols, reach_ref, core_ref, gate_ref, gain, kept_ref[j])
     depth = half * DV
-    product_ref[...] = mm(first, weight_ref[pl.ds(pl.multiple_of(place_ref[4] * DV, depth), depth), :])
-
-
-def finish_kernel(offset, place_ref, reach_ref, core_ref, gate_ref, gain_ref, got_ref, weight_ref, early_ref, *refs):
+    product_ref[...] = mm(gated_ref[...], weight_ref[pl.ds(pl.multiple_of(place_ref[4] * DV, depth), depth), :])
+
+
+def finish_kernel(offset, place_ref, reach_ref, core_ref, gate_ref, gain_ref, got_ref, weight_ref, *refs):
     gated_ref, (send_x_ref, send_y_ref, keep_l_ref, keep_r_ref) = refs[-1], refs[-5:-1]
-    product_ref = refs[0] if len(refs) > 5 else None
+    product_ref = refs[0] if len(refs) == 6 else None
     size = send_x_ref.shape[1]
     gain = gain_ref[...]
     half = got_ref.shape[0]
@@ -374,7 +373,12 @@
     here = pl.ds(pl.multiple_of(place_ref[4] * DV, depth), depth)
     there = pl.ds(pl.multiple_of((half - place_ref[4]) * DV, depth), depth)
     if product_ref is None:
-        early = jnp.concatenate([early_ref[r, :] for r in rows], axis=0)
+        early = []
+        for j in range(half):
+            own = slice(j * DV, (j + 1) * DV)
+            cols = pl.ds(pl.multiple_of((place_ref[4] + j) * DV, DV), DV)
+            early.append(gated_rows(rows, own, cols, refs[0], refs[1], gate_ref, gain, refs[2][j]))
+        early = jnp.concatenate(early, axis=1)
     width = weight_ref.shape[1] // 2
     sums = []
     for cols in (slice(0, width), slice(width, 2 * width)):
@@ -398,12 +402,10 @@
     local = pl.BlockSpec(memory_space=pltpu.VMEM)
     return pl.pallas_call(
         functools.partial(early_kernel, size),
-        out_shape=[
-            jax.ShapeDtypeStruct((tokens, kept.shape[0] * DV), BF16),
-            jax.ShapeDtypeStruct((4 * size, weight.shape[1]), F32),
-        ],
+        out_shape=jax.ShapeDtypeStruct((4 * size, weight.shape[1]), F32),
         in_specs=[pl.BlockSpec(memory_space=pltpu.SMEM)] + [local] * 6,
-        out_specs=[local] * 2,
+        out_specs=local,
+        scratch_shapes=[pltpu.VMEM((4 * size, kept.shape[0] * DV), BF16)],
         compiler_params=pltpu.CompilerParams(vmem_limit_bytes=FINISH_VMEM),
         cost_estimate=pl.CostEstimate(flops=10**9, bytes_accessed=6 * 10**6, transcendentals=tokens * 512),
         name="early",
@@ -522,7 +524,7 @@
     along_y = [(i, i ^ 2) for i in range(4)]
     halves, offset = [], 0
     for size in PARTS:
-        send_x, send_y, keep_l, keep_r = finish(offset, size, place, reads[1], gate, gain, got, weight, early[: 1 if offset else 2])
+        send_x, send_y, keep_l, keep_r = finish(offset, size, place, reads[1], gate, gain, got, weight, (*reads[0], kept) if offset else (early,))
         offset += size
         got_x = lax.ppermute(send_x, "tp", along_x)
         got_y = lax.ppermute(send_y, "tp", along_y)

time: 78.1 us -> 77.6 us (level)
  transfers between devices with their start and end apart: 16 -> 16, of which waited for: 9 -> 10; matrix products, arithmetic and copies ran while one was open for 0% -> 0% of each run, Pallas kernels for 17% -> 17%
where the time goes in v5:
time: 77.6 us; the launch traced here: 77.3 us
  waiting for transfers between devices  28.8 us (37%)
  Pallas kernels  26.6 us (34%)
  starting transfers between devices  17.5 us (23%)
  other arithmetic  2.6 us (3%)
  local copies, waits for them, and re-layouts  1.15 us (1%)
    ppermute x3, waiting for transfers between devices, shards(): got_x = lax.ppermute(send_x, 'tp', along_x)  12 us
    pallas_call x1, Pallas kernels, state_maps(): pl.pallas_call(functools.partial(maps_kernel, chunks, key_heads), out_sha...  10.3 us
    ppermute x3, waiting for transfers between devices, shards(): last_l = lax.ppermute(keep_l[1] + got_x[1], 'tp', along_y)  8.96 us
    pallas_call x2, Pallas kernels, read_out(): pl.pallas_call(functools.partial(read_kernel, step, chunks, key_heads), o...  7.26 us
    ppermute x2, waiting for transfers between devices, group_hops(): state = lax.ppermute(leaving, 'outer', step)  5.31 us
    pallas_call x3, Pallas kernels, finish(): pl.pallas_call(functools.partial(finish_kernel, offset), out_shape=[jax.S...  5.31 us
    ppermute x2, starting transfers between devices, group_hops(): state = lax.ppermute(leaving, 'outer', step)  5.28 us
    ppermute x3, starting transfers between devices, shards(): got_x = lax.ppermute(send_x, 'tp', along_x)  3.71 us
  transfers between devices with their start and end apart: 16, of which 10 were waited for; matrix products, arithmetic and copies ran while one was open for 0% of the time, Pallas kernels for 17%

profile of v5, /device:TPU:12, one launch (start us, length us, event | category | flops | bytes accessed | tf_op | source)
XLA Modules:
  0.0 77.3 jit_solution(14196524434040129190)
XLA Ops:
  0.0 0.7 pad_convert_fusion
  0.7 0.7 pad_maximum_fusion.rates_hbm
  1.5 1.0 %copy-done.2 = bf16[512,512]{1,0:T(8,128)(2,1)S(1)} copy-done((bf16[512,512]{1,0:T(8,128)(2,1)S(1)}, bf16[512,512]{1,0:T(8,128)(2,1)}, u32[]{:S(2)}) %copy-start.2) | copy-done | bytes 524312
  2.5 10.3 %state_maps.1 = (f32[4,128,256]{2,1,0:T(8,128)S(1)}, f32[4,128,256]{2,1,0:T(8,128)S(1)}, bf16[4,512,256]{2,1,0:T(8,128)(2,1)S(1)}, bf16[4,512,256]{2,1,0:T(8,128...) custom-call(s32[6]{0:T(128)S(1)} %stack.27.place_ref.core_ref, ...), custom_call_target="tpu_custom_call" | custom-call | tf_op jit(solution)/shard_map/state_maps/pallas_call | solution.py:195
  13.0 1.9 %collective-permute-done.other_ref = f32[4,128,256]{2,1,0:T(8,128)S(1)} collective-permute-done((f32[4,128,256]{2,1,0:T(8,128)S(1)}, f32[4,128,256]{2,1,0:T(8,128)S(1)}, u32[]{:S(2)}, u32[]{:S(2)}) %collective-permute-start) | collective-permute-done | bytes 524320 | tf_op jit(solution)/shard_map/ppermute | solution.py:501
  14.8 0.8 %shard_map.91 = f32[4,128,128]{2,1,0:T(8,128)S(1)} custom-call(s32[6]{0:T(128)S(1)} %stack.27.place_ref.core_ref, f32[4,128,256]{2,1,0:T(8,128)S(1)} %get-tuple-element.40.mine_ref, f32[4,128,256]{2,1,0:T(8,128)S(1)} %collective-permute-done.other_ref), custom_call_target="tpu_custom_call" | custom-call | tf_op jit(solution)/shard_map/pallas_call | solution.py:324
  15.7 1.6 %collective-permute-start.1 = (f32[4,128,128]{2,1,0:T(8,128)S(1)}, f32[4,128,128]{2,1,0:T(8,128)S(1)}, u32[]{:S(2)}, u32[]{:S(2)}) collective-permute-start(f32[4,128,128]{2,1,0:T(8,128)S(1)} %shard_map.91), channel_id=1, source_target_pairs={{0,1},{1,2},{2,3},{3,0},{4,5},{5,6},{6,7},{7,4},{8,9},{9,10},{10,1... | collective-permute-start | bytes 786440 | tf_op jit(solution)/shard_map/ppermute | solution.py:451
  17.3 0.8 %shard_map.92 = f32[4,128,128]{2,1,0:T(8,128)S(1)} custom-call(s32[6]{0:T(128)S(1)} %stack.27.place_ref.core_ref, f32[4,128,256]{2,1,0:T(8,128)S(1)} %get-tuple-element.40.mine_ref, f32[4,128,256]{2,1,0:T(8,128)S(1)} %collective-permute-done.other_ref), custom_call_target="tpu_custom_call" | custom-call | tf_op jit(solution)/shard_map/pallas_call | solution.py:324
  18.1 3.6 %read_out.2 = (bf16[512,512]{1,0:T(8,128)(2,1)S(1)}, f32[512,512]{1,0:T(8,128)S(1)}) custom-call(s32[6]{0:T(128)S(1)} %stack.27.place_ref.core_ref, bf16[512,512]{1,0:T(8,128)(2,1)S(1)} %copy-done.4, bf16[512,512]{1,0:T(8,128)(2,1)S(1)} %copy-done.2, f32[40,128]{1,0:T(8,128)S(1)} %get-tuple-element.43.cum_ref, ...), custom_call_target="tpu_custom_call" | custom-call | flops 2000000000 | bytes 6000000 | tf_op jit(solution)/shard_map/read_out/pallas_call | solution.py:262
  21.8 2.3 %collective-permute-done.1.former_ref = f32[4,128,128]{2,1,0:T(8,128)S(1)} collective-permute-done((f32[4,128,128]{2,1,0:T(8,128)S(1)}, f32[4,128,128]{2,1,0:T(8,128)S(1)}, u32[]{:S(2)}, u32[]{:S(2)}) %collective-permute-start.1) | collective-permute-done | bytes 262176 | tf_op jit(solution)/shard_map/ppermute | solution.py:451
  24.5 3.6 %collective-permute-start.2 = (f32[4,128,128]{2,1,0:T(8,128)S(1)}, f32[4,128,128]{2,1,0:T(8,128)S(1)}, u32[]{:S(2)}, u32[]{:S(2)}) collective-permute-start(f32[4,128,128]{2,1,0:T(8,128)S(1)} %convolution_add_fusion), channel_id=1, source_target_pairs={{1,2},{2,3},{3,1},{5,6},{6,7},{7,5},{9,10},{10,11},{11,9},{13,14},... | collective-permute-start | bytes 786440 | tf_op jit(solution)/shard_map/ppermute | solution.py:451
  28.2 3.6 %read_out.3 = (bf16[512,512]{1,0:T(8,128)(2,1)S(1)}, f32[512,512]{1,0:T(8,128)S(1)}) custom-call(s32[6]{0:T(128)S(1)} %stack.27.place_ref.core_ref, bf16[512,512]{1,0:T(8,128)(2,1)S(1)} %copy-done.4, bf16[512,512]{1,0:T(8,128)(2,1)S(1)} %copy-done.2, f32[40,128]{1,0:T(8,128)S(1)} %get-tuple-element.50.cum_ref, ...), custom_call_target="tpu_custom_call" | custom-call | flops 2000000000 | bytes 6000000 | tf_op jit(solution)/shard_map/read_out/pallas_call | solution.py:262
  31.8 3.0 %collective-permute-done.2.latter_ref = f32[4,128,128]{2,1,0:T(8,128)S(1)} collective-permute-done((f32[4,128,128]{2,1,0:T(8,128)S(1)}, f32[4,128,128]{2,1,0:T(8,128)S(1)}, u32[]{:S(2)}, u32[]{:S(2)}) %collective-permute-start.2) | collective-permute-done | bytes 262176 | tf_op jit(solution)/shard_map/ppermute | solution.py:451
  34.8 0.8 %shard_map.93 = (f32[4,128,128]{2,1,0:T(8,128)S(1)}, f32[4,128,128]{2,1,0:T(8,128)S(1)}) custom-call(s32[6]{0:T(128)S(1)} %stack.27.place_ref.core_ref, f32[4,128,256]{2,1,0:T(8,128)S(1)} %get-tuple-element.40.mine_ref, f32[4,128,256]{2,1,0:T(8,128)S(1)} %collective-permute-done.other_ref, f32[4,128,128]{2,1,0:T(8,128)S(1)} %collective-permute-done.1.former_ref, ...), custom_call_target="tpu_custom_call" | custom-call | tf_op jit(solution)/shard_map/pallas_call | solution.py:324
  35.7 1.3 %early.1.refs_0_ = f32[128,2048]{1,0:T(8,128)S(1)} custom-call(s32[6]{0:T(128)S(1)} %stack.27.place_ref.core_ref, bf16[512,512]{1,0:T(8,128)(2,1)S(1)} %get-tuple-element.60.reach_ref.refs_0_, f32[512,512]{1,0:T(8,128)S(1)} %get-tuple-element.61.core_ref.refs_1_, bf16[512,1024]{1,0:T(8,128)(2,1)S(1)} %copy-done.1, f32[1,128]{1,0:T(1,128)S(1)} %bitcast.57, ...), custom_call_target="tpu_custom_call" | custom-call | flops 1000000000 | bytes 6000000 | tf_op jit(solution)/shard_map/early/pallas_call | solution.py:403
  37.2 1.3 %finish.3 = (f32[2,32,1024]{2,1,0:T(8,128)S(1)}, f32[2,32,1024]{2,1,0:T(8,128)S(1)}, f32[2,32,1024]{2,1,0:T(8,128)S(1)}, f32[2,32,1024]{2,1,0:T(8,128)S(1)}) custom-call(s32[6]{0:T(128)S(1)} %stack.27.place_ref.core_ref, bf16[512,512]{1,0:T(8,128)(2,1)S(1)} %get-tuple-element.55.reach_ref, f32[512,512]{1,0:T(8,128)S(1)} %get-tuple-element.56.core_ref, ...), custom_call_target="tpu_custom_call" | custom-call | flops 536870912 | bytes 524288 | tf_op jit(solution)/shard_map/finish/pallas_call | solution.py:419
  38.5 1.6 %collective-permute-start.4 = (f32[2,32,1024]{2,1,0:T(8,128)S(1)}, f32[2,32,1024]{2,1,0:T(8,128)S(1)}, u32[]{:S(2)}, u32[]{:S(2)}) collective-permute-start(f32[2,32,1024]{2,1,0:T(8,128)S(1)} %get-tuple-element.64), channel_id=1, source_target_pairs={{0,8},{8,0},{16,24},{24,16},{1,9},{9,1},{17,25},{25,17},{2,10},{10... | collective-permute-start | bytes 786440 | tf_op jit(solution)/shard_map/ppermute | solution.py:529
  40.5 2.0 %finish.4 = (f32[2,48,1024]{2,1,0:T(8,128)S(1)}, f32[2,48,1024]{2,1,0:T(8,128)S(1)}, f32[2,48,1024]{2,1,0:T(8,128)S(1)}, f32[2,48,1024]{2,1,0:T(8,128)S(1)}) custom-call(s32[6]{0:T(128)S(1)} %stack.27.place_ref.core_ref, bf16[512,512]{1,0:T(8,128)(2,1)S(1)} %get-tuple-element.55.reach_ref, f32[512,512]{1,0:T(8,128)S(1)} %get-tuple-element.56.core_ref, ...), custom_call_target="tpu_custom_call" | custom-call | flops 805306368 | bytes 786432 | tf_op jit(solution)/shard_map/finish/pallas_call | solution.py:419
  42.6 0.6 collective-permute-start.8
  43.2 1.5 %collective-permute-start.10 = (f32[2,48,1024]{2,1,0:T(8,128)S(1)}, f32[2,48,1024]{2,1,0:T(8,128)S(1)}, u32[]{:S(2)}, u32[]{:S(2)}) collective-permute-start(f32[2,48,1024]{2,1,0:T(8,128)S(1)} %get-tuple-element.70), channel_id=1, source_target_pairs={{0,16},{8,24},{16,0},{24,8},{1,17},{9,25},{17,1},{25,9},{2,18},{10... | collective-permute-start | bytes 1179656 | tf_op jit(solution)/shard_map/ppermute | solution.py:530
  44.7 2.0 %finish.5 = (f32[2,48,1024]{2,1,0:T(8,128)S(1)}, f32[2,48,1024]{2,1,0:T(8,128)S(1)}, f32[2,48,1024]{2,1,0:T(8,128)S(1)}, f32[2,48,1024]{2,1,0:T(8,128)S(1)}) custom-call(s32[6]{0:T(128)S(1)} %stack.27.place_ref.core_ref, bf16[512,512]{1,0:T(8,128)(2,1)S(1)} %get-tuple-element.55.reach_ref, f32[512,512]{1,0:T(8,128)S(1)} %get-tuple-element.56.core_ref, ...), custom_call_target="tpu_custom_call" | custom-call | flops 805306368 | bytes 786432 | tf_op jit(solution)/shard_map/finish/pallas_call | solution.py:419
  46.7 1.6 %collective-permute-start.12 = (f32[2,48,1024]{2,1,0:T(8,128)S(1)}, f32[2,48,1024]{2,1,0:T(8,128)S(1)}, u32[]{:S(2)}, u32[]{:S(2)}) collective-permute-start(f32[2,48,1024]{2,1,0:T(8,128)S(1)} %get-tuple-element.72), channel_id=1, source_target_pairs={{0,8},{8,0},{16,24},{24,16},{1,9},{9,1},{17,25},{25,17},{2,10},{10... | collective-permute-start | bytes 1179656 | tf_op jit(solution)/shard_map/ppermute | solution.py:529
  49.2 1.2 %collective-permute-start.5 = (f32[32,1024]{1,0:T(8,128)S(1)}, f32[32,1024]{1,0:T(8,128)S(1)}, u32[]{:S(2)}, u32[]{:S(2)}) collective-permute-start(f32[32,1024]{1,0:T(8,128)S(1)} %fusion.20), channel_id=1, source_target_pairs={{0,16},{8,24},{16,0},{24,8},{1,17},{9,25},{17,1},{25,9},{2,18},{10... | collective-permute-start | bytes 393224 | tf_op jit(solution)/shard_map/ppermute | solution.py:534
  50.4 5.7 %collective-permute-done.8 = f32[2,48,1024]{2,1,0:T(8,128)S(1)} collective-permute-done((f32[2,48,1024]{2,1,0:T(8,128)S(1)}, f32[2,48,1024]{2,1,0:T(8,128)S(1)}, u32[]{:S(2)}, u32[]{:S(2)}) %collective-permute-start.8) | collective-permute-done | bytes 393248 | tf_op jit(solution)/shard_map/ppermute | solution.py:529
  56.1 1.5 %collective-permute-start.7 = (f32[32,1024]{1,0:T(8,128)S(1)}, f32[32,1024]{1,0:T(8,128)S(1)}, u32[]{:S(2)}, u32[]{:S(2)}) collective-permute-start(f32[32,1024]{1,0:T(8,128)S(1)} %fusion.16), channel_id=1, source_target_pairs={{0,8},{8,0},{16,24},{24,16},{1,9},{9,1},{17,25},{25,17},{2,10},{10... | collective-permute-start | bytes 393224 | tf_op jit(solution)/shard_map/ppermute | solution.py:535
  57.7 0.6 collective-permute-start.9
  58.2 6.3 %collective-permute-done.12 = f32[2,48,1024]{2,1,0:T(8,128)S(1)} collective-permute-done((f32[2,48,1024]{2,1,0:T(8,128)S(1)}, f32[2,48,1024]{2,1,0:T(8,128)S(1)}, u32[]{:S(2)}, u32[]{:S(2)}) %collective-permute-start.12) | collective-permute-done | bytes 393248 | tf_op jit(solution)/shard_map/ppermute | solution.py:529
  64.5 1.5 %collective-permute-start.11 = (f32[48,1024]{1,0:T(8,128)S(1)}, f32[48,1024]{1,0:T(8,128)S(1)}, u32[]{:S(2)}, u32[]{:S(2)}) collective-permute-start(f32[48,1024]{1,0:T(8,128)S(1)} %fusion.8), channel_id=1, source_target_pairs={{0,8},{8,0},{16,24},{24,16},{1,9},{9,1},{17,25},{25,17},{2,10},{10... | collective-permute-start | bytes 589832 | tf_op jit(solution)/shard_map/ppermute | solution.py:535
  66.7 2.2 %collective-permute-done.5 = f32[32,1024]{1,0:T(8,128)S(1)} collective-permute-done((f32[32,1024]{1,0:T(8,128)S(1)}, f32[32,1024]{1,0:T(8,128)S(1)}, u32[]{:S(2)}, u32[]{:S(2)}) %collective-permute-start.5) | collective-permute-done | bytes 131104 | tf_op jit(solution)/shard_map/ppermute | solution.py:534
  69.5 3.6 %collective-permute-done.9 = f32[48,1024]{1,0:T(8,128)S(1)} collective-permute-done((f32[48,1024]{1,0:T(8,128)S(1)}, f32[48,1024]{1,0:T(8,128)S(1)}, u32[]{:S(2)}, u32[]{:S(2)}) %collective-permute-start.9) | collective-permute-done | bytes 196640 | tf_op jit(solution)/shard_map/ppermute | solution.py:534
  73.2 3.1 %collective-permute-done.13 = f32[48,1024]{1,0:T(8,128)S(1)} collective-permute-done((f32[48,1024]{1,0:T(8,128)S(1)}, f32[48,1024]{1,0:T(8,128)S(1)}, u32[]{:S(2)}, u32[]{:S(2)}) %collective-permute-start.13) | collective-permute-done | bytes 196640 | tf_op jit(solution)/shard_map/ppermute | solution.py:534
  76.4 0.8 %maximum_maximum_fusion = bf16[128,2048]{1,0:T(8,128)(2,1)} fusion(bf16[48,1024]{1,0:T(8,128)(2,1)S(1)} %fusion.3, bf16[48,1024]{1,0:T(8,128)(2,1)S(1)} %fusion.7, bf16[48,1024]{1,0:T(8,128)(2,1)S(1)} %fusion.11, bf16[48,1024]{1,0:T(8,128)(2,1)S(1)} %fusion.15, bf16[32,1024]{1,0:T(8,128)(2,1)S(1)} %fusion.19, bf16[32,1024]{1,0:T(8,128)(2,1)S(1)} %fusion.23), kind=kLoop, calls=%fused_computation.1 | loop fusion | flops 3145728 | bytes 1048576 | tf_op jit(solution)/shard_map/concatenate | solution.py:539
  (38 shorter events, 3.8 us)
Async XLA Ops:
  1.5 1.0 %copy-start.2 = (bf16[512,512]{1,0:T(8,128)(2,1)S(1)}, bf16[512,512]{1,0:T(8,128)(2,1)}, u32[]{:S(2)}) copy-start(bf16[512,512]{1,0:T(8,128)(2,1)} %k_ref.3) | copy-start | bytes 1572868
  2.5 15.6 %copy-start.4 = (bf16[512,512]{1,0:T(8,128)(2,1)S(1)}, bf16[512,512]{1,0:T(8,128)(2,1)}, u32[]{:S(2)}) copy-start(bf16[512,512]{1,0:T(8,128)(2,1)} %q_ref.3) | copy-start | bytes 1572868
  12.9 2.0 %collective-permute-start = (f32[4,128,256]{2,1,0:T(8,128)S(1)}, f32[4,128,256]{2,1,0:T(8,128)S(1)}, u32[]{:S(2)}, u32[]{:S(2)}) collective-permute-start(f32[4,128,256]{2,1,0:T(8,128)S(1)} %get-tuple-element.41), channel_id=1, source_target_pairs={{0,4},{4,0},{1,5},{5,1},{2,6},{6,2},{3,7},{7,3},{8,12},{12,8},{9,1... | collective-permute-start | bytes 1572872 | tf_op jit(solution)/shard_map/ppermute | solution.py:501
  15.7 8.4 %collective-permute-start.1 = (f32[4,128,128]{2,1,0:T(8,128)S(1)}, f32[4,128,128]{2,1,0:T(8,128)S(1)}, u32[]{:S(2)}, u32[]{:S(2)}) collective-permute-start(f32[4,128,128]{2,1,0:T(8,128)S(1)} %shard_map.91), channel_id=1, source_target_pairs={{0,1},{1,2},{2,3},{3,0},{4,5},{5,6},{6,7},{7,4},{8,9},{9,10},{10,1... | collective-permute-start | bytes 786440 | tf_op jit(solution)/shard_map/ppermute | solution.py:451
  24.5 10.3 %collective-permute-start.2 = (f32[4,128,128]{2,1,0:T(8,128)S(1)}, f32[4,128,128]{2,1,0:T(8,128)S(1)}, u32[]{:S(2)}, u32[]{:S(2)}) collective-permute-start(f32[4,128,128]{2,1,0:T(8,128)S(1)} %convolution_add_fusion), channel_id=1, source_target_pairs={{1,2},{2,3},{3,1},{5,6},{6,7},{7,5},{9,10},{10,11},{11,9},{13,14},... | collective-permute-start | bytes 786440 | tf_op jit(solution)/shard_map/ppermute | solution.py:451
  28.1 7.6 %copy-start = (bf16[1024,2048]{1,0:T(8,128)(2,1)S(1)}, bf16[1024,2048]{1,0:T(8,128)(2,1)}, u32[]{:S(2)}) copy-start(bf16[1024,2048]{1,0:T(8,128)(2,1)} %weight_ref.7) | copy-start | bytes 12582916
  28.2 7.6 %copy-start.1 = (bf16[512,1024]{1,0:T(8,128)(2,1)S(1)}, bf16[512,1024]{1,0:T(8,128)(2,1)}, u32[]{:S(2)}) copy-start(bf16[512,1024]{1,0:T(8,128)(2,1)} %gate_ref.7) | copy-start | bytes 3145732
  28.2 7.6 %copy-start.3 = (f32[128]{0:T(128)S(1)}, f32[128]{0:T(128)}, u32[]{:S(2)}) copy-start(f32[128]{0:T(128)} %param.16) | copy-start | bytes 1540
  35.6 1.6 %collective-permute-start.3 = (f32[4,128,128]{2,1,0:T(8,128)S(1)}, f32[4,128,128]{2,1,0:T(8,128)S(1)}, u32[]{:S(2)}, u32[]{:S(2)}) collective-permute-start(f32[4,128,128]{2,1,0:T(8,128)S(1)} %get-tuple-element.58), channel_id=1, source_target_pairs={{0,4},{4,0},{1,5},{5,1},{2,6},{6,2},{3,7},{7,3},{8,12},{12,8},{9,1... | collective-permute-start | bytes 786440 | tf_op jit(solution)/shard_map/ppermute | solution.py:511
  38.5 9.8 %collective-permute-start.4 = (f32[2,32,1024]{2,1,0:T(8,128)S(1)}, f32[2,32,1024]{2,1,0:T(8,128)S(1)}, u32[]{:S(2)}, u32[]{:S(2)}) collective-permute-start(f32[2,32,1024]{2,1,0:T(8,128)S(1)} %get-tuple-element.64), channel_id=1, source_target_pairs={{0,8},{8,0},{16,24},{24,16},{1,9},{9,1},{17,25},{25,17},{2,10},{10... | collective-permute-start | bytes 786440 | tf_op jit(solution)/shard_map/ppermute | solution.py:529
  40.0 9.2 %collective-permute-start.6 = (f32[2,32,1024]{2,1,0:T(8,128)S(1)}, f32[2,32,1024]{2,1,0:T(8,128)S(1)}, u32[]{:S(2)}, u32[]{:S(2)}) collective-permute-start(f32[2,32,1024]{2,1,0:T(8,128)S(1)} %get-tuple-element.66), channel_id=1, source_target_pairs={{0,16},{8,24},{16,0},{24,8},{1,17},{9,25},{17,1},{25,9},{2,18},{10... | collective-permute-start | bytes 786440 | tf_op jit(solution)/shard_map/ppermute | solution.py:530
  42.6 13.5 %collective-permute-start.8 = (f32[2,48,1024]{2,1,0:T(8,128)S(1)}, f32[2,48,1024]{2,1,0:T(8,128)S(1)}, u32[]{:S(2)}, u32[]{:S(2)}) collective-permute-start(f32[2,48,1024]{2,1,0:T(8,128)S(1)} %get-tuple-element.68), channel_id=1, source_target_pairs={{0,8},{8,0},{16,24},{24,16},{1,9},{9,1},{17,25},{25,17},{2,10},{10... | collective-permute-start | bytes 1179656 | tf_op jit(solution)/shard_map/ppermute | solution.py:529
  43.2 14.5 %collective-permute-start.10 = (f32[2,48,1024]{2,1,0:T(8,128)S(1)}, f32[2,48,1024]{2,1,0:T(8,128)S(1)}, u32[]{:S(2)}, u32[]{:S(2)}) collective-permute-start(f32[2,48,1024]{2,1,0:T(8,128)S(1)} %get-tuple-element.70), channel_id=1, source_target_pairs={{0,16},{8,24},{16,0},{24,8},{1,17},{9,25},{17,1},{25,9},{2,18},{10... | collective-permute-start | bytes 1179656 | tf_op jit(solution)/shard_map/ppermute | solution.py:530
  46.7 17.8 %collective-permute-start.12 = (f32[2,48,1024]{2,1,0:T(8,128)S(1)}, f32[2,48,1024]{2,1,0:T(8,128)S(1)}, u32[]{:S(2)}, u32[]{:S(2)}) collective-permute-start(f32[2,48,1024]{2,1,0:T(8,128)S(1)} %get-tuple-element.72), channel_id=1, source_target_pairs={{0,8},{8,0},{16,24},{24,16},{1,9},{9,1},{17,25},{25,17},{2,10},{10... | collective-permute-start | bytes 1179656 | tf_op jit(solution)/shard_map/ppermute | solution.py:529
  48.3 17.8 %collective-permute-start.14 = (f32[2,48,1024]{2,1,0:T(8,128)S(1)}, f32[2,48,1024]{2,1,0:T(8,128)S(1)}, u32[]{:S(2)}, u32[]{:S(2)}) collective-permute-start(f32[2,48,1024]{2,1,0:T(8,128)S(1)} %get-tuple-element.74), channel_id=1, source_target_pairs={{0,16},{8,24},{16,0},{24,8},{1,17},{9,25},{17,1},{25,9},{2,18},{10... | collective-permute-start | bytes 1179656 | tf_op jit(solution)/shard_map/ppermute | solution.py:530
  49.2 19.7 %collective-permute-start.5 = (f32[32,1024]{1,0:T(8,128)S(1)}, f32[32,1024]{1,0:T(8,128)S(1)}, u32[]{:S(2)}, u32[]{:S(2)}) collective-permute-start(f32[32,1024]{1,0:T(8,128)S(1)} %fusion.20), channel_id=1, source_target_pairs={{0,16},{8,24},{16,0},{24,8},{1,17},{9,25},{17,1},{25,9},{2,18},{10... | collective-permute-start | bytes 393224 | tf_op jit(solution)/shard_map/ppermute | solution.py:534
  56.1 13.3 %collective-permute-start.7 = (f32[32,1024]{1,0:T(8,128)S(1)}, f32[32,1024]{1,0:T(8,128)S(1)}, u32[]{:S(2)}, u32[]{:S(2)}) collective-permute-start(f32[32,1024]{1,0:T(8,128)S(1)} %fusion.16), channel_id=1, source_target_pairs={{0,8},{8,0},{16,24},{24,16},{1,9},{9,1},{17,25},{25,17},{2,10},{10... | collective-permute-start | bytes 393224 | tf_op jit(solution)/shard_map/ppermute | solution.py:535
  57.7 15.4 %collective-permute-start.9 = (f32[48,1024]{1,0:T(8,128)S(1)}, f32[48,1024]{1,0:T(8,128)S(1)}, u32[]{:S(2)}, u32[]{:S(2)}) collective-permute-start(f32[48,1024]{1,0:T(8,128)S(1)} %fusion.12), channel_id=1, source_target_pairs={{0,16},{8,24},{16,0},{24,8},{1,17},{9,25},{17,1},{25,9},{2,18},{10... | collective-permute-start | bytes 589832 | tf_op jit(solution)/shard_map/ppermute | solution.py:534
  64.5 8.6 %collective-permute-start.11 = (f32[48,1024]{1,0:T(8,128)S(1)}, f32[48,1024]{1,0:T(8,128)S(1)}, u32[]{:S(2)}, u32[]{:S(2)}) collective-permute-start(f32[48,1024]{1,0:T(8,128)S(1)} %fusion.8), channel_id=1, source_target_pairs={{0,8},{8,0},{16,24},{24,16},{1,9},{9,1},{17,25},{25,17},{2,10},{10... | collective-permute-start | bytes 589832 | tf_op jit(solution)/shard_map/ppermute | solution.py:535
  66.1 10.2 %collective-permute-start.13 = (f32[48,1024]{1,0:T(8,128)S(1)}, f32[48,1024]{1,0:T(8,128)S(1)}, u32[]{:S(2)}, u32[]{:S(2)}) collective-permute-start(f32[48,1024]{1,0:T(8,128)S(1)} %fusion.4), channel_id=1, source_target_pairs={{0,16},{8,24},{16,0},{24,8},{1,17},{9,25},{17,1},{25,9},{2,18},{10... | collective-permute-start | bytes 589832 | tf_op jit(solution)/shard_map/ppermute | solution.py:534
  68.9 7.5 %collective-permute-start.15 = (f32[48,1024]{1,0:T(8,128)S(1)}, f32[48,1024]{1,0:T(8,128)S(1)}, u32[]{:S(2)}, u32[]{:S(2)}) collective-permute-start(f32[48,1024]{1,0:T(8,128)S(1)} %fusion), channel_id=1, source_target_pairs={{0,8},{8,0},{16,24},{24,16},{1,9},{9,1},{17,25},{25,17},{2,10},{10... | collective-permute-start | bytes 589832 | tf_op jit(solution)/shard_map/ppermute | solution.py:535

commit v6 on v5

--- a/solution.py
+++ b/solution.py
@@ -431,7 +431,7 @@
 
 
 def precise(left, right):
-    return jnp.einsum("hij,hjk->hik", left, right, precision=lax.Precision.HIGHEST)
+    return jnp.einsum("hij,hjk->hik", left, right, precision=lax.Precision.HIGH)
 
 
 def combine(earlier, later):

time: 77.6 us -> 77.5 us (level)
  no operation moved by 1% of the time
where the time goes in v6:
time: 77.5 us; the launch traced here: 77.1 us
  waiting for transfers between devices  28.9 us (37%)
  Pallas kernels  26.6 us (34%)
  starting transfers between devices  17.5 us (23%)
  other arithmetic  2.6 us (3%)
  local copies, waits for them, and re-layouts  1.15 us (1%)
    ppermute x3, waiting for transfers between devices, shards(): got_x = lax.ppermute(send_x, 'tp', along_x)  12 us
    pallas_call x1, Pallas kernels, state_maps(): pl.pallas_call(functools.partial(maps_kernel, chunks, key_heads), out_sha...  10.3 us
    ppermute x3, waiting for transfers between devices, shards(): last_l = lax.ppermute(keep_l[1] + got_x[1], 'tp', along_y)  8.96 us
    pallas_call x2, Pallas kernels, read_out(): pl.pallas_call(functools.partial(read_kernel, step, chunks, key_heads), o...  7.26 us
    ppermute x2, waiting for transfers between devices, group_hops(): state = lax.ppermute(leaving, 'outer', step)  5.31 us
    pallas_call x3, Pallas kernels, finish(): pl.pallas_call(functools.partial(finish_kernel, offset), out_shape=[jax.S...  5.3 us
    ppermute x2, starting transfers between devices, group_hops(): state = lax.ppermute(leaving, 'outer', step)  5.28 us
    ppermute x3, starting transfers between devices, shards(): got_x = lax.ppermute(send_x, 'tp', along_x)  3.72 us
  transfers between devices with their start and end apart: 16, of which 10 were waited for; matrix products, arithmetic and copies ran while one was open for 0% of the time, Pallas kernels for 17%

profile of v6, /device:TPU:12, one launch (start us, length us, event | category | flops | bytes accessed | tf_op | source)
XLA Modules:
  0.0 77.1 jit_solution(6175797038735254707)
XLA Ops:
  0.0 0.7 pad_convert_fusion
  0.7 0.7 pad_maximum_fusion.rates_hbm
  1.5 1.0 %copy-done.2 = bf16[512,512]{1,0:T(8,128)(2,1)S(1)} copy-done((bf16[512,512]{1,0:T(8,128)(2,1)S(1)}, bf16[512,512]{1,0:T(8,128)(2,1)}, u32[]{:S(2)}) %copy-start.2) | copy-done | bytes 524312
  2.5 10.3 %state_maps.1 = (f32[4,128,256]{2,1,0:T(8,128)S(1)}, f32[4,128,256]{2,1,0:T(8,128)S(1)}, bf16[4,512,256]{2,1,0:T(8,128)(2,1)S(1)}, bf16[4,512,256]{2,1,0:T(8,128...) custom-call(s32[6]{0:T(128)S(1)} %stack.27.place_ref.core_ref, ...), custom_call_target="tpu_custom_call" | custom-call | tf_op jit(solution)/shard_map/state_maps/pallas_call | solution.py:195
  13.0 1.9 %collective-permute-done.other_ref = f32[4,128,256]{2,1,0:T(8,128)S(1)} collective-permute-done((f32[4,128,256]{2,1,0:T(8,128)S(1)}, f32[4,128,256]{2,1,0:T(8,128)S(1)}, u32[]{:S(2)}, u32[]{:S(2)}) %collective-permute-start) | collective-permute-done | bytes 524320 | tf_op jit(solution)/shard_map/ppermute | solution.py:501
  14.8 0.8 %shard_map.91 = f32[4,128,128]{2,1,0:T(8,128)S(1)} custom-call(s32[6]{0:T(128)S(1)} %stack.27.place_ref.core_ref, f32[4,128,256]{2,1,0:T(8,128)S(1)} %get-tuple-element.40.mine_ref, f32[4,128,256]{2,1,0:T(8,128)S(1)} %collective-permute-done.other_ref), custom_call_target="tpu_custom_call" | custom-call | tf_op jit(solution)/shard_map/pallas_call | solution.py:324
  15.7 1.6 %collective-permute-start.1 = (f32[4,128,128]{2,1,0:T(8,128)S(1)}, f32[4,128,128]{2,1,0:T(8,128)S(1)}, u32[]{:S(2)}, u32[]{:S(2)}) collective-permute-start(f32[4,128,128]{2,1,0:T(8,128)S(1)} %shard_map.91), channel_id=1, source_target_pairs={{0,1},{1,2},{2,3},{3,0},{4,5},{5,6},{6,7},{7,4},{8,9},{9,10},{10,1... | collective-permute-start | bytes 786440 | tf_op jit(solution)/shard_map/ppermute | solution.py:451
  17.3 0.8 %shard_map.92 = f32[4,128,128]{2,1,0:T(8,128)S(1)} custom-call(s32[6]{0:T(128)S(1)} %stack.27.place_ref.core_ref, f32[4,128,256]{2,1,0:T(8,128)S(1)} %get-tuple-element.40.mine_ref, f32[4,128,256]{2,1,0:T(8,128)S(1)} %collective-permute-done.other_ref), custom_call_target="tpu_custom_call" | custom-call | tf_op jit(solution)/shard_map/pallas_call | solution.py:324
  18.1 3.6 %read_out.2 = (bf16[512,512]{1,0:T(8,128)(2,1)S(1)}, f32[512,512]{1,0:T(8,128)S(1)}) custom-call(s32[6]{0:T(128)S(1)} %stack.27.place_ref.core_ref, bf16[512,512]{1,0:T(8,128)(2,1)S(1)} %copy-done.4, bf16[512,512]{1,0:T(8,128)(2,1)S(1)} %copy-done.2, f32[40,128]{1,0:T(8,128)S(1)} %get-tuple-element.43.cum_ref, ...), custom_call_target="tpu_custom_call" | custom-call | flops 2000000000 | bytes 6000000 | tf_op jit(solution)/shard_map/read_out/pallas_call | solution.py:262
  21.8 2.3 %collective-permute-done.1.former_ref = f32[4,128,128]{2,1,0:T(8,128)S(1)} collective-permute-done((f32[4,128,128]{2,1,0:T(8,128)S(1)}, f32[4,128,128]{2,1,0:T(8,128)S(1)}, u32[]{:S(2)}, u32[]{:S(2)}) %collective-permute-start.1) | collective-permute-done | bytes 262176 | tf_op jit(solution)/shard_map/ppermute | solution.py:451
  24.4 3.6 %collective-permute-start.2 = (f32[4,128,128]{2,1,0:T(8,128)S(1)}, f32[4,128,128]{2,1,0:T(8,128)S(1)}, u32[]{:S(2)}, u32[]{:S(2)}) collective-permute-start(f32[4,128,128]{2,1,0:T(8,128)S(1)} %convolution_add_fusion), channel_id=1, source_target_pairs={{1,2},{2,3},{3,1},{5,6},{6,7},{7,5},{9,10},{10,11},{11,9},{13,14},... | collective-permute-start | bytes 786440 | tf_op jit(solution)/shard_map/ppermute | solution.py:451
  28.0 3.6 %read_out.3 = (bf16[512,512]{1,0:T(8,128)(2,1)S(1)}, f32[512,512]{1,0:T(8,128)S(1)}) custom-call(s32[6]{0:T(128)S(1)} %stack.27.place_ref.core_ref, bf16[512,512]{1,0:T(8,128)(2,1)S(1)} %copy-done.4, bf16[512,512]{1,0:T(8,128)(2,1)S(1)} %copy-done.2, f32[40,128]{1,0:T(8,128)S(1)} %get-tuple-element.50.cum_ref, ...), custom_call_target="tpu_custom_call" | custom-call | flops 2000000000 | bytes 6000000 | tf_op jit(solution)/shard_map/read_out/pallas_call | solution.py:262
  31.7 3.0 %collective-permute-done.2.latter_ref = f32[4,128,128]{2,1,0:T(8,128)S(1)} collective-permute-done((f32[4,128,128]{2,1,0:T(8,128)S(1)}, f32[4,128,128]{2,1,0:T(8,128)S(1)}, u32[]{:S(2)}, u32[]{:S(2)}) %collective-permute-start.2) | collective-permute-done | bytes 262176 | tf_op jit(solution)/shard_map/ppermute | solution.py:451
  34.7 0.8 %shard_map.93 = (f32[4,128,128]{2,1,0:T(8,128)S(1)}, f32[4,128,128]{2,1,0:T(8,128)S(1)}) custom-call(s32[6]{0:T(128)S(1)} %stack.27.place_ref.core_ref, f32[4,128,256]{2,1,0:T(8,128)S(1)} %get-tuple-element.40.mine_ref, f32[4,128,256]{2,1,0:T(8,128)S(1)} %collective-permute-done.other_ref, f32[4,128,128]{2,1,0:T(8,128)S(1)} %collective-permute-done.1.former_ref, ...), custom_call_target="tpu_custom_call" | custom-call | tf_op jit(solution)/shard_map/pallas_call | solution.py:324
  35.6 1.3 %early.1.refs_0_ = f32[128,2048]{1,0:T(8,128)S(1)} custom-call(s32[6]{0:T(128)S(1)} %stack.27.place_ref.core_ref, bf16[512,512]{1,0:T(8,128)(2,1)S(1)} %get-tuple-element.60.reach_ref.refs_0_, f32[512,512]{1,0:T(8,128)S(1)} %get-tuple-element.61.core_ref.refs_1_, bf16[512,1024]{1,0:T(8,128)(2,1)S(1)} %copy-done.1, f32[1,128]{1,0:T(1,128)S(1)} %bitcast.57, ...), custom_call_target="tpu_custom_call" | custom-call | flops 1000000000 | bytes 6000000 | tf_op jit(solution)/shard_map/early/pallas_call | solution.py:403
  37.1 1.3 %finish.3 = (f32[2,32,1024]{2,1,0:T(8,128)S(1)}, f32[2,32,1024]{2,1,0:T(8,128)S(1)}, f32[2,32,1024]{2,1,0:T(8,128)S(1)}, f32[2,32,1024]{2,1,0:T(8,128)S(1)}) custom-call(s32[6]{0:T(128)S(1)} %stack.27.place_ref.core_ref, bf16[512,512]{1,0:T(8,128)(2,1)S(1)} %get-tuple-element.55.reach_ref, f32[512,512]{1,0:T(8,128)S(1)} %get-tuple-element.56.core_ref, ...), custom_call_target="tpu_custom_call" | custom-call | flops 536870912 | bytes 524288 | tf_op jit(solution)/shard_map/finish/pallas_call | solution.py:419
  38.4 1.6 %collective-permute-start.4 = (f32[2,32,1024]{2,1,0:T(8,128)S(1)}, f32[2,32,1024]{2,1,0:T(8,128)S(1)}, u32[]{:S(2)}, u32[]{:S(2)}) collective-permute-start(f32[2,32,1024]{2,1,0:T(8,128)S(1)} %get-tuple-element.64), channel_id=1, source_target_pairs={{0,8},{8,0},{16,24},{24,16},{1,9},{9,1},{17,25},{25,17},{2,10},{10... | collective-permute-start | bytes 786440 | tf_op jit(solution)/shard_map/ppermute | solution.py:529
  40.4 2.0 %finish.4 = (f32[2,48,1024]{2,1,0:T(8,128)S(1)}, f32[2,48,1024]{2,1,0:T(8,128)S(1)}, f32[2,48,1024]{2,1,0:T(8,128)S(1)}, f32[2,48,1024]{2,1,0:T(8,128)S(1)}) custom-call(s32[6]{0:T(128)S(1)} %stack.27.place_ref.core_ref, bf16[512,512]{1,0:T(8,128)(2,1)S(1)} %get-tuple-element.55.reach_ref, f32[512,512]{1,0:T(8,128)S(1)} %get-tuple-element.56.core_ref, ...), custom_call_target="tpu_custom_call" | custom-call | flops 805306368 | bytes 786432 | tf_op jit(solution)/shard_map/finish/pallas_call | solution.py:419
  42.4 0.6 collective-permute-start.8
  43.0 1.5 %collective-permute-start.10 = (f32[2,48,1024]{2,1,0:T(8,128)S(1)}, f32[2,48,1024]{2,1,0:T(8,128)S(1)}, u32[]{:S(2)}, u32[]{:S(2)}) collective-permute-start(f32[2,48,1024]{2,1,0:T(8,128)S(1)} %get-tuple-element.70), channel_id=1, source_target_pairs={{0,16},{8,24},{16,0},{24,8},{1,17},{9,25},{17,1},{25,9},{2,18},{10... | collective-permute-start | bytes 1179656 | tf_op jit(solution)/shard_map/ppermute | solution.py:530
  44.6 2.0 %finish.5 = (f32[2,48,1024]{2,1,0:T(8,128)S(1)}, f32[2,48,1024]{2,1,0:T(8,128)S(1)}, f32[2,48,1024]{2,1,0:T(8,128)S(1)}, f32[2,48,1024]{2,1,0:T(8,128)S(1)}) custom-call(s32[6]{0:T(128)S(1)} %stack.27.place_ref.core_ref, bf16[512,512]{1,0:T(8,128)(2,1)S(1)} %get-tuple-element.55.reach_ref, f32[512,512]{1,0:T(8,128)S(1)} %get-tuple-element.56.core_ref, ...), custom_call_target="tpu_custom_call" | custom-call | flops 805306368 | bytes 786432 | tf_op jit(solution)/shard_map/finish/pallas_call | solution.py:419
  46.6 1.6 %collective-permute-start.12 = (f32[2,48,1024]{2,1,0:T(8,128)S(1)}, f32[2,48,1024]{2,1,0:T(8,128)S(1)}, u32[]{:S(2)}, u32[]{:S(2)}) collective-permute-start(f32[2,48,1024]{2,1,0:T(8,128)S(1)} %get-tuple-element.72), channel_id=1, source_target_pairs={{0,8},{8,0},{16,24},{24,16},{1,9},{9,1},{17,25},{25,17},{2,10},{10... | collective-permute-start | bytes 1179656 | tf_op jit(solution)/shard_map/ppermute | solution.py:529
  49.1 1.2 %collective-permute-start.5 = (f32[32,1024]{1,0:T(8,128)S(1)}, f32[32,1024]{1,0:T(8,128)S(1)}, u32[]{:S(2)}, u32[]{:S(2)}) collective-permute-start(f32[32,1024]{1,0:T(8,128)S(1)} %fusion.20), channel_id=1, source_target_pairs={{0,16},{8,24},{16,0},{24,8},{1,17},{9,25},{17,1},{25,9},{2,18},{10... | collective-permute-start | bytes 393224 | tf_op jit(solution)/shard_map/ppermute | solution.py:534
  50.3 5.7 %collective-permute-done.8 = f32[2,48,1024]{2,1,0:T(8,128)S(1)} collective-permute-done((f32[2,48,1024]{2,1,0:T(8,128)S(1)}, f32[2,48,1024]{2,1,0:T(8,128)S(1)}, u32[]{:S(2)}, u32[]{:S(2)}) %collective-permute-start.8) | collective-permute-done | bytes 393248 | tf_op jit(solution)/shard_map/ppermute | solution.py:529
  56.0 1.5 %collective-permute-start.7 = (f32[32,1024]{1,0:T(8,128)S(1)}, f32[32,1024]{1,0:T(8,128)S(1)}, u32[]{:S(2)}, u32[]{:S(2)}) collective-permute-start(f32[32,1024]{1,0:T(8,128)S(1)} %fusion.16), channel_id=1, source_target_pairs={{0,8},{8,0},{16,24},{24,16},{1,9},{9,1},{17,25},{25,17},{2,10},{10... | collective-permute-start | bytes 393224 | tf_op jit(solution)/shard_map/ppermute | solution.py:535
  57.5 0.6 collective-permute-start.9
  58.1 6.3 %collective-permute-done.12 = f32[2,48,1024]{2,1,0:T(8,128)S(1)} collective-permute-done((f32[2,48,1024]{2,1,0:T(8,128)S(1)}, f32[2,48,1024]{2,1,0:T(8,128)S(1)}, u32[]{:S(2)}, u32[]{:S(2)}) %collective-permute-start.12) | collective-permute-done | bytes 393248 | tf_op jit(solution)/shard_map/ppermute | solution.py:529
  64.4 1.5 %collective-permute-start.11 = (f32[48,1024]{1,0:T(8,128)S(1)}, f32[48,1024]{1,0:T(8,128)S(1)}, u32[]{:S(2)}, u32[]{:S(2)}) collective-permute-start(f32[48,1024]{1,0:T(8,128)S(1)} %fusion.8), channel_id=1, source_target_pairs={{0,8},{8,0},{16,24},{24,16},{1,9},{9,1},{17,25},{25,17},{2,10},{10... | collective-permute-start | bytes 589832 | tf_op jit(solution)/shard_map/ppermute | solution.py:535
  66.5 2.2 %collective-permute-done.5 = f32[32,1024]{1,0:T(8,128)S(1)} collective-permute-done((f32[32,1024]{1,0:T(8,128)S(1)}, f32[32,1024]{1,0:T(8,128)S(1)}, u32[]{:S(2)}, u32[]{:S(2)}) %collective-permute-start.5) | collective-permute-done | bytes 131104 | tf_op jit(solution)/shard_map/ppermute | solution.py:534
  69.4 3.6 %collective-permute-done.9 = f32[48,1024]{1,0:T(8,128)S(1)} collective-permute-done((f32[48,1024]{1,0:T(8,128)S(1)}, f32[48,1024]{1,0:T(8,128)S(1)}, u32[]{:S(2)}, u32[]{:S(2)}) %collective-permute-start.9) | collective-permute-done | bytes 196640 | tf_op jit(solution)/shard_map/ppermute | solution.py:534
  73.1 3.1 %collective-permute-done.13 = f32[48,1024]{1,0:T(8,128)S(1)} collective-permute-done((f32[48,1024]{1,0:T(8,128)S(1)}, f32[48,1024]{1,0:T(8,128)S(1)}, u32[]{:S(2)}, u32[]{:S(2)}) %collective-permute-start.13) | collective-permute-done | bytes 196640 | tf_op jit(solution)/shard_map/ppermute | solution.py:534
  76.3 0.8 %maximum_maximum_fusion = bf16[128,2048]{1,0:T(8,128)(2,1)} fusion(bf16[48,1024]{1,0:T(8,128)(2,1)S(1)} %fusion.3, bf16[48,1024]{1,0:T(8,128)(2,1)S(1)} %fusion.7, bf16[48,1024]{1,0:T(8,128)(2,1)S(1)} %fusion.11, bf16[48,1024]{1,0:T(8,128)(2,1)S(1)} %fusion.15, bf16[32,1024]{1,0:T(8,128)(2,1)S(1)} %fusion.19, bf16[32,1024]{1,0:T(8,128)(2,1)S(1)} %fusion.23), kind=kLoop, calls=%fused_computation.1 | loop fusion | flops 3145728 | bytes 1048576 | tf_op jit(solution)/shard_map/concatenate | solution.py:539
  (38 shorter events, 3.7 us)
Async XLA Ops:
  1.5 1.0 %copy-start.2 = (bf16[512,512]{1,0:T(8,128)(2,1)S(1)}, bf16[512,512]{1,0:T(8,128)(2,1)}, u32[]{:S(2)}) copy-start(bf16[512,512]{1,0:T(8,128)(2,1)} %k_ref.3) | copy-start | bytes 1572868
  2.5 15.6 %copy-start.4 = (bf16[512,512]{1,0:T(8,128)(2,1)S(1)}, bf16[512,512]{1,0:T(8,128)(2,1)}, u32[]{:S(2)}) copy-start(bf16[512,512]{1,0:T(8,128)(2,1)} %q_ref.3) | copy-start | bytes 1572868
  12.9 2.0 %collective-permute-start = (f32[4,128,256]{2,1,0:T(8,128)S(1)}, f32[4,128,256]{2,1,0:T(8,128)S(1)}, u32[]{:S(2)}, u32[]{:S(2)}) collective-permute-start(f32[4,128,256]{2,1,0:T(8,128)S(1)} %get-tuple-element.41), channel_id=1, source_target_pairs={{0,4},{4,0},{1,5},{5,1},{2,6},{6,2},{3,7},{7,3},{8,12},{12,8},{9,1... | collective-permute-start | bytes 1572872 | tf_op jit(solution)/shard_map/ppermute | solution.py:501
  15.7 8.4 %collective-permute-start.1 = (f32[4,128,128]{2,1,0:T(8,128)S(1)}, f32[4,128,128]{2,1,0:T(8,128)S(1)}, u32[]{:S(2)}, u32[]{:S(2)}) collective-permute-start(f32[4,128,128]{2,1,0:T(8,128)S(1)} %shard_map.91), channel_id=1, source_target_pairs={{0,1},{1,2},{2,3},{3,0},{4,5},{5,6},{6,7},{7,4},{8,9},{9,10},{10,1... | collective-permute-start | bytes 786440 | tf_op jit(solution)/shard_map/ppermute | solution.py:451
  24.4 10.3 %collective-permute-start.2 = (f32[4,128,128]{2,1,0:T(8,128)S(1)}, f32[4,128,128]{2,1,0:T(8,128)S(1)}, u32[]{:S(2)}, u32[]{:S(2)}) collective-permute-start(f32[4,128,128]{2,1,0:T(8,128)S(1)} %convolution_add_fusion), channel_id=1, source_target_pairs={{1,2},{2,3},{3,1},{5,6},{6,7},{7,5},{9,10},{10,11},{11,9},{13,14},... | collective-permute-start | bytes 786440 | tf_op jit(solution)/shard_map/ppermute | solution.py:451
  28.0 7.6 %copy-start = (bf16[1024,2048]{1,0:T(8,128)(2,1)S(1)}, bf16[1024,2048]{1,0:T(8,128)(2,1)}, u32[]{:S(2)}) copy-start(bf16[1024,2048]{1,0:T(8,128)(2,1)} %weight_ref.7) | copy-start | bytes 12582916
  28.0 7.6 %copy-start.1 = (bf16[512,1024]{1,0:T(8,128)(2,1)S(1)}, bf16[512,1024]{1,0:T(8,128)(2,1)}, u32[]{:S(2)}) copy-start(bf16[512,1024]{1,0:T(8,128)(2,1)} %gate_ref.7) | copy-start | bytes 3145732
  28.0 7.6 %copy-start.3 = (f32[128]{0:T(128)S(1)}, f32[128]{0:T(128)}, u32[]{:S(2)}) copy-start(f32[128]{0:T(128)} %param.16) | copy-start | bytes 1540
  35.5 1.6 %collective-permute-start.3 = (f32[4,128,128]{2,1,0:T(8,128)S(1)}, f32[4,128,128]{2,1,0:T(8,128)S(1)}, u32[]{:S(2)}, u32[]{:S(2)}) collective-permute-start(f32[4,128,128]{2,1,0:T(8,128)S(1)} %get-tuple-element.58), channel_id=1, source_target_pairs={{0,4},{4,0},{1,5},{5,1},{2,6},{6,2},{3,7},{7,3},{8,12},{12,8},{9,1... | collective-permute-start | bytes 786440 | tf_op jit(solution)/shard_map/ppermute | solution.py:511
  38.4 9.8 %collective-permute-start.4 = (f32[2,32,1024]{2,1,0:T(8,128)S(1)}, f32[2,32,1024]{2,1,0:T(8,128)S(1)}, u32[]{:S(2)}, u32[]{:S(2)}) collective-permute-start(f32[2,32,1024]{2,1,0:T(8,128)S(1)} %get-tuple-element.64), channel_id=1, source_target_pairs={{0,8},{8,0},{16,24},{24,16},{1,9},{9,1},{17,25},{25,17},{2,10},{10... | collective-permute-start | bytes 786440 | tf_op jit(solution)/shard_map/ppermute | solution.py:529
  39.9 9.2 %collective-permute-start.6 = (f32[2,32,1024]{2,1,0:T(8,128)S(1)}, f32[2,32,1024]{2,1,0:T(8,128)S(1)}, u32[]{:S(2)}, u32[]{:S(2)}) collective-permute-start(f32[2,32,1024]{2,1,0:T(8,128)S(1)} %get-tuple-element.66), channel_id=1, source_target_pairs={{0,16},{8,24},{16,0},{24,8},{1,17},{9,25},{17,1},{25,9},{2,18},{10... | collective-permute-start | bytes 786440 | tf_op jit(solution)/shard_map/ppermute | solution.py:530
  42.4 13.6 %collective-permute-start.8 = (f32[2,48,1024]{2,1,0:T(8,128)S(1)}, f32[2,48,1024]{2,1,0:T(8,128)S(1)}, u32[]{:S(2)}, u32[]{:S(2)}) collective-permute-start(f32[2,48,1024]{2,1,0:T(8,128)S(1)} %get-tuple-element.68), channel_id=1, source_target_pairs={{0,8},{8,0},{16,24},{24,16},{1,9},{9,1},{17,25},{25,17},{2,10},{10... | collective-permute-start | bytes 1179656 | tf_op jit(solution)/shard_map/ppermute | solution.py:529
  43.0 14.5 %collective-permute-start.10 = (f32[2,48,1024]{2,1,0:T(8,128)S(1)}, f32[2,48,1024]{2,1,0:T(8,128)S(1)}, u32[]{:S(2)}, u32[]{:S(2)}) collective-permute-start(f32[2,48,1024]{2,1,0:T(8,128)S(1)} %get-tuple-element.70), channel_id=1, source_target_pairs={{0,16},{8,24},{16,0},{24,8},{1,17},{9,25},{17,1},{25,9},{2,18},{10... | collective-permute-start | bytes 1179656 | tf_op jit(solution)/shard_map/ppermute | solution.py:530
  46.6 17.8 %collective-permute-start.12 = (f32[2,48,1024]{2,1,0:T(8,128)S(1)}, f32[2,48,1024]{2,1,0:T(8,128)S(1)}, u32[]{:S(2)}, u32[]{:S(2)}) collective-permute-start(f32[2,48,1024]{2,1,0:T(8,128)S(1)} %get-tuple-element.72), channel_id=1, source_target_pairs={{0,8},{8,0},{16,24},{24,16},{1,9},{9,1},{17,25},{25,17},{2,10},{10... | collective-permute-start | bytes 1179656 | tf_op jit(solution)/shard_map/ppermute | solution.py:529
  48.2 17.8 %collective-permute-start.14 = (f32[2,48,1024]{2,1,0:T(8,128)S(1)}, f32[2,48,1024]{2,1,0:T(8,128)S(1)}, u32[]{:S(2)}, u32[]{:S(2)}) collective-permute-start(f32[2,48,1024]{2,1,0:T(8,128)S(1)} %get-tuple-element.74), channel_id=1, source_target_pairs={{0,16},{8,24},{16,0},{24,8},{1,17},{9,25},{17,1},{25,9},{2,18},{10... | collective-permute-start | bytes 1179656 | tf_op jit(solution)/shard_map/ppermute | solution.py:530
  49.1 19.7 %collective-permute-start.5 = (f32[32,1024]{1,0:T(8,128)S(1)}, f32[32,1024]{1,0:T(8,128)S(1)}, u32[]{:S(2)}, u32[]{:S(2)}) collective-permute-start(f32[32,1024]{1,0:T(8,128)S(1)} %fusion.20), channel_id=1, source_target_pairs={{0,16},{8,24},{16,0},{24,8},{1,17},{9,25},{17,1},{25,9},{2,18},{10... | collective-permute-start | bytes 393224 | tf_op jit(solution)/shard_map/ppermute | solution.py:534
  56.0 13.3 %collective-permute-start.7 = (f32[32,1024]{1,0:T(8,128)S(1)}, f32[32,1024]{1,0:T(8,128)S(1)}, u32[]{:S(2)}, u32[]{:S(2)}) collective-permute-start(f32[32,1024]{1,0:T(8,128)S(1)} %fusion.16), channel_id=1, source_target_pairs={{0,8},{8,0},{16,24},{24,16},{1,9},{9,1},{17,25},{25,17},{2,10},{10... | collective-permute-start | bytes 393224 | tf_op jit(solution)/shard_map/ppermute | solution.py:535
  57.5 15.4 %collective-permute-start.9 = (f32[48,1024]{1,0:T(8,128)S(1)}, f32[48,1024]{1,0:T(8,128)S(1)}, u32[]{:S(2)}, u32[]{:S(2)}) collective-permute-start(f32[48,1024]{1,0:T(8,128)S(1)} %fusion.12), channel_id=1, source_target_pairs={{0,16},{8,24},{16,0},{24,8},{1,17},{9,25},{17,1},{25,9},{2,18},{10... | collective-permute-start | bytes 589832 | tf_op jit(solution)/shard_map/ppermute | solution.py:534
  64.4 8.6 %collective-permute-start.11 = (f32[48,1024]{1,0:T(8,128)S(1)}, f32[48,1024]{1,0:T(8,128)S(1)}, u32[]{:S(2)}, u32[]{:S(2)}) collective-permute-start(f32[48,1024]{1,0:T(8,128)S(1)} %fusion.8), channel_id=1, source_target_pairs={{0,8},{8,0},{16,24},{24,16},{1,9},{9,1},{17,25},{25,17},{2,10},{10... | collective-permute-start | bytes 589832 | tf_op jit(solution)/shard_map/ppermute | solution.py:535
  66.0 10.2 %collective-permute-start.13 = (f32[48,1024]{1,0:T(8,128)S(1)}, f32[48,1024]{1,0:T(8,128)S(1)}, u32[]{:S(2)}, u32[]{:S(2)}) collective-permute-start(f32[48,1024]{1,0:T(8,128)S(1)} %fusion.4), channel_id=1, source_target_pairs={{0,16},{8,24},{16,0},{24,8},{1,17},{9,25},{17,1},{25,9},{2,18},{10... | collective-permute-start | bytes 589832 | tf_op jit(solution)/shard_map/ppermute | solution.py:534
  68.8 7.5 %collective-permute-start.15 = (f32[48,1024]{1,0:T(8,128)S(1)}, f32[48,1024]{1,0:T(8,128)S(1)}, u32[]{:S(2)}, u32[]{:S(2)}) collective-permute-start(f32[48,1024]{1,0:T(8,128)S(1)} %fusion), channel_id=1, source_target_pairs={{0,8},{8,0},{16,24},{24,16},{1,9},{9,1},{17,25},{25,17},{2,10},{10... | collective-permute-start | bytes 589832 | tf_op jit(solution)/shard_map/ppermute | solution.py:535
